TPU v7x, 256 devices: a whole 4x4x8 slice. The times are simulated.
256 devices in a mesh: space: 64 (over y, z, core), rep: 4 (over x).
Axes of the slice: x: 4, y: 4, z: 8, core: 2. Of those that a mesh axis runs over, the one named last changes fastest.
Arguments:
- features: bfloat16 [512, 96, 512], P(('rep', 'space')), parts along dimension 0, may hold values from -6 to 6
- occupancy: int32 [512, 16], P(('rep', 'space')), parts along dimension 0, may hold values from -2147483647 to 2147483646, as said below
- neighbours: int32 [512, 27], P(('rep', 'space')), parts along dimension 0, may hold values from 0 to 6, as said below
- live_count: int32 [256], P(('rep', 'space')), parts along dimension 0, may hold values from 1 to 2, as said below
- w_subm: bfloat16 [27, 96, 96], replicated, may hold values from -0.15625 to 0.15625
- w_down: bfloat16 [8, 96, 96], replicated, may hold values from -0.3125 to 0.3125
- grad_coarse: bfloat16 [16384, 768], P(('rep', 'space')), parts along dimension 0, may hold values from -6 to 6
Outputs:
- coarse_out: bfloat16 [16384, 768], P(('rep', 'space')), parts along dimension 0
- grad_features: bfloat16 [512, 96, 512], P(('rep', 'space')), parts along dimension 0
- grad_subm: float32 [108, 96, 96], P('rep'), parts along dimension 0
- grad_down: float32 [32, 96, 96], P('rep'), parts along dimension 0
There are 4 independent parts, one for each index of `rep`. A program takes and returns all parts, laid end to end along the dimension named above; an argument that names none is the same for every part. Nothing has to cross between parts.
Inputs may be any that keep to these rules, and one draw needn't show every extreme that they name: `neighbours`: entry 13 of each block's row is 2 plus its own slot; 6 means empty. `live_count`: some device has all 2 slots live; live slots are the lowest ones. `occupancy`: any 32-bit pattern.
All inputs are finite; a program needn't handle non-finite values.
Results may differ from a plain program's by a relative error of at most 0.0054.
Values may be sent and summed in bfloat16 or wider, within the bound.
A program may use at most 128 MiB of HBM per device.

v0:
```python
import jax
import jax.numpy as jnp
from jax import lax
from jax.sharding import PartitionSpec as P

stencil_offsets = [
    (first, second, third) for first in (-1, 0, 1) for second in (-1, 0, 1) for third in (-1, 0, 1)
]
slab_spans = {-1: (7, 8, 0, 1), 0: (0, 8, 1, 9), 1: (0, 1, 9, 10)}


def padded_2(value, sides, width):
    for axis, dim in sides:
        count, length = (lax.axis_size(axis), value.shape[dim])
        up = [(i, (i + 1) % count) for i in range(count - 1)]
        down = [(j, i) for i, j in up]
        last = lax.slice_in_dim(value, length - width, length, axis=dim)
        leading = lax.slice_in_dim(value, 0, width, axis=dim)
        before = lax.ppermute(last, axis, up)
        after = lax.ppermute(leading, axis, down)
        value = jnp.concatenate([before, value, after], axis=dim)
    return value


def entering(part, axis, combine, identity):
    place = lax.axis_index(axis)
    gathered = lax.all_gather(part, axis)
    state = jnp.zeros_like(part) + jnp.asarray(identity, part.dtype)

    def one(step, state):
        return combine(state, lax.dynamic_index_in_dim(gathered, step, 0, False))

    return lax.fori_loop(0, place, one, state)


def shifted(block, axis, distance):
    devices = range(lax.axis_size(axis))
    route = [(i - distance, i) for i in devices if i - distance in devices]
    return lax.ppermute(block, axis, route)


def source_slices(first, second, third):
    return tuple(
        (slice(slab_spans[offset][0], slab_spans[offset][1]) for offset in (first, second, third))
    )


def target_slices(first, second, third):
    return tuple(
        (slice(slab_spans[offset][2], slab_spans[offset][3]) for offset in (first, second, third))
    )


def unpack_bits(words):
    position = jnp.arange(512, dtype=jnp.int32)
    chosen = words[:, position // 32]
    return jnp.bitwise_and(jnp.right_shift(chosen, position % 32), 1)


def rim_cubes(received, count, chans):
    return received.reshape(count, chans, 8, 8, 8)


def widen(received, cube):
    count, chans = (cube.shape[0], cube.shape[1])
    lower = rim_cubes(received[:count], count, chans)
    upper = rim_cubes(received[2 * count :], count, chans)
    return jnp.concatenate([lower, cube, upper, jnp.zeros((1, chans, 8, 8, 8), cube.dtype)], axis=0)


def build_pad(source, table):
    count = table.shape[0]
    chans = source.shape[1]
    padded = jnp.zeros((count, chans, 10, 10, 10), source.dtype)
    for index, (first, second, third) in enumerate(stencil_offsets):
        piece = source[(slice(None), slice(None)) + source_slices(first, second, third)]
        piece = jnp.take(piece, table[:, index], axis=0)
        padded = padded.at[(slice(None), slice(None)) + target_slices(first, second, third)].set(
            piece
        )
    return padded


def window(padded, first, second, third):
    count, chans = (padded.shape[0], padded.shape[1])
    return padded[
        :, :, 1 + first : 9 + first, 1 + second : 9 + second, 1 + third : 9 + third
    ].reshape(count, chans, 512)


def child(hidden, index):
    count, chans = (hidden.shape[0], hidden.shape[1])
    return hidden.reshape(count, chans, 4, 2, 4, 2, 4, 2)[
        :, :, :, index // 4, :, index // 2 % 2, :, index % 2
    ].reshape(count, chans, 64)


def place_children(pieces):
    count, chans = (pieces[0].shape[0], pieces[0].shape[1])
    stacked = jnp.stack(pieces, axis=-1).reshape(count, chans, 4, 4, 4, 2, 2, 2)
    return jnp.transpose(stacked, (0, 1, 2, 5, 3, 6, 4, 7)).reshape(count, chans, 512)


def gelu_tanh(values):
    return jax.nn.gelu(values, approximate=True)


def add_counts(earlier, later):
    return earlier + later


def gradient_source(dpre, table, w_subm):
    count, chans = (dpre.shape[0], dpre.shape[1])
    gpad = jnp.zeros((count, chans, 10, 10, 10), jnp.float32)
    for index, (first, second, third) in enumerate(stencil_offsets):
        term = jnp.einsum(
            "cd,bdv->bcv", w_subm[index], dpre, preferred_element_type=jnp.float32
        ).reshape(count, chans, 8, 8, 8)
        gpad = gpad.at[
            :, :, 1 + first : 9 + first, 1 + second : 9 + second, 1 + third : 9 + third
        ].add(term)
    gsource = jnp.zeros((3 * count + 1, chans, 8, 8, 8), jnp.float32)
    for index, (first, second, third) in enumerate(stencil_offsets):
        gsource = gsource.at[
            (table[:, index], slice(None)) + source_slices(first, second, third)
        ].add(gpad[(slice(None), slice(None)) + target_slices(first, second, third)])
    return gsource


def per_device(features, occupancy, neighbours, live_count, w_subm, w_down, grad_coarse):
    count, chans = (features.shape[0], features.shape[1])
    peers = lax.axis_size("space")
    capacity = grad_coarse.shape[0] // peers
    slots = jnp.arange(count, dtype=jnp.int32)
    alive = (slots < live_count[0]).astype(jnp.int32)
    mask = unpack_bits(occupancy) * alive[:, None]
    mask_f = mask.astype(jnp.float32)
    masked = jnp.where(mask[:, None, :] > 0, features, jnp.zeros_like(features))
    cube = masked.reshape(count, chans, 8, 8, 8)
    received = padded_2(masked, (("space", 0),), count)
    padded = build_pad(widen(received, cube), neighbours)
    pre = jnp.zeros((count, chans, 512), jnp.float32)
    for index, (first, second, third) in enumerate(stencil_offsets):
        pre = pre + jnp.einsum(
            "bcv,cd->bdv",
            window(padded, first, second, third),
            w_subm[index],
            preferred_element_type=jnp.float32,
        )
    hidden = (gelu_tanh(pre) * mask_f[:, None, :]).astype(jnp.bfloat16)
    cmask = jnp.max(mask_f.reshape(count, 4, 2, 4, 2, 4, 2), axis=(2, 4, 6)).reshape(count, 64)
    coarse = jnp.zeros((count, chans, 64), jnp.float32)
    for index in range(8):
        coarse = coarse + jnp.einsum(
            "bcu,cd->bdu", child(hidden, index), w_down[index], preferred_element_type=jnp.float32
        )
    coarse = (coarse * cmask[:, None, :]).astype(jnp.bfloat16)
    pieces = jnp.transpose(coarse.reshape(count, chans, 8, 8), (0, 2, 1, 3)).reshape(
        count, 8, chans * 8
    )
    below = entering(live_count, "space", add_counts, jnp.zeros_like(live_count))
    start = below[0]
    peer_ids = jnp.arange(peers, dtype=jnp.int32)[:, None]
    place_ids = jnp.arange(capacity, dtype=jnp.int32)[None, :]
    which = place_ids * peers + jnp.mod(peer_ids - 8 * start, peers)
    usable = which < 8 * live_count[0]
    chosen = pieces[jnp.clip(which // 8, 0, count - 1), which % 8]
    outbox = jnp.where(usable[..., None], chosen, jnp.zeros((), chosen.dtype))
    inbox = lax.all_to_all(outbox, "space", split_axis=0, concat_axis=0, tiled=True)
    coarse_out = inbox.reshape(peers * capacity, chans * 8)
    returned = lax.all_to_all(
        grad_coarse.reshape(peers, capacity, chans * 8),
        "space",
        split_axis=0,
        concat_axis=0,
        tiled=True,
    )
    stream = 8 * slots[:, None] + jnp.arange(8, dtype=jnp.int32)[None, :]
    taken = returned[jnp.mod(8 * start + stream, peers), stream // peers]
    taken = jnp.where(alive[:, None, None] > 0, taken, jnp.zeros((), taken.dtype))
    dz = jnp.transpose(taken.reshape(count, 8, chans, 8), (0, 2, 1, 3)).reshape(count, chans, 64)
    dz = jnp.where(cmask[:, None, :] > 0, dz, jnp.zeros((), dz.dtype))
    grad_down = jnp.stack(
        [
            jnp.einsum("bcu,bdu->cd", child(hidden, index), dz, preferred_element_type=jnp.float32)
            for index in range(8)
        ]
    )
    dh = place_children(
        [
            jnp.einsum("bdu,cd->bcu", dz, w_down[index], preferred_element_type=jnp.float32)
            for index in range(8)
        ]
    )
    _, pull = jax.vjp(gelu_tanh, pre)
    dpre = pull(dh * mask_f[:, None, :])[0].astype(jnp.bfloat16)
    grad_subm = jnp.stack(
        [
            jnp.einsum(
                "bcv,bdv->cd",
                window(padded, first, second, third),
                dpre,
                preferred_element_type=jnp.float32,
            )
            for first, second, third in stencil_offsets
        ]
    )
    gsource = gradient_source(dpre, neighbours, w_subm)
    lower_part = gsource[:count]
    upper_part = gsource[2 * count : 3 * count]
    from_upper = shifted(lower_part.astype(jnp.bfloat16), "space", -1).astype(jnp.float32)
    from_lower = shifted(upper_part.astype(jnp.bfloat16), "space", 1).astype(jnp.float32)
    total_grad = gsource[count : 2 * count] + from_upper + from_lower
    grad_features = (total_grad.reshape(count, chans, 512) * mask_f[:, None, :]).astype(
        jnp.bfloat16
    )
    grad_subm, grad_down = lax.psum((grad_subm, grad_down), "space")
    return (coarse_out, grad_features, grad_subm, grad_down)


def solution(mesh):
    placed = (
        P(("rep", "space"), None, None),
        P(("rep", "space"), None),
        P(("rep", "space"), None),
        P(("rep", "space")),
        P(),
        P(),
        P(("rep", "space"), None),
    )
    return jax.shard_map(
        per_device,
        mesh=mesh,
        in_specs=placed,
        out_specs=(
            P(("rep", "space"), None),
            P(("rep", "space"), None, None),
            P("rep", None, None),
            P("rep", None, None),
        ),
        check_vma=False,
    )
```

profile of v0, /device:TPU:1, one launch (start us, length us, event | category | flops | bytes accessed | tf_op | source)
XLA Modules:
  0.0 982.0 jit_solution(6809363856094243288)
XLA Ops:
  22.2 13.1 %all-to-all-start.1 = ((bf16[64,2,384]{2,1,0:T(2,128)(2,1)}), bf16[64,2,384]{2,1,0:T(2,128)(2,1)S(1)}, u32[]{:S(2)}, u32[]{:S(2)}) async-start(bf16[64,2,384]{2,1,0:T(2,128)(2,1)} %reshape.4927), calls=%async_computation.1 | async-start | bytes 196608 | tf_op jit(solution)/shard_map/all_to_all | solution.py:171
  47.4 16.9 %all-reduce.14 = s32[64]{0:T(128)S(1)} all-reduce(s32[64]{0:T(128)S(1)} %dynamic-update-slice.214), channel_id=2, replica_groups=mesh['space'=64,'rep'=4] {'space'}, use_global_device_ids=true, to_apply=%add.14 | all-reduce | flops 64 | bytes 512
  172.7 6.0 scatter-add.329
  293.4 20.1 %while.91 = (s32[]{:T(128)}, f32[7,96,8,8,8]{1,4,3,2,0:T(8,128)S(1)}, s32[2,4]{1,0:T(2,128)S(1)}, f32[2,96,1,1,1]{1,4,3,2,0:T(1,128)S(1)}, s32[]{:T(128)}, /*index=5*/s32[5]{0:T(128)S(1)}, s32[1]{0:T(128)}, s32[]{:T(128)}) while((s32[]{:T(128)}, f32[7,96,8,8,8]{1,4,3,2,0:T(8,128)S(1)}, s32[2,4]{1,0:T(2,128)S(1)}, ...), condition=%wide.while_cond.54, body=%wide.while_body.54.sunk | while | flops 213 | bytes 2179 | solution.py:126
  313.5 12.1 %while.92 = (s32[]{:T(128)}, f32[7,96,8,8,8]{1,4,3,2,0:T(8,128)S(1)}, s32[2,3]{1,0:T(2,128)S(1)}, f32[2,96,1,1,8]{1,4,3,2,0:T(8,128)S(1)}, s32[]{:T(128)}, /*index=5*/s32[5]{0:T(128)S(1)}, s32[1]{0:T(128)}) while((s32[]{:T(128)}, f32[7,96,8,8,8]{1,4,3,2,0:T(8,128)S(1)}, s32[2,3]{1,0:T(2,128)S(1)}, f32[2,96,1,1,8]{1,4,3,2,0:T(8,128)S(1)}, ...), condition=%wide.while_cond.55, body=%wide.while_body.55.sunk | while | flops 1557 | bytes 12515 | solution.py:126
  325.6 20.1 %while.93 = (s32[]{:T(128)}, f32[7,96,8,8,8]{1,4,3,2,0:T(8,128)S(1)}, s32[2,4]{1,0:T(2,128)S(1)}, f32[2,96,1,1,1]{1,4,3,2,0:T(1,128)S(1)}, s32[]{:T(128)}, /*index=5*/s32[5]{0:T(128)S(1)}, s32[1]{0:T(128)}, s32[]{:T(128)}) while((s32[]{:T(128)}, f32[7,96,8,8,8]{1,4,3,2,0:T(8,128)S(1)}, s32[2,4]{1,0:T(2,128)S(1)}, ...), condition=%wide.while_cond.56, body=%wide.while_body.56.sunk | while | flops 213 | bytes 2179 | solution.py:126
  345.8 16.1 %while.94 = (s32[]{:T(128)}, f32[7,96,8,8,8]{1,4,3,2,0:T(8,128)S(1)}, s32[2,3]{1,0:T(2,128)S(1)}, f32[2,96,1,8,1]{1,4,3,2,0:T(1,128)S(1)}, s32[]{:T(128)}, /*index=5*/s32[5]{0:T(128)S(1)}, s32[1]{0:T(128)}, s32[]{:T(128)}) while((s32[]{:T(128)}, f32[7,96,8,8,8]{1,4,3,2,0:T(8,128)S(1)}, s32[2,3]{1,0:T(2,128)S(1)}, ...), condition=%wide.while_cond.57, body=%wide.while_body.57.sunk | while | flops 1557 | bytes 15599 | solution.py:126
  362.0 9.2 while.95
  371.2 16.5 %while.96 = (s32[]{:T(128)}, f32[7,96,8,8,8]{1,4,3,2,0:T(8,128)S(1)}, s32[2,3]{1,0:T(2,128)S(1)}, f32[2,96,1,8,1]{1,4,3,2,0:T(1,128)S(1)}, s32[]{:T(128)}, /*index=5*/s32[5]{0:T(128)S(1)}, s32[1]{0:T(128)}, s32[]{:T(128)}) while((s32[]{:T(128)}, f32[7,96,8,8,8]{1,4,3,2,0:T(8,128)S(1)}, s32[2,3]{1,0:T(2,128)S(1)}, ...), condition=%wide.while_cond.59, body=%wide.while_body.59.sunk | while | flops 1557 | bytes 15599 | solution.py:126
  387.7 20.3 %while.97 = (s32[]{:T(128)}, f32[7,96,8,8,8]{1,4,3,2,0:T(8,128)S(1)}, s32[2,4]{1,0:T(2,128)S(1)}, f32[2,96,1,1,1]{1,4,3,2,0:T(1,128)S(1)}, s32[]{:T(128)}, /*index=5*/s32[5]{0:T(128)S(1)}, s32[1]{0:T(128)}, s32[]{:T(128)}) while((s32[]{:T(128)}, f32[7,96,8,8,8]{1,4,3,2,0:T(8,128)S(1)}, s32[2,4]{1,0:T(2,128)S(1)}, ...), condition=%wide.while_cond.60, body=%wide.while_body.60.sunk | while | flops 213 | bytes 2179 | solution.py:126
  408.1 11.9 %while.98 = (s32[]{:T(128)}, f32[7,96,8,8,8]{1,4,3,2,0:T(8,128)S(1)}, s32[2,3]{1,0:T(2,128)S(1)}, f32[2,96,1,1,8]{1,4,3,2,0:T(8,128)S(1)}, s32[]{:T(128)}, /*index=5*/s32[5]{0:T(128)S(1)}, s32[1]{0:T(128)}) while((s32[]{:T(128)}, f32[7,96,8,8,8]{1,4,3,2,0:T(8,128)S(1)}, s32[2,3]{1,0:T(2,128)S(1)}, f32[2,96,1,1,8]{1,4,3,2,0:T(8,128)S(1)}, ...), condition=%wide.while_cond.61, body=%wide.while_body.61.sunk | while | flops 1557 | bytes 12515 | solution.py:126
  420.1 19.5 %while.99 = (s32[]{:T(128)}, f32[7,96,8,8,8]{1,4,3,2,0:T(8,128)S(1)}, s32[2,4]{1,0:T(2,128)S(1)}, f32[2,96,1,1,1]{1,4,3,2,0:T(1,128)S(1)}, s32[]{:T(128)}, /*index=5*/s32[5]{0:T(128)S(1)}, s32[1]{0:T(128)}, s32[]{:T(128)}) while((s32[]{:T(128)}, f32[7,96,8,8,8]{1,4,3,2,0:T(8,128)S(1)}, s32[2,4]{1,0:T(2,128)S(1)}, ...), condition=%wide.while_cond.62, body=%wide.while_body.62.sunk | while | flops 213 | bytes 2179 | solution.py:126
  439.6 15.9 %while.100 = (s32[]{:T(128)}, f32[7,96,8,8,8]{1,4,3,2,0:T(8,128)S(1)}, s32[2,3]{1,0:T(2,128)S(1)}, f32[2,96,8,1,1]{1,4,3,2,0:T(1,128)S(1)}, s32[]{:T(128)}, /*index=5*/s32[5]{0:T(128)S(1)}, s32[1]{0:T(128)}, s32[]{:T(128)}) while((s32[]{:T(128)}, f32[7,96,8,8,8]{1,4,3,2,0:T(8,128)S(1)}, s32[2,3]{1,0:T(2,128)S(1)}, ...), condition=%wide.while_cond.63, body=%wide.while_body.63.sunk | while | flops 1557 | bytes 15599 | solution.py:126
  455.5 9.0 while.101
  464.5 15.2 %while.102 = (s32[]{:T(128)}, f32[7,96,8,8,8]{1,4,3,2,0:T(8,128)S(1)}, s32[2,3]{1,0:T(2,128)S(1)}, f32[2,96,8,1,1]{1,4,3,2,0:T(1,128)S(1)}, s32[]{:T(128)}, /*index=5*/s32[5]{0:T(128)S(1)}, s32[1]{0:T(128)}, s32[]{:T(128)}) while((s32[]{:T(128)}, f32[7,96,8,8,8]{1,4,3,2,0:T(8,128)S(1)}, s32[2,3]{1,0:T(2,128)S(1)}, ...), condition=%wide.while_cond.65, body=%wide.while_body.65.sunk | while | flops 1557 | bytes 15599 | solution.py:126
  479.8 11.7 %while.103 = (s32[]{:T(128)}, f32[7,96,8,8,8]{1,4,3,2,0:T(8,128)S(1)}, s32[2,2]{1,0:T(2,128)S(1)}, f32[2,96,8,8,1]{1,4,3,2,0:T(1,128)S(1)}, s32[]{:T(128)}, /*index=5*/s32[5]{0:T(128)S(1)}, s32[1]{0:T(128)}, s32[]{:T(128)}) while((s32[]{:T(128)}, f32[7,96,8,8,8]{1,4,3,2,0:T(8,128)S(1)}, s32[2,2]{1,0:T(2,128)S(1)}, ...), condition=%wide.while_cond.66, body=%wide.while_body.66.sunk | while | flops 12309 | bytes 123099 | solution.py:126
  492.5 12.3 %while.104 = (s32[]{:T(128)}, f32[7,96,8,8,8]{1,4,3,2,0:T(8,128)S(1)}, s32[2,2]{1,0:T(2,128)S(1)}, f32[2,96,8,8,1]{1,4,3,2,0:T(1,128)S(1)}, s32[]{:T(128)}, /*index=5*/s32[5]{0:T(128)S(1)}, s32[1]{0:T(128)}, s32[]{:T(128)}) while((s32[]{:T(128)}, f32[7,96,8,8,8]{1,4,3,2,0:T(8,128)S(1)}, s32[2,2]{1,0:T(2,128)S(1)}, ...), condition=%wide.while_cond.67, body=%wide.while_body.67.sunk | while | flops 12309 | bytes 123099 | solution.py:126
  504.9 15.9 %while.105 = (s32[]{:T(128)}, f32[7,96,8,8,8]{1,4,3,2,0:T(8,128)S(1)}, s32[2,3]{1,0:T(2,128)S(1)}, f32[2,96,8,1,1]{1,4,3,2,0:T(1,128)S(1)}, s32[]{:T(128)}, /*index=5*/s32[5]{0:T(128)S(1)}, s32[1]{0:T(128)}, s32[]{:T(128)}) while((s32[]{:T(128)}, f32[7,96,8,8,8]{1,4,3,2,0:T(8,128)S(1)}, s32[2,3]{1,0:T(2,128)S(1)}, ...), condition=%wide.while_cond.68, body=%wide.while_body.68.sunk | while | flops 1557 | bytes 15599 | solution.py:126
  520.8 9.3 while.106
  530.2 15.6 %while.107 = (s32[]{:T(128)}, f32[7,96,8,8,8]{1,4,3,2,0:T(8,128)S(1)}, s32[2,3]{1,0:T(2,128)S(1)}, f32[2,96,8,1,1]{1,4,3,2,0:T(1,128)S(1)}, s32[]{:T(128)}, /*index=5*/s32[5]{0:T(128)S(1)}, s32[1]{0:T(128)}, s32[]{:T(128)}) while((s32[]{:T(128)}, f32[7,96,8,8,8]{1,4,3,2,0:T(8,128)S(1)}, s32[2,3]{1,0:T(2,128)S(1)}, ...), condition=%wide.while_cond.70, body=%wide.while_body.70.sunk | while | flops 1557 | bytes 15599 | solution.py:126
  545.8 19.1 %while.108 = (s32[]{:T(128)}, f32[7,96,8,8,8]{1,4,3,2,0:T(8,128)S(1)}, s32[2,4]{1,0:T(2,128)S(1)}, f32[2,96,1,1,1]{1,4,3,2,0:T(1,128)S(1)}, s32[]{:T(128)}, /*index=5*/s32[5]{0:T(128)S(1)}, s32[1]{0:T(128)}, s32[]{:T(128)}) while((s32[]{:T(128)}, f32[7,96,8,8,8]{1,4,3,2,0:T(8,128)S(1)}, s32[2,4]{1,0:T(2,128)S(1)}, ...), condition=%wide.while_cond.71, body=%wide.while_body.71.sunk | while | flops 213 | bytes 2179 | solution.py:126
  564.9 11.6 %while.109 = (s32[]{:T(128)}, f32[7,96,8,8,8]{1,4,3,2,0:T(8,128)S(1)}, s32[2,3]{1,0:T(2,128)S(1)}, f32[2,96,1,1,8]{1,4,3,2,0:T(8,128)S(1)}, s32[]{:T(128)}, /*index=5*/s32[5]{0:T(128)S(1)}, s32[1]{0:T(128)}) while((s32[]{:T(128)}, f32[7,96,8,8,8]{1,4,3,2,0:T(8,128)S(1)}, s32[2,3]{1,0:T(2,128)S(1)}, f32[2,96,1,1,8]{1,4,3,2,0:T(8,128)S(1)}, ...), condition=%wide.while_cond.72, body=%wide.while_body.72.sunk | while | flops 1557 | bytes 12515 | solution.py:126
  576.5 19.3 %while.110 = (s32[]{:T(128)}, f32[7,96,8,8,8]{1,4,3,2,0:T(8,128)S(1)}, s32[2,4]{1,0:T(2,128)S(1)}, f32[2,96,1,1,1]{1,4,3,2,0:T(1,128)S(1)}, s32[]{:T(128)}, /*index=5*/s32[5]{0:T(128)S(1)}, s32[1]{0:T(128)}, s32[]{:T(128)}) while((s32[]{:T(128)}, f32[7,96,8,8,8]{1,4,3,2,0:T(8,128)S(1)}, s32[2,4]{1,0:T(2,128)S(1)}, ...), condition=%wide.while_cond.73, body=%wide.while_body.73.sunk | while | flops 213 | bytes 2179 | solution.py:126
  595.8 15.2 %while.111 = (s32[]{:T(128)}, f32[7,96,8,8,8]{1,4,3,2,0:T(8,128)S(1)}, s32[2,3]{1,0:T(2,128)S(1)}, f32[2,96,1,8,1]{1,4,3,2,0:T(1,128)S(1)}, s32[]{:T(128)}, /*index=5*/s32[5]{0:T(128)S(1)}, s32[1]{0:T(128)}, s32[]{:T(128)}) while((s32[]{:T(128)}, f32[7,96,8,8,8]{1,4,3,2,0:T(8,128)S(1)}, s32[2,3]{1,0:T(2,128)S(1)}, ...), condition=%wide.while_cond.74, body=%wide.while_body.74.sunk | while | flops 1557 | bytes 15599 | solution.py:126
  611.1 8.8 while.112
  619.9 15.6 %while.113 = (s32[]{:T(128)}, f32[7,96,8,8,8]{1,4,3,2,0:T(8,128)S(1)}, s32[2,3]{1,0:T(2,128)S(1)}, f32[2,96,1,8,1]{1,4,3,2,0:T(1,128)S(1)}, s32[]{:T(128)}, /*index=5*/s32[5]{0:T(128)S(1)}, s32[1]{0:T(128)}, s32[]{:T(128)}) while((s32[]{:T(128)}, f32[7,96,8,8,8]{1,4,3,2,0:T(8,128)S(1)}, s32[2,3]{1,0:T(2,128)S(1)}, ...), condition=%wide.while_cond.76, body=%wide.while_body.76.sunk | while | flops 1557 | bytes 15599 | solution.py:126
  635.5 18.8 %while.114 = (s32[]{:T(128)}, f32[7,96,8,8,8]{1,4,3,2,0:T(8,128)S(1)}, s32[2,4]{1,0:T(2,128)S(1)}, f32[2,96,1,1,1]{1,4,3,2,0:T(1,128)S(1)}, s32[]{:T(128)}, /*index=5*/s32[5]{0:T(128)S(1)}, s32[1]{0:T(128)}, s32[]{:T(128)}) while((s32[]{:T(128)}, f32[7,96,8,8,8]{1,4,3,2,0:T(8,128)S(1)}, s32[2,4]{1,0:T(2,128)S(1)}, ...), condition=%wide.while_cond.77, body=%wide.while_body.77.sunk | while | flops 213 | bytes 2179 | solution.py:126
  654.4 11.5 %while.115 = (s32[]{:T(128)}, f32[7,96,8,8,8]{1,4,3,2,0:T(8,128)S(1)}, s32[2,3]{1,0:T(2,128)S(1)}, f32[2,96,1,1,8]{1,4,3,2,0:T(8,128)S(1)}, s32[]{:T(128)}, /*index=5*/s32[5]{0:T(128)S(1)}, s32[1]{0:T(128)}) while((s32[]{:T(128)}, f32[7,96,8,8,8]{1,4,3,2,0:T(8,128)S(1)}, s32[2,3]{1,0:T(2,128)S(1)}, f32[2,96,1,1,8]{1,4,3,2,0:T(8,128)S(1)}, ...), condition=%wide.while_cond.78, body=%wide.while_body.78.sunk | while | flops 1557 | bytes 12515 | solution.py:126
  665.9 19.4 %while.116 = (s32[]{:T(128)}, f32[7,96,8,8,8]{1,4,3,2,0:T(8,128)S(1)}, s32[2,4]{1,0:T(2,128)S(1)}, f32[2,96,1,1,1]{1,4,3,2,0:T(1,128)S(1)}, s32[]{:T(128)}, /*index=5*/s32[5]{0:T(128)S(1)}, s32[1]{0:T(128)}, s32[]{:T(128)}) while((s32[]{:T(128)}, f32[7,96,8,8,8]{1,4,3,2,0:T(8,128)S(1)}, s32[2,4]{1,0:T(2,128)S(1)}, ...), condition=%wide.while_cond.79, body=%wide.while_body.79.sunk | while | flops 213 | bytes 2179 | solution.py:126
  702.1 77.8 %all-to-all-start = ((bf16[64,2,384]{2,1,0:T(2,128)(2,1)}), bf16[64,2,384]{2,1,0:T(2,128)(2,1)S(1)}, u32[]{:S(2)}, u32[]{:S(2)}) async-start(bf16[64,2,384]{2,1,0:T(2,128)(2,1)} %reshape.4925), calls=%async_computation | async-start | bytes 196608 | tf_op jit(solution)/shard_map/all_to_all | solution.py:169
  780.9 9.2 all-to-all-done
  792.7 179.0 %all-reduce.18.cloned.1.call-done = (f32[27,96,96]{2,1,0:T(8,128)}, f32[8,96,96]{2,1,0:T(8,128)}) async-done(((f32[27,96,96]{2,1,0:T(8,128)}, f32[8,96,96]{2,1,0:T(8,128)}), (f32[27,96,96]{2,1,0:T(8,128)}, f32[8,96,96]{2,1,0:T(8,128)})) %all-reduce.18.cloned.1.call-update) | async-done | bytes 1290256 | tf_op jit(solution)/shard_map/psum | solution.py:217
  (1069 shorter events, 660.0 us)
Async XLA Ops:
  12.7 69.4 %collective-permute-start = (bf16[2,96,512]{2,1,0:T(8,128)(2,1)S(1)}, bf16[2,96,512]{2,1,0:T(8,128)(2,1)S(1)}, u32[]{:S(2)}, u32[]{:S(2)}) collective-permute-start(bf16[2,96,512]{2,1,0:T(8,128)(2,1)S(1)} %broadcast_select_fusion.19), channel_id=1, source_target_pairs={{0,4},{4,8},{8,12},{12,16},{16,20},{20,24},{24,28},{28,32},{32,36}... | collective-permute-start | bytes 589832 | tf_op jit(solution)/shard_map/ppermute | solution.py:19
  17.6 64.6 %collective-permute-start.1 = (bf16[2,96,512]{2,1,0:T(8,128)(2,1)S(1)}, bf16[2,96,512]{2,1,0:T(8,128)(2,1)S(1)}, u32[]{:S(2)}, u32[]{:S(2)}) collective-permute-start(bf16[2,96,512]{2,1,0:T(8,128)(2,1)S(1)} %broadcast_select_fusion.19), channel_id=1, source_target_pairs={{4,0},{8,4},{12,8},{16,12},{20,16},{24,20},{28,24},{32,28},{36,32}... | collective-permute-start | bytes 589832 | tf_op jit(solution)/shard_map/ppermute | solution.py:20
  22.2 55.8 %all-to-all-start.1 = ((bf16[64,2,384]{2,1,0:T(2,128)(2,1)}), bf16[64,2,384]{2,1,0:T(2,128)(2,1)S(1)}, u32[]{:S(2)}, u32[]{:S(2)}) async-start(bf16[64,2,384]{2,1,0:T(2,128)(2,1)} %reshape.4927), calls=%async_computation.1 | async-start | bytes 196608 | tf_op jit(solution)/shard_map/all_to_all | solution.py:171
  293.3 114.8 %copy-start.81 = (f32[2,96,1,1,8]{1,4,3,2,0:T(8,128)S(1)}, f32[2,96,1,1,8]{1,4,3,2,0:T(8,128)}, u32[]{:S(2)}) copy-start(f32[2,96,1,1,8]{1,4,3,2,0:T(8,128)} %get-tuple-element.2440) | copy-start | bytes 18436
  293.3 114.8 %copy-start.138 = (s32[2,3]{1,0:T(2,128)S(1)}, s32[2,3]{1,0:T(2,128)}, u32[]{:S(2)}) copy-start(s32[2,3]{1,0:T(2,128)} %get-tuple-element.2439) | copy-start | bytes 76
  293.3 126.7 %copy-start.88 = (f32[2,96,1,1,1]{1,4,3,2,0:T(1,128)S(1)}, f32[2,96,1,1,1]{1,4,3,2,0:T(1,128)}, u32[]{:S(2)}) copy-start(f32[2,96,1,1,1]{1,4,3,2,0:T(1,128)} %get-tuple-element.2461) | copy-start | bytes 2308
  293.3 126.7 %copy-start.117 = (s32[2,4]{1,0:T(2,128)S(1)}, s32[2,4]{1,0:T(2,128)}, u32[]{:S(2)}) copy-start(s32[2,4]{1,0:T(2,128)} %get-tuple-element.2460) | copy-start | bytes 100
  293.3 146.2 %copy-start.80 = (f32[2,96,8,1,1]{1,4,3,2,0:T(1,128)S(1)}, f32[2,96,8,1,1]{1,4,3,2,0:T(1,128)}, u32[]{:S(2)}) copy-start(f32[2,96,8,1,1]{1,4,3,2,0:T(1,128)} %get-tuple-element.2485) | copy-start | bytes 18436
  293.3 146.2 %copy-start.128 = (s32[2,3]{1,0:T(2,128)S(1)}, s32[2,3]{1,0:T(2,128)}, u32[]{:S(2)}) copy-start(s32[2,3]{1,0:T(2,128)} %concatenate.290) | copy-start | bytes 76
  293.4 146.2 %copy-start.155 = (s32[5]{0:T(128)S(1)}, s32[5]{0:T(128)}, u32[]{:S(2)}) copy-start(s32[5]{0:T(128)} %constant.3328) | copy-start | bytes 64
  313.5 142.0 %copy-start.59 = (f32[2,96,8,1,8]{1,4,3,2,0:T(8,128)S(1)}, f32[2,96,8,1,8]{1,4,3,2,0:T(8,128)}, u32[]{:S(2)}) copy-start(f32[2,96,8,1,8]{1,4,3,2,0:T(8,128)} %get-tuple-element.2509) | copy-start | bytes 147460
  313.5 142.0 %copy-start.127 = (s32[2,2]{1,0:T(2,128)S(1)}, s32[2,2]{1,0:T(2,128)}, u32[]{:S(2)}) copy-start(s32[2,2]{1,0:T(2,128)} %concatenate.291) | copy-start | bytes 52
  313.5 142.0 %copy-start.156 = (s32[5]{0:T(128)S(1)}, s32[5]{0:T(128)}, u32[]{:S(2)}) copy-start(s32[5]{0:T(128)} %constant.3342) | copy-start | bytes 64
  345.7 118.8 %copy-start.79 = (f32[2,96,8,1,1]{1,4,3,2,0:T(1,128)S(1)}, f32[2,96,8,1,1]{1,4,3,2,0:T(1,128)}, u32[]{:S(2)}) copy-start(f32[2,96,8,1,1]{1,4,3,2,0:T(1,128)} %get-tuple-element.2530) | copy-start | bytes 18436
  345.7 118.8 %copy-start.137 = (s32[2,3]{1,0:T(2,128)S(1)}, s32[2,3]{1,0:T(2,128)}, u32[]{:S(2)}) copy-start(s32[2,3]{1,0:T(2,128)} %get-tuple-element.2529) | copy-start | bytes 76
  361.9 117.9 %copy-start.58 = (f32[2,96,8,8,1]{1,4,3,2,0:T(1,128)S(1)}, f32[2,96,8,8,1]{1,4,3,2,0:T(1,128)}, u32[]{:S(2)}) copy-start(f32[2,96,8,8,1]{1,4,3,2,0:T(1,128)} %get-tuple-element.2554) | copy-start | bytes 147460
  361.9 117.9 %copy-start.126 = (s32[2,2]{1,0:T(2,128)S(1)}, s32[2,2]{1,0:T(2,128)}, u32[]{:S(2)}) copy-start(s32[2,2]{1,0:T(2,128)} %concatenate.293) | copy-start | bytes 52
  361.9 117.9 %copy-start.157 = (s32[5]{0:T(128)S(1)}, s32[5]{0:T(128)}, u32[]{:S(2)}) copy-start(s32[5]{0:T(128)} %constant.3368) | copy-start | bytes 64
  387.7 103.8 %copy-start.94 = (s32[2]{0:T(128)S(1)}, s32[2]{0:T(128)}, u32[]{:S(2)}) copy-start(s32[2]{0:T(128)} %copy-done.93) | copy-start | bytes 28
  492.5 103.3 %copy-start.75 = (f32[2,96,1,8,1]{1,4,3,2,0:T(1,128)S(1)}, f32[2,96,1,8,1]{1,4,3,2,0:T(1,128)}, u32[]{:S(2)}) copy-start(f32[2,96,1,8,1]{1,4,3,2,0:T(1,128)} %get-tuple-element.2740) | copy-start | bytes 18436
  492.5 118.5 %copy-start.122 = (s32[2,2]{1,0:T(2,128)S(1)}, s32[2,2]{1,0:T(2,128)}, u32[]{:S(2)}) copy-start(s32[2,2]{1,0:T(2,128)} %concatenate.302) | copy-start | bytes 52
  504.8 115.0 %copy-start.74 = (f32[2,96,1,8,1]{1,4,3,2,0:T(1,128)S(1)}, f32[2,96,1,8,1]{1,4,3,2,0:T(1,128)}, u32[]{:S(2)}) copy-start(f32[2,96,1,8,1]{1,4,3,2,0:T(1,128)} %get-tuple-element.2785) | copy-start | bytes 18436
  504.9 115.0 %copy-start.121 = (s32[2,3]{1,0:T(2,128)S(1)}, s32[2,3]{1,0:T(2,128)}, u32[]{:S(2)}) copy-start(s32[2,3]{1,0:T(2,128)} %concatenate.303) | copy-start | bytes 76
  520.8 114.7 %copy-start.85 = (f32[2,96,1,1,1]{1,4,3,2,0:T(1,128)S(1)}, f32[2,96,1,1,1]{1,4,3,2,0:T(1,128)}, u32[]{:S(2)}) copy-start(f32[2,96,1,1,1]{1,4,3,2,0:T(1,128)} %get-tuple-element.2809) | copy-start | bytes 2308
  520.8 114.7 %copy-start.115 = (s32[2,4]{1,0:T(2,128)S(1)}, s32[2,4]{1,0:T(2,128)}, u32[]{:S(2)}) copy-start(s32[2,4]{1,0:T(2,128)} %get-tuple-element.2808) | copy-start | bytes 100
  530.1 124.2 %copy-start.120 = (s32[2,3]{1,0:T(2,128)S(1)}, s32[2,3]{1,0:T(2,128)}, u32[]{:S(2)}) copy-start(s32[2,3]{1,0:T(2,128)} %concatenate.305) | copy-start | bytes 76
  530.1 135.7 %copy-start.92 = (f32[2,96,1,1,1]{1,4,3,2,0:T(1,128)S(1)}, f32[2,96,1,1,1]{1,4,3,2,0:T(1,128)}, u32[]{:S(2)}) copy-start(f32[2,96,1,1,1]{1,4,3,2,0:T(1,128)} %slice.3868) | copy-start | bytes 2308
  530.2 135.7 %copy-start.114 = (s32[2,4]{1,0:T(2,128)S(1)}, s32[2,4]{1,0:T(2,128)}, u32[]{:S(2)}) copy-start(s32[2,4]{1,0:T(2,128)} %get-tuple-element.2853) | copy-start | bytes 100
  686.3 104.5 %collective-permute-start.2 = (bf16[2,96,8,8,8]{1,4,3,2,0:T(8,128)(2,1)}, bf16[2,96,8,8,8]{1,4,3,2,0:T(8,128)(2,1)S(1)}, u32[]{:S(2)}, u32[]{:S(2)}) collective-permute-start(bf16[2,96,8,8,8]{1,4,3,2,0:T(8,128)(2,1)} %get-tuple-element.1269), channel_id=1, source_target_pairs={{4,0},{8,4},{12,8},{16,12},{20,16},{24,20},{28,24},{32,28},{36,32}... | collective-permute-start | bytes 589832 | tf_op jit(solution)/shard_map/ppermute | solution.py:39
  691.7 99.1 %collective-permute-start.3 = (bf16[2,96,8,8,8]{1,4,3,2,0:T(8,128)(2,1)S(1)}, bf16[2,96,8,8,8]{1,4,3,2,0:T(8,128)(2,1)}, u32[]{:S(2)}, u32[]{:S(2)}) collective-permute-start(bf16[2,96,8,8,8]{1,4,3,2,0:T(8,128)(2,1)S(1)} %get-tuple-element.1270), channel_id=1, source_target_pairs={{0,4},{4,8},{8,12},{12,16},{16,20},{20,24},{24,28},{28,32},{32,36}... | collective-permute-start | bytes 589832 | tf_op jit(solution)/shard_map/ppermute | solution.py:39
  702.1 88.0 %all-to-all-start = ((bf16[64,2,384]{2,1,0:T(2,128)(2,1)}), bf16[64,2,384]{2,1,0:T(2,128)(2,1)S(1)}, u32[]{:S(2)}, u32[]{:S(2)}) async-start(bf16[64,2,384]{2,1,0:T(2,128)(2,1)} %reshape.4925), calls=%async_computation | async-start | bytes 196608 | tf_op jit(solution)/shard_map/all_to_all | solution.py:169
  779.9 191.8 %all-reduce.18.cloned.1.call-start = ((), (), s32[]{:S(2)}) async-start(), calls=%async_computation.2 | async-start | bytes 3440640 | tf_op jit(solution)/shard_map/psum | solution.py:217
  (133 other events, 2227.0 us)
Sparse Core Ops, SparseCore 0:
  784.8 186.8 all-reduce.17
where the time goes:
time: 998 us; the launch traced here: 982 us
  local copies, waits for them, and re-layouts  392 us (39%)
  other arithmetic  211 us (21%)
  waiting for transfers between devices  188 us (19%)
  starting transfers between devices  108 us (11%)
  matrix products  44.9 us (4%)
  between operations  18.9 us (2%)
  blocking collectives  16.9 us (2%)
    scatter-add x192, local copies, waits for them, and re-layouts  218 us
    psum x1, waiting for transfers between devices, per_device(): grad_subm, grad_down = lax.psum((grad_subm, grad_down), 'space')  179 us
    scatter-add x104, other arithmetic  170 us
    all_to_all x1, starting transfers between devices, per_device(): lax.all_to_all(outbox, 'space', split_axis=0, concat_axis=0, tiled=True)  77.8 us
    scatter-add x19, local copies, waits for them, and re-layouts, gradient_source(): gpad = gpad.at[:, :, 1 + first:9 + first, 1 + second:9 + second, 1 + thir...  64.4 us
    transpose x27, local copies, waits for them, and re-layouts, gradient_source(): jnp.einsum('cd,bdv->bcv', w_subm[index], dpre, preferred_element_type=jnp...  38.3 us
    dot_general x27, matrix products, gradient_source(): jnp.einsum('cd,bdv->bcv', w_subm[index], dpre, preferred_element_type=jnp...  24.2 us
    unnamed x336, local copies, waits for them, and re-layouts  21.7 us
  transfers between devices with their start and end apart: 7, of which 2 were waited for; matrix products, arithmetic and copies ran while one was open for 4% of the time, Pallas kernels for 0%

commit v1 on v0

v1 whole, which is shorter than its diff:
```python
import functools

import jax
import jax.numpy as jnp
from jax import lax
from jax.experimental import pallas as pl
from jax.experimental.pallas import tpu as pltpu
from jax.sharding import PartitionSpec as P

C, L, V = 96, 128, 512
OFFSETS = [(a, b, c) for a in (-1, 0, 1) for b in (-1, 0, 1) for c in (-1, 0, 1)]
VMEM_LIMIT = 50 * 2**20
F32, BF16 = jnp.float32, jnp.bfloat16
NT = (((1,), (1,)), ((), ()))


def segments(a, b, c):
    span = {-1: [(7, 0)], 0: [(i, i + 1) for i in range(8)], 1: [(0, 9)]}
    xs, ys, zs = span[a], span[b], span[c]
    if c == 0:
        return [(x * 64 + y * 8, 1, tx * 100 + ty * 10 + 1, 1, 8) for x, tx in xs for y, ty in ys]
    z, tz = zs[0]
    if b == 0:
        return [(x * 64 + z, 8, tx * 100 + 10 + tz, 10, 8) for x, tx in xs]
    y, ty = ys[0]
    if a == 0:
        return [(y * 8 + z, 64, 100 + ty * 10 + tz, 100, 8)]
    x, tx = xs[0]
    return [(x * 64 + y * 8 + z, 1, tx * 100 + ty * 10 + tz, 1, 1)]


def rows(start, count, stride):
    return pl.ds(start, count) if stride == 1 else pl.ds(start, count, stride=stride)


def mask_row(words, live, g):
    lane = lax.broadcasted_iota(jnp.int32, (1, V), 1)
    word = jnp.zeros((1, V), jnp.int32)
    for w in range(16):
        word = jnp.where(lane // 32 == w, words[g, w], word)
    bit = jnp.bitwise_and(jnp.right_shift(word, jnp.bitwise_and(lane, 31)), 1)
    return jnp.where(g < live, bit, 0)


def masked_rows(features, words, live, g):
    bit = mask_row(words, live, g)
    values = jnp.where(bit > 0, features[g].astype(F32), 0.0)
    marks = jnp.broadcast_to(bit.astype(F32), (L - C, V))
    return jnp.transpose(jnp.concatenate([values, marks], axis=0)).astype(BF16)


def mask_kernel(live_ref, occupancy_ref, features_ref, out_ref):
    for g in range(2):
        out_ref[g] = masked_rows(features_ref, occupancy_ref, live_ref[0], g)


def block_kernel(
    table, live_ref, lower, own, upper, inbox, w_subm, w_down,
    outbox, part_own, part_lower, part_upper, sums,
    source, pad, cols, wf, wb, wd, perm, spread, pre, hid, dpre3, u, gpad, gsource,
):
    me = lax.axis_index("space")
    wf[...] = jnp.zeros_like(wf)
    wb[...] = jnp.zeros_like(wb)
    wd[...] = jnp.zeros_like(wd)
    for k in range(27):
        a, bc = divmod(k, 9)
        w = w_subm[k]
        wf[k * L : k * L + C, :C] = w
        wb[bc * L : bc * L + C, a * L : a * L + C] = w
    for j in range(8):
        wd[j * L : j * L + C, :C] = w_down[j]
    i = lax.broadcasted_iota(jnp.int32, (V, V), 0)
    v = lax.broadcasted_iota(jnp.int32, (V, V), 1)
    j, t = i // 64, i % 64
    x, y, z = 2 * (t // 16) + j // 4, 2 * (t // 4 % 4) + j // 2 % 2, 2 * (t % 4) + j % 2
    perm[...] = jnp.where(x * 64 + y * 8 + z == v, 1.0, 0.0).astype(BF16)
    spread[...] = jnp.where(
        lax.broadcasted_iota(jnp.int32, (L, 6 * L), 1) // 8
        == lax.broadcasted_iota(jnp.int32, (L, 6 * L), 0),
        1.0, 0.0,
    ).astype(BF16)
    pick = (
        lax.broadcasted_iota(jnp.int32, (8, L), 1) % 8 == lax.broadcasted_iota(jnp.int32, (8, L), 0)
    )

    for n, ref in enumerate((lower, own, upper)):
        for g in range(2):
            source[(2 * n + g) * V : (2 * n + g + 1) * V, :] = ref[g].astype(F32)
    source[6 * V :, :] = jnp.zeros((V, L), F32)

    for g in range(2):
        for k, offset in enumerate(OFFSETS):
            base = table[g, k] * V
            for s0, ss, p0, ps, count in segments(*offset):
                pad[rows(g * 1000 + p0, count, ps), :] = source[rows(base + s0, count, ss), :]

    def columns(gx, carry):
        for b in range(3):
            for c in range(3):
                piece = jnp.concatenate(
                    [pad[pl.ds(gx * 100 + (yy + b) * 10 + c, 8), :] for yy in range(8)], axis=0
                )
                bc = 3 * b + c
                cols[pl.ds(gx * 64, 64), bc * L : (bc + 1) * L] = piece.astype(BF16)
        return carry

    lax.fori_loop(0, 20, columns, 0)

    for g in range(2):
        acc = jnp.zeros((V, L), F32)
        for a in range(3):
            acc += jnp.dot(
                cols[g * 640 + a * 64 : g * 640 + a * 64 + V, :],
                wf[a * 9 * L : (a + 1) * 9 * L, :],
                preferred_element_type=F32,
            )
        pre[g * V : (g + 1) * V, :] = acc

    counts = inbox[:, 6, :]
    place = lax.broadcasted_iota(jnp.int32, (64, L), 0)
    start = jnp.sum(jnp.where(place < me, counts, 0.0), axis=0, keepdims=True)[0, 0].astype(jnp.int32)
    live = live_ref[0]
    outbox[...] = jnp.zeros_like(outbox)
    s, q = 0.7978845608028654, 0.044715
    dpre3[...] = jnp.zeros_like(dpre3)
    down = jnp.zeros((L, 8 * L), F32)
    for g in range(2):
        mask = jnp.broadcast_to(own[g, :, C : C + 1].astype(F32), (V, L))
        tt = pre[g * V : (g + 1) * V, :]
        th = jnp.tanh(s * (tt + q * tt * tt * tt))
        hidden = (0.5 * tt * (1.0 + th) * mask).astype(BF16)
        slope = (0.5 * (1.0 + th) + 0.5 * tt * (1.0 - th * th) * (s * (1.0 + 3.0 * q * tt * tt))) * mask
        both = jnp.dot(
            perm[...], jnp.concatenate([hidden, mask.astype(BF16)], axis=1),
            preferred_element_type=F32,
        )
        kids = both[:, :L].astype(BF16)
        hid[...] = kids
        cmask = both[:64, L:]
        coarse = jnp.dot(kids[:64], wd[:L, :], preferred_element_type=F32)
        for j in range(1, 8):
            cmask = jnp.maximum(cmask, both[j * 64 : (j + 1) * 64, L:])
            coarse += jnp.dot(
                kids[j * 64 : (j + 1) * 64], wd[j * L : (j + 1) * L, :], preferred_element_type=F32
            )
        coarse = (coarse * cmask).astype(BF16)
        group = jnp.bitwise_and(start + g, 7)
        alive = g < live
        flat = jnp.dot(coarse, spread[...], preferred_element_type=F32)
        for t in range(8):
            for n in range(6):
                tile = jnp.where(pick, flat[t * 8 : t * 8 + 8, n * L : (n + 1) * L], 0.0)
                line = jnp.where(alive, jnp.sum(tile, axis=0, keepdims=True), 0.0)

                @pl.when(alive)
                def _():
                    outbox[group * 8 + t, n : n + 1, :] = line

        dz = []
        for t in range(8):
            dz.append(
                jnp.concatenate(
                    [
                        jnp.where(pick, jnp.broadcast_to(inbox[group * 8 + t, n : n + 1, :], (8, L)), 0.0)
                        for n in range(6)
                    ],
                    axis=1,
                )
            )
        dz = jnp.concatenate(dz, axis=0).astype(BF16)
        dz = lax.dot_general(dz, spread[...], NT, preferred_element_type=F32)
        dz = jnp.where(alive & (cmask > 0), dz, 0.0).astype(BF16)
        dzt = jnp.transpose(dz.astype(F32)).astype(BF16)
        down += jnp.dot(
            dzt, jnp.concatenate([kids[j * 64 : (j + 1) * 64] for j in range(8)], axis=1),
            preferred_element_type=F32,
        )
        dh = jnp.concatenate(
            [
                lax.dot_general(dz, wd[j * L : (j + 1) * L, :], NT, preferred_element_type=F32)
                for j in range(8)
            ],
            axis=0,
        )
        high = dh.astype(BF16)
        low = (dh - high.astype(F32)).astype(BF16)
        dh = lax.dot_general(
            perm[...], jnp.concatenate([high, low], axis=1), (((0,), (0,)), ((), ())),
            preferred_element_type=F32,
        )
        dh = dh[:, :L] + dh[:, L:]
        dpre = slope * dh
        dpre16 = dpre.astype(BF16)
        for a in range(3):
            dpre3[g * 640 + a * 64 : g * 640 + a * 64 + V, a * L : (a + 1) * L] = dpre16
        hid[...] = dpre16
        pre[g * V : (g + 1) * V, :] = dpre
    for j in range(8):
        sums[27 + j] = down[:C, j * L : (j + 1) * L].astype(sums.dtype)

    dt = jnp.transpose(pre[...]).astype(BF16)
    for a in range(3):
        for bc in range(0, 9, 2):
            lanes = slice(bc * L, min(bc + 2, 9) * L)
            total = jnp.dot(
                dt[:, :V], cols[a * 64 : a * 64 + V, lanes], preferred_element_type=F32
            ) + jnp.dot(
                dt[:, V:], cols[640 + a * 64 : 640 + a * 64 + V, lanes], preferred_element_type=F32
            )
            for n in range(min(2, 9 - bc)):
                sums[a * 9 + bc + n] = total[:C, n * L : (n + 1) * L].astype(sums.dtype)

    gpad[...] = jnp.zeros_like(gpad)
    for bc in range(0, 9, 2):
        width = min(2, 9 - bc)
        u[:, : width * L] = lax.dot_general(
            dpre3[...], wb[bc * L : (bc + width) * L, :], NT, preferred_element_type=F32
        )

        def add(gx, carry):
            for n in range(width):
                b, c = divmod(bc + n, 3)
                for yy in range(8):
                    at = pl.ds(gx * 100 + (yy + b) * 10 + c, 8)
                    gpad[at, :] += u[pl.ds(gx * 64 + yy * 8, 8), n * L : (n + 1) * L]
            return carry

        lax.fori_loop(0, 20, add, 0)

    gsource[...] = jnp.zeros_like(gsource)
    for g in range(2):
        for k, offset in enumerate(OFFSETS):
            base = table[g, k] * V
            for s0, ss, p0, ps, count in segments(*offset):
                gsource[rows(base + s0, count, ss), :] += gpad[rows(g * 1000 + p0, count, ps), :]
    for g in range(2):
        part_lower[g] = gsource[g * V : (g + 1) * V, :].astype(BF16)
        part_own[g] = gsource[(2 + g) * V : (3 + g) * V, :]
        part_upper[g] = gsource[(4 + g) * V : (5 + g) * V, :].astype(BF16)


def smem():
    return pl.BlockSpec(memory_space=pltpu.SMEM)


def vmem(n):
    return [pl.BlockSpec(memory_space=pltpu.VMEM)] * n


def run_blocks(neighbours, live_count, lower, own, upper, inbox, w_subm, w_down, kind=F32):
    return pl.pallas_call(
        block_kernel,
        out_shape=(
            jax.ShapeDtypeStruct((64, 8, L), F32),
            jax.ShapeDtypeStruct((2, V, L), F32),
            jax.ShapeDtypeStruct((2, V, L), BF16),
            jax.ShapeDtypeStruct((2, V, L), BF16),
            jax.ShapeDtypeStruct((35, C, L), kind),
        ),
        in_specs=[smem(), smem()] + vmem(6),
        out_specs=tuple(vmem(5)),
        scratch_shapes=[
            pltpu.VMEM((7 * V, L), F32),
            pltpu.VMEM((2000, L), F32),
            pltpu.VMEM((1280, 9 * L), BF16),
            pltpu.VMEM((27 * L, L), BF16),
            pltpu.VMEM((9 * L, 3 * L), BF16),
            pltpu.VMEM((8 * L, L), BF16),
            pltpu.VMEM((V, V), BF16),
            pltpu.VMEM((L, 6 * L), BF16),
            pltpu.VMEM((2 * V, L), F32),
            pltpu.VMEM((V, L), BF16),
            pltpu.VMEM((1280, 3 * L), BF16),
            pltpu.VMEM((1280, 2 * L), F32),
            pltpu.VMEM((2000, L), F32),
            pltpu.VMEM((7 * V, L), F32),
        ],
        compiler_params=pltpu.CompilerParams(vmem_limit_bytes=VMEM_LIMIT),
    )(neighbours, live_count, lower, own, upper, inbox, w_subm, w_down)


def run_mask(features, occupancy, live_count):
    return pl.pallas_call(
        mask_kernel,
        out_shape=jax.ShapeDtypeStruct((2, V, L), BF16),
        in_specs=[smem(), smem()] + vmem(1),
        out_specs=vmem(1)[0],
        compiler_params=pltpu.CompilerParams(vmem_limit_bytes=VMEM_LIMIT),
    )(live_count, occupancy, features)


def finish_kernel(part_own, from_lower, from_upper, own, out):
    for g in range(2):
        total = part_own[g] + from_lower[g].astype(F32) + from_upper[g].astype(F32)
        total = total * jnp.broadcast_to(own[g, :, C : C + 1].astype(F32), (V, L))
        out[g] = jnp.transpose(total)[:C, :].astype(BF16)


def run_finish(part_own, from_lower, from_upper, own):
    return pl.pallas_call(
        finish_kernel,
        out_shape=jax.ShapeDtypeStruct((2, C, V), BF16),
        in_specs=vmem(4),
        out_specs=vmem(1)[0],
        compiler_params=pltpu.CompilerParams(vmem_limit_bytes=VMEM_LIMIT),
    )(part_own, from_lower, from_upper, own)


def shifted(block, distance):
    devices = range(lax.axis_size("space"))
    route = [(i - distance, i) for i in devices if i - distance in devices]
    return lax.ppermute(block, "space", route)


def exchanged(boxes):
    return lax.all_to_all(boxes, "space", split_axis=0, concat_axis=0, tiled=True)


def per_device(features, occupancy, neighbours, live_count, w_subm, w_down, grad_coarse):
    own = run_mask(features, occupancy, live_count)
    counts = jnp.broadcast_to(live_count.astype(F32)[:, None, None], (64, 2, L))
    inbox = exchanged(
        jnp.concatenate([grad_coarse.reshape(64, 6, L).astype(F32), counts], axis=1)
    )
    lower, upper = shifted(own, 1), shifted(own, -1)
    outbox, part_own, part_lower, part_upper, sums = run_blocks(
        neighbours, live_count, lower, own, upper, inbox, w_subm, w_down
    )
    coarse_out = exchanged(outbox)[:, :6, :].reshape(64, 6 * L).astype(BF16)
    grad_features = run_finish(part_own, shifted(part_upper, 1), shifted(part_lower, -1), own)
    sums = jnp.transpose(lax.psum(sums, "space")[:, :, :C], (0, 2, 1))
    return coarse_out, grad_features, sums[:27], sums[27:]


def solution(mesh):
    blocks = P(("rep", "space"), None)
    return jax.shard_map(
        per_device,
        mesh=mesh,
        in_specs=(
            P(("rep", "space"), None, None), blocks, blocks, P(("rep", "space")), P(), P(), blocks,
        ),
        out_specs=(
            blocks, P(("rep", "space"), None, None), P("rep", None, None), P("rep", None, None),
        ),
        check_vma=False,
    )
```

time: 998 us -> 252 us (0.25); the launches traced: 982 us -> 251 us
  local copies, waits for them, and re-layouts: 392 us -> 8.09 us
  other arithmetic: 211 us -> 0.02 us
  starting transfers between devices: 108 us -> 23 us
  matrix products: 44.9 us -> 0 us
  waiting for transfers between devices: 188 us -> 165 us
  Pallas kernels: 0 us -> 17.6 us
    scatter-add x211 -> x0, local copies, waits for them, and re-layouts: 283 us -> none
    scatter-add x113 -> x0, other arithmetic: 173 us -> none
    all_to_all x2 -> x1, starting transfers between devices: 90.8 us -> 13.2 us  [exchanged(): lax.all_to_all(boxes, 'space', split_axis=0, concat_axis=0, tiled=True)]
    dot_general x105 -> x0, matrix products: 44.9 us -> none  [the longest x27 24.2 us: gradient_source(): jnp.einsum('cd,bdv->bcv', w_subm[index], dpre, preferred_element_type=jnp...]
    transpose x27 -> x1, local copies, waits for them, and re-layouts: 38.3 us -> 1.57 us  [per_device(): sums = jnp.transpose(lax.psum(sums, 'space')[:, :, :C], (0, 2, 1))]
    all_to_all x0 -> x1, blocking collectives: none -> 22.7 us  [exchanged(): lax.all_to_all(boxes, 'space', split_axis=0, concat_axis=0, tiled=True)]
    psum x1, waiting for transfers between devices: 179 us -> 159 us  [per_device(): sums = jnp.transpose(lax.psum(sums, 'space')[:, :, :C], (0, 2, 1))]
    gather x33 -> x0, local copies, waits for them, and re-layouts: 18.8 us -> none  [the longest x27 15.3 us: build_pad(): piece = jnp.take(piece, table[:, index], axis=0)]
  transfers between devices with their start and end apart: 7 -> 6, of which waited for: 2 -> 3; matrix products, arithmetic and copies ran while one was open for 4% -> 0% of each run, Pallas kernels for 0% -> 1%
where the time goes in v1:
time: 252 us; the launch traced here: 251 us
  waiting for transfers between devices  165 us (65%)
  starting transfers between devices  23 us (9%)
  blocking collectives  22.7 us (9%)
  Pallas kernels  17.6 us (7%)
  between operations  14.9 us (6%)
  local copies, waits for them, and re-layouts  8.09 us (3%)
    psum x1, waiting for transfers between devices, per_device(): sums = jnp.transpose(lax.psum(sums, 'space')[:, :, :C], (0, 2, 1))  159 us
    all_to_all x1, blocking collectives, exchanged(): lax.all_to_all(boxes, 'space', split_axis=0, concat_axis=0, tiled=True)  22.7 us
    pallas_call x1, Pallas kernels, run_blocks(): pl.pallas_call(block_kernel, out_shape=(jax.ShapeDtypeStruct((64, 8, L),...  16 us
    all_to_all x1, starting transfers between devices, exchanged(): lax.all_to_all(boxes, 'space', split_axis=0, concat_axis=0, tiled=True)  13.2 us
    ppermute x4, starting transfers between devices, shifted(): return lax.ppermute(block, 'space', route)  9.8 us
    ppermute x4, waiting for transfers between devices, shifted(): return lax.ppermute(block, 'space', route)  5.77 us
  transfers between devices with their start and end apart: 6, of which 3 were waited for; matrix products, arithmetic and copies ran while one was open for 0% of the time, Pallas kernels for 1%

profile of v1, /device:TPU:1, one launch (start us, length us, event | category | flops | bytes accessed | tf_op | source)
XLA Modules:
  0.0 251.0 jit_solution(16485281213356162008)
XLA Ops:
  7.2 0.0 copy-start.4
  7.2 0.0 copy-start
  7.2 0.0 copy-start.1
  7.9 1.0 reshape.14
  8.9 0.7 concatenate.3
  9.7 13.2 %all-to-all-start = ((f32[64,8,128]{2,1,0:T(8,128)}), f32[64,8,128]{2,1,0:T(8,128)S(1)}, u32[]{:S(2)}, u32[]{:S(2)}) async-start(f32[64,8,128]{2,1,0:T(8,128)} %concatenate.3), calls=%async_computation | async-start | bytes 524288 | tf_op jit(solution)/shard_map/all_to_all | solution.py:317
  22.8 0.0 all-reduce.3.cloned.1.call-start
  22.9 0.0 copy-start.2
  22.9 0.9 copy-done.2
  23.8 0.7 copy-done.3
  24.5 0.7 shard_map.102.own
  25.2 3.5 %collective-permute-start = (bf16[2,512,128]{2,1,0:T(8,128)(2,1)S(1)}, bf16[2,512,128]{2,1,0:T(8,128)(2,1)S(1)}, u32[]{:S(2)}, u32[]{:S(2)}) collective-permute-start(bf16[2,512,128]{2,1,0:T(8,128)(2,1)S(1)} %shard_map.102.own), channel_id=1, source_target_pairs={{0,4},{4,8},{8,12},{12,16},{16,20},{20,24},{24,28},{28,32},{32,36}... | collective-permute-start | bytes 786440 | tf_op jit(solution)/shard_map/ppermute | solution.py:313
  28.7 1.9 collective-permute-start.1
  30.7 2.1 collective-permute-done.lower
  32.7 3.7 %collective-permute-done.1.upper = bf16[2,512,128]{2,1,0:T(8,128)(2,1)S(1)} collective-permute-done((bf16[2,512,128]{2,1,0:T(8,128)(2,1)S(1)}, bf16[2,512,128]{2,1,0:T(8,128)(2,1)S(1)}, u32[]{:S(2)}, u32[]{:S(2)}) %collective-permute-start.1) | collective-permute-done | bytes 262176 | tf_op jit(solution)/shard_map/ppermute | solution.py:313
  36.4 0.0 all-to-all-done.inbox
  36.4 0.0 copy-done.4
  36.4 0.0 copy-done
  36.5 16.0 %shard_map.103 = (f32[64,8,128]{2,1,0:T(8,128)S(1)}, f32[2,512,128]{2,1,0:T(8,128)S(1)}, bf16[2,512,128]{2,1,0:T(8,128)(2,1)S(1)}, bf16[2,512,128]{2,1,0:T(8,128)(2,1)S(1)}, f32[35,96,128]{2,1,0:T(8,128)}) custom-call(s32[2,27]{1,0:T(2,128)S(1)} %copy-done.4, s32[1]{0:T(128)S(6)} %copy.19.live_ref, bf16[2,512,128]{2,1,0:T(8,128)(2,1)S(1)} %collective-permute-done.lower, ...), custom_call_target="tpu_custom_call" | custom-call | tf_op jit(solution)/shard_map/pallas_call | solution.py:252
  52.4 0.0 all-reduce.3.cloned.1.call-update
  52.4 1.9 collective-permute-start.2
  54.4 2.4 collective-permute-start.3
  56.8 22.7 %all_to_all.10 = bf16[64,8,128]{2,1,0:T(8,128)(2,1)S(1)} all-to-all(bf16[64,8,128]{2,1,0:T(8,128)(2,1)S(1)} %convert.6), channel_id=1, replica_groups=mesh['space'=64,'rep'=4] {'space'}, dimensions={0} | all-to-all | bytes 262144 | tf_op jit(solution)/shard_map/all_to_all | solution.py:317
  79.5 0.7 copy.17
  80.2 0.0 collective-permute-done.2.from_lower
  80.2 0.0 collective-permute-done.3.from_upper
  80.2 0.9 shard_map.104
  81.1 159.0 %all-reduce.3.cloned.1.call-done = f32[35,96,128]{2,1,0:T(8,128)} async-done(((f32[35,96,128]{2,1,0:T(8,128)}), f32[35,96,128]{2,1,0:T(8,128)}) %all-reduce.3.cloned.1.call-update) | async-done | bytes 1720336 | tf_op jit(solution)/shard_map/psum | solution.py:332
  240.1 1.6 slice_bitcast_fusion
  241.7 0.1 slice.19
  241.8 1.5 copy.13
  243.3 0.9 copy.14
  (4 shorter events, 0.0 us)
Async XLA Ops:
  7.2 29.3 %copy-start.4 = (s32[2,27]{1,0:T(2,128)S(1)}, s32[2,27]{1,0:T(2,128)}, u32[]{:S(2)}) copy-start(s32[2,27]{1,0:T(2,128)} %table.1) | copy-start | bytes 652
  7.2 29.3 %copy-start = (bf16[27,96,96]{2,1,0:T(8,128)(2,1)S(1)}, bf16[27,96,96]{2,1,0:T(8,128)(2,1)}, u32[]{:S(2)}) copy-start(bf16[27,96,96]{2,1,0:T(8,128)(2,1)} %w_subm.1) | copy-start | bytes 1492996
  7.2 29.3 %copy-start.1 = (bf16[8,96,96]{2,1,0:T(8,128)(2,1)S(1)}, bf16[8,96,96]{2,1,0:T(8,128)(2,1)}, u32[]{:S(2)}) copy-start(bf16[8,96,96]{2,1,0:T(8,128)(2,1)} %w_down.1) | copy-start | bytes 442372
  9.7 26.8 %all-to-all-start = ((f32[64,8,128]{2,1,0:T(8,128)}), f32[64,8,128]{2,1,0:T(8,128)S(1)}, u32[]{:S(2)}, u32[]{:S(2)}) async-start(f32[64,8,128]{2,1,0:T(8,128)} %concatenate.3), calls=%async_computation | async-start | bytes 524288 | tf_op jit(solution)/shard_map/all_to_all | solution.py:317
  22.8 217.3 %all-reduce.3.cloned.1.call-start = ((), (), s32[]{:S(2)}) async-start(), calls=%async_computation.2 | async-start | bytes 3440640 | tf_op jit(solution)/shard_map/psum | solution.py:332
  22.9 0.9 copy-start.2
  23.8 0.7 copy-start.3
  25.2 7.5 %collective-permute-start = (bf16[2,512,128]{2,1,0:T(8,128)(2,1)S(1)}, bf16[2,512,128]{2,1,0:T(8,128)(2,1)S(1)}, u32[]{:S(2)}, u32[]{:S(2)}) collective-permute-start(bf16[2,512,128]{2,1,0:T(8,128)(2,1)S(1)} %shard_map.102.own), channel_id=1, source_target_pairs={{0,4},{4,8},{8,12},{12,16},{16,20},{20,24},{24,28},{28,32},{32,36}... | collective-permute-start | bytes 786440 | tf_op jit(solution)/shard_map/ppermute | solution.py:313
  28.7 7.7 %collective-permute-start.1 = (bf16[2,512,128]{2,1,0:T(8,128)(2,1)S(1)}, bf16[2,512,128]{2,1,0:T(8,128)(2,1)S(1)}, u32[]{:S(2)}, u32[]{:S(2)}) collective-permute-start(bf16[2,512,128]{2,1,0:T(8,128)(2,1)S(1)} %shard_map.102.own), channel_id=1, source_target_pairs={{4,0},{8,4},{12,8},{16,12},{20,16},{24,20},{28,24},{32,28},{36,32}... | collective-permute-start | bytes 786440 | tf_op jit(solution)/shard_map/ppermute | solution.py:313
  52.4 27.8 %collective-permute-start.2 = (bf16[2,512,128]{2,1,0:T(8,128)(2,1)S(1)}, bf16[2,512,128]{2,1,0:T(8,128)(2,1)S(1)}, u32[]{:S(2)}, u32[]{:S(2)}) collective-permute-start(bf16[2,512,128]{2,1,0:T(8,128)(2,1)S(1)} %get-tuple-element.11), channel_id=1, source_target_pairs={{0,4},{4,8},{8,12},{12,16},{16,20},{20,24},{24,28},{28,32},{32,36}... | collective-permute-start | bytes 786440 | tf_op jit(solution)/shard_map/ppermute | solution.py:313
  54.4 25.8 %collective-permute-start.3 = (bf16[2,512,128]{2,1,0:T(8,128)(2,1)S(1)}, bf16[2,512,128]{2,1,0:T(8,128)(2,1)S(1)}, u32[]{:S(2)}, u32[]{:S(2)}) collective-permute-start(bf16[2,512,128]{2,1,0:T(8,128)(2,1)S(1)} %get-tuple-element.12), channel_id=1, source_target_pairs={{4,0},{8,4},{12,8},{16,12},{20,16},{24,20},{28,24},{32,28},{36,32}... | collective-permute-start | bytes 786440 | tf_op jit(solution)/shard_map/ppermute | solution.py:313
Sparse Core Ops, SparseCore 0:
  52.6 187.4 all-reduce.2

commit v2 on v1

--- a/solution.py
+++ b/solution.py
@@ -9,6 +9,7 @@
 
 C, L, V = 96, 128, 512
 OFFSETS = [(a, b, c) for a in (-1, 0, 1) for b in (-1, 0, 1) for c in (-1, 0, 1)]
+PEERS, SHARDS, CHIPS, SHARD = 64, 27, 32, 48
 VMEM_LIMIT = 50 * 2**20
 F32, BF16 = jnp.float32, jnp.bfloat16
 NT = (((1,), (1,)), ((), ()))
@@ -49,9 +50,109 @@
     return jnp.transpose(jnp.concatenate([values, marks], axis=0)).astype(BF16)
 
 
-def mask_kernel(live_ref, occupancy_ref, features_ref, out_ref):
+def remote(source, target, sent, arrived, peer):
+    return pltpu.make_async_remote_copy(
+        src_ref=source, dst_ref=target, send_sem=sent, recv_sem=arrived,
+        device_id={"space": peer}, device_id_type=pl.DeviceIdType.MESH,
+    )
+
+
+def greet_all(me):
+    barrier = pltpu.get_barrier_semaphore()
+
+    def tell(i, carry):
+        pl.semaphore_signal(
+            barrier, inc=1, device_id={"space": lax.rem(me + i, PEERS)},
+            device_id_type=pl.DeviceIdType.MESH,
+        )
+        return carry
+
+    lax.fori_loop(1, PEERS, tell, 0)
+
+
+def greeted():
+    pl.semaphore_wait(pltpu.get_barrier_semaphore(), PEERS - 1)
+
+
+def swap(me, outbox, inbox, sent, arrived):
+    def box(i):
+        peer = lax.rem(me + i, PEERS)
+        return pl.ds(pl.multiple_of(peer * 8, 8), 8), peer
+
+    def start(i, carry):
+        at, peer = box(i)
+        mine = pl.ds(pl.multiple_of(me * 8, 8), 8)
+        remote(outbox.at[at], inbox.at[mine], sent.at[peer], arrived.at[me], peer).start()
+        return carry
+
+    def finish(i, carry):
+        at, peer = box(i)
+        remote(outbox.at[at], inbox.at[at], sent.at[peer], arrived.at[peer], peer).wait()
+        return carry
+
+    return (
+        lambda: lax.fori_loop(1, PEERS, start, 0),
+        lambda: lax.fori_loop(1, PEERS, finish, 0),
+    )
+
+
+def spread_kernel(
+    live_ref, occupancy_ref, features_ref, cotangent_ref,
+    own, lower, upper, inbox,
+    outbox, box_sent, box_arrived, halo_sent, halo_arrived,
+):
+    me = lax.axis_index("space")
+    greet_all(me)
+    for n in range(6):
+        outbox[pl.ds(n, PEERS, stride=8), :] = cotangent_ref[:, n * L : (n + 1) * L].astype(F32)
+    live = jnp.broadcast_to(live_ref[0].astype(F32), (PEERS, L))
+    for n in (6, 7):
+        outbox[pl.ds(n, PEERS, stride=8), :] = live
     for g in range(2):
-        out_ref[g] = masked_rows(features_ref, occupancy_ref, live_ref[0], g)
+        own[g] = masked_rows(features_ref, occupancy_ref, live_ref[0], g)
+    greeted()
+    up = remote(own, lower, halo_sent.at[0], halo_arrived.at[0], lax.min(me + 1, PEERS - 1))
+    down = remote(own, upper, halo_sent.at[1], halo_arrived.at[1], lax.max(me - 1, 0))
+    has_up, has_down = me < PEERS - 1, me > 0
+    start, finish = swap(me, outbox, inbox, box_sent, box_arrived)
+
+    @pl.when(has_up)
+    def _():
+        up.start()
+
+    @pl.when(has_down)
+    def _():
+        down.start()
+
+    start()
+    mine = pl.ds(pl.multiple_of(me * 8, 8), 8)
+    inbox[mine, :] = outbox[mine, :]
+
+    @pl.when(has_down)
+    def _():
+        up.wait_recv()
+
+    @pl.when(jnp.logical_not(has_down))
+    def _():
+        lower[...] = jnp.zeros_like(lower)
+
+    @pl.when(has_up)
+    def _():
+        down.wait_recv()
+
+    @pl.when(jnp.logical_not(has_up))
+    def _():
+        upper[...] = jnp.zeros_like(upper)
+
+    finish()
+
+    @pl.when(has_up)
+    def _():
+        up.wait_send()
+
+    @pl.when(has_down)
+    def _():
+        down.wait_send()
 
 
 def block_kernel(
@@ -196,8 +297,20 @@
             dpre3[g * 640 + a * 64 : g * 640 + a * 64 + V, a * L : (a + 1) * L] = dpre16
         hid[...] = dpre16
         pre[g * V : (g + 1) * V, :] = dpre
-    for j in range(8):
-        sums[27 + j] = down[:C, j * L : (j + 1) * L].astype(sums.dtype)
+    lane = lax.broadcasted_iota(jnp.int32, (C, L), 1)
+    held = {}
+
+    def keep(k, product):
+        held[k % 4] = jnp.transpose(product)[:C]
+        if k % 4 == 3 or k == 34:
+            last = held.get(3)
+            for n in range(3):
+                slab = held[n]
+                if last is not None:
+                    slab = jnp.where(lane < C, slab, pltpu.roll(last, C - 32 * n, 1))
+                at = (3 * (k // 4) + n) * C
+                sums[at : at + C, :] = slab.astype(BF16)
+            held.clear()
 
     dt = jnp.transpose(pre[...]).astype(BF16)
     for a in range(3):
@@ -209,7 +322,9 @@
                 dt[:, V:], cols[640 + a * 64 : 640 + a * 64 + V, lanes], preferred_element_type=F32
             )
             for n in range(min(2, 9 - bc)):
-                sums[a * 9 + bc + n] = total[:C, n * L : (n + 1) * L].astype(sums.dtype)
+                keep(a * 9 + bc + n, total[:, n * L : (n + 1) * L])
+    for j in range(8):
+        keep(27 + j, down[:, j * L : (j + 1) * L])
 
     gpad[...] = jnp.zeros_like(gpad)
     for bc in range(0, 9, 2):
@@ -248,7 +363,7 @@
     return [pl.BlockSpec(memory_space=pltpu.VMEM)] * n
 
 
-def run_blocks(neighbours, live_count, lower, own, upper, inbox, w_subm, w_down, kind=F32):
+def run_blocks(neighbours, live_count, lower, own, upper, inbox, w_subm, w_down):
     return pl.pallas_call(
         block_kernel,
         out_shape=(
@@ -256,7 +371,7 @@
             jax.ShapeDtypeStruct((2, V, L), F32),
             jax.ShapeDtypeStruct((2, V, L), BF16),
             jax.ShapeDtypeStruct((2, V, L), BF16),
-            jax.ShapeDtypeStruct((35, C, L), kind),
+            jax.ShapeDtypeStruct((27 * C, L), BF16),
         ),
         in_specs=[smem(), smem()] + vmem(6),
         out_specs=tuple(vmem(5)),
@@ -280,57 +395,261 @@
     )(neighbours, live_count, lower, own, upper, inbox, w_subm, w_down)
 
 
-def run_mask(features, occupancy, live_count):
+def run_spread(features, occupancy, live_count, grad_coarse):
+    halo = jax.ShapeDtypeStruct((2, V, L), BF16)
     return pl.pallas_call(
-        mask_kernel,
-        out_shape=jax.ShapeDtypeStruct((2, V, L), BF16),
-        in_specs=[smem(), smem()] + vmem(1),
-        out_specs=vmem(1)[0],
-        compiler_params=pltpu.CompilerParams(vmem_limit_bytes=VMEM_LIMIT),
-    )(live_count, occupancy, features)
-
-
-def finish_kernel(part_own, from_lower, from_upper, own, out):
+        spread_kernel,
+        out_shape=(halo, halo, halo, jax.ShapeDtypeStruct((8 * PEERS, L), F32)),
+        in_specs=[smem(), smem()] + vmem(2),
+        out_specs=tuple(vmem(4)),
+        scratch_shapes=[
+            pltpu.VMEM((8 * PEERS, L), F32),
+            pltpu.SemaphoreType.DMA((PEERS,)),
+            pltpu.SemaphoreType.DMA((PEERS,)),
+            pltpu.SemaphoreType.DMA((2,)),
+            pltpu.SemaphoreType.DMA((2,)),
+        ],
+        compiler_params=pltpu.CompilerParams(
+            vmem_limit_bytes=VMEM_LIMIT, collective_id=0, has_side_effects=True
+        ),
+    )(live_count, occupancy, features, grad_coarse)
+
+
+def gather_kernel(
+    outbox, part_own, part_lower, part_upper, own, sums,
+    coarse_out, grad_features, grad_subm, grad_down,
+    inbox, from_lower, from_upper, other, chip, shares, total,
+    box_sent, box_arrived, halo_sent, halo_arrived, pair_sent, pair_arrived,
+    share_sent, share_arrived, total_sent, total_arrived, copy_sent, copy_arrived,
+):
+    me = lax.axis_index("space")
+    here, core = me // 2, lax.rem(me, 2)
+    partner = me + 1 - 2 * core
+    half = SHARDS * SHARD
+
+    def rows_of(shard):
+        return pl.ds(pl.multiple_of(shard * SHARD, SHARD), SHARD)
+
+    def chip_of(shard):
+        return shard + shard // 6
+
+    mine = here - here // 7
+    owns = (lax.rem(here, 7) != 6) & (here < CHIPS - 1)
+
+    greet_all(me)
+    greeted()
+
+    def half_of(which):
+        return pl.ds(pl.multiple_of(which * half, half), half)
+
+    pair = remote(sums.at[half_of(1 - core)], other, pair_sent, pair_arrived, partner)
+    pair.start()
+    up = remote(part_upper, from_lower, halo_sent.at[0], halo_arrived.at[0], lax.min(me + 1, PEERS - 1))
+    down = remote(part_lower, from_upper, halo_sent.at[1], halo_arrived.at[1], lax.max(me - 1, 0))
+    has_up, has_down = me < PEERS - 1, me > 0
+    start, finish = swap(me, outbox, inbox, box_sent, box_arrived)
+
+    @pl.when(has_up)
+    def _():
+        up.start()
+
+    @pl.when(has_down)
+    def _():
+        down.start()
+
+    pair.wait_recv()
+    chip[...] = (sums[half_of(core), :].astype(F32) + other[...].astype(F32)).astype(BF16)
+
+    def share(shard):
+        peer = chip_of(shard) * 2 + core
+        return peer, remote(
+            chip.at[rows_of(shard)], shares.at[rows_of(here)],
+            share_sent.at[shard], share_arrived.at[here], peer,
+        )
+
+    def share_start(i, carry):
+        shard = lax.rem(mine + i, SHARDS)
+        peer, copy = share(shard)
+
+        @pl.when(peer != me)
+        def _():
+            copy.start()
+
+        return carry
+
+    lax.fori_loop(0, SHARDS, share_start, 0)
+    start()
+    box = pl.ds(pl.multiple_of(me * 8, 8), 8)
+    inbox[box, :] = outbox[box, :]
+
+    @pl.when(has_down)
+    def _():
+        up.wait_recv()
+
+    @pl.when(jnp.logical_not(has_down))
+    def _():
+        from_lower[...] = jnp.zeros_like(from_lower)
+
+    @pl.when(has_up)
+    def _():
+        down.wait_recv()
+
+    @pl.when(jnp.logical_not(has_up))
+    def _():
+        from_upper[...] = jnp.zeros_like(from_upper)
+
     for g in range(2):
-        total = part_own[g] + from_lower[g].astype(F32) + from_upper[g].astype(F32)
-        total = total * jnp.broadcast_to(own[g, :, C : C + 1].astype(F32), (V, L))
-        out[g] = jnp.transpose(total)[:C, :].astype(BF16)
-
-
-def run_finish(part_own, from_lower, from_upper, own):
+        value = part_own[g] + from_lower[g].astype(F32) + from_upper[g].astype(F32)
+        value = value * jnp.broadcast_to(own[g, :, C : C + 1].astype(F32), (V, L))
+        grad_features[g] = jnp.transpose(value)[:C, :].astype(BF16)
+
+    def handed(shard, peer):
+        at = pl.ds(pl.multiple_of(core * half + shard * SHARD, SHARD), SHARD)
+        return remote(total.at[at], total.at[at], total_sent.at[peer // 2], total_arrived.at[shard], peer)
+
+    def copied(shard, which):
+        at = pl.ds(pl.multiple_of(which * half + shard * SHARD, SHARD), SHARD)
+        return remote(total.at[at], total.at[at], copy_sent.at[shard], copy_arrived.at[shard], partner)
+
+    @pl.when(owns)
+    def _():
+        shares[rows_of(here), :] = chip[rows_of(mine), :]
+
+        def arrived(i, carry):
+            there = lax.rem(here + i, CHIPS)
+            remote(
+                chip.at[rows_of(0)], shares.at[rows_of(there)],
+                share_sent.at[0], share_arrived.at[there], there * 2 + core,
+            ).wait_recv()
+            return carry
+
+        lax.fori_loop(1, CHIPS, arrived, 0)
+
+        def plus(i, value):
+            return value + shares[rows_of(i), :].astype(F32)
+
+        value = lax.fori_loop(0, CHIPS, plus, jnp.zeros((SHARD, L), F32))
+        at = pl.ds(pl.multiple_of(core * half + mine * SHARD, SHARD), SHARD)
+        total[at, :] = value.astype(BF16)
+
+        def hand(i, carry):
+            handed(mine, lax.rem(here + i, CHIPS) * 2 + core).start()
+            return carry
+
+        lax.fori_loop(1, CHIPS, hand, 0)
+        copied(mine, core).start()
+
+    def pass_on(i, carry):
+        shard = lax.rem(mine + i, SHARDS)
+
+        @pl.when(chip_of(shard) != here)
+        def _():
+            handed(shard, chip_of(shard) * 2 + core).wait_recv()
+            copied(shard, core).start()
+
+        return carry
+
+    lax.fori_loop(0, SHARDS, pass_on, 0)
+
+    finish()
+    for n in range(6):
+        coarse_out[:, n * L : (n + 1) * L] = inbox[pl.ds(n, PEERS, stride=8), :].astype(BF16)
+
+    def copied_in(i, carry):
+        copied(i, 1 - core).wait_recv()
+        return carry
+
+    lax.fori_loop(0, SHARDS, copied_in, 0)
+
+    for k in range(35):
+        quad, n = divmod(k, 4)
+        if n < 3:
+            at = (3 * quad + n) * C
+            value = total[at : at + C, :].astype(F32)[:, :C]
+        else:
+            lane = lax.broadcasted_iota(jnp.int32, (C, L), 1)
+            value = jnp.zeros((C, L), F32)
+            for m in range(3):
+                at = (3 * quad + m) * C
+                piece = pltpu.roll(total[at : at + C, :].astype(F32), 32 + 32 * m, 1)
+                value = jnp.where(lane // 32 == m, piece, value)
+            value = value[:, :C]
+        if k < 27:
+            grad_subm[k] = value
+        else:
+            grad_down[k - 27] = value
+
+    pair.wait_send()
+
+    @pl.when(has_up)
+    def _():
+        up.wait_send()
+
+    @pl.when(has_down)
+    def _():
+        down.wait_send()
+
+    def share_done(i, carry):
+        peer, copy = share(i)
+
+        @pl.when(peer != me)
+        def _():
+            copy.wait_send()
+
+        return carry
+
+    lax.fori_loop(0, SHARDS, share_done, 0)
+
+    @pl.when(owns)
+    def _():
+        def done(i, carry):
+            handed(mine, lax.rem(here + i, CHIPS) * 2 + core).wait_send()
+            return carry
+
+        lax.fori_loop(1, CHIPS, done, 0)
+
+    def copied_out(i, carry):
+        copied(i, core).wait_send()
+        return carry
+
+    lax.fori_loop(0, SHARDS, copied_out, 0)
+
+
+def run_gather(outbox, part_own, part_lower, part_upper, own, sums):
+    dma = pltpu.SemaphoreType.DMA
     return pl.pallas_call(
-        finish_kernel,
-        out_shape=jax.ShapeDtypeStruct((2, C, V), BF16),
-        in_specs=vmem(4),
-        out_specs=vmem(1)[0],
-        compiler_params=pltpu.CompilerParams(vmem_limit_bytes=VMEM_LIMIT),
-    )(part_own, from_lower, from_upper, own)
-
-
-def shifted(block, distance):
-    devices = range(lax.axis_size("space"))
-    route = [(i - distance, i) for i in devices if i - distance in devices]
-    return lax.ppermute(block, "space", route)
-
-
-def exchanged(boxes):
-    return lax.all_to_all(boxes, "space", split_axis=0, concat_axis=0, tiled=True)
+        gather_kernel,
+        out_shape=(
+            jax.ShapeDtypeStruct((PEERS, 6 * L), BF16),
+            jax.ShapeDtypeStruct((2, C, V), BF16),
+            jax.ShapeDtypeStruct((27, C, C), F32),
+            jax.ShapeDtypeStruct((8, C, C), F32),
+        ),
+        in_specs=vmem(6),
+        out_specs=tuple(vmem(4)),
+        scratch_shapes=[
+            pltpu.VMEM((8 * PEERS, L), F32),
+            pltpu.VMEM((2, V, L), BF16),
+            pltpu.VMEM((2, V, L), BF16),
+            pltpu.VMEM((SHARDS * SHARD, L), BF16),
+            pltpu.VMEM((SHARDS * SHARD, L), BF16),
+            pltpu.VMEM((CHIPS * SHARD, L), BF16),
+            pltpu.VMEM((2 * SHARDS * SHARD, L), BF16),
+            dma((PEERS,)), dma((PEERS,)), dma((2,)), dma((2,)), dma(()), dma(()),
+            dma((SHARDS,)), dma((CHIPS,)), dma((CHIPS,)), dma((SHARDS,)), dma((SHARDS,)), dma((SHARDS,)),
+        ],
+        compiler_params=pltpu.CompilerParams(
+            vmem_limit_bytes=VMEM_LIMIT, collective_id=1, has_side_effects=True
+        ),
+    )(outbox, part_own, part_lower, part_upper, own, sums)
 
 
 def per_device(features, occupancy, neighbours, live_count, w_subm, w_down, grad_coarse):
-    own = run_mask(features, occupancy, live_count)
-    counts = jnp.broadcast_to(live_count.astype(F32)[:, None, None], (64, 2, L))
-    inbox = exchanged(
-        jnp.concatenate([grad_coarse.reshape(64, 6, L).astype(F32), counts], axis=1)
+    own, lower, upper, inbox = run_spread(features, occupancy, live_count, grad_coarse)
+    outbox, part_own, part_lower, part_upper, sums = run_blocks(
+        neighbours, live_count, lower, own, upper, inbox.reshape(PEERS, 8, L), w_subm, w_down
     )
-    lower, upper = shifted(own, 1), shifted(own, -1)
-    outbox, part_own, part_lower, part_upper, sums = run_blocks(
-        neighbours, live_count, lower, own, upper, inbox, w_subm, w_down
-    )
-    coarse_out = exchanged(outbox)[:, :6, :].reshape(64, 6 * L).astype(BF16)
-    grad_features = run_finish(part_own, shifted(part_upper, 1), shifted(part_lower, -1), own)
-    sums = jnp.transpose(lax.psum(sums, "space")[:, :, :C], (0, 2, 1))
-    return coarse_out, grad_features, sums[:27], sums[27:]
+    return run_gather(outbox.reshape(8 * PEERS, L), part_own, part_lower, part_upper, own, sums)
 
 
 def solution(mesh):

time: 252 us -> 92.5 us (0.37)
  waiting for transfers between devices: 165 us -> 0 us
  Pallas kernels: 17.6 us -> 81.1 us
  starting transfers between devices: 23 us -> 0 us
  blocking collectives: 22.7 us -> 0 us
  between operations: 14.9 us -> 1.32 us
    psum x1 -> x0, waiting for transfers between devices: 159 us -> none  [per_device(): sums = jnp.transpose(lax.psum(sums, 'space')[:, :, :C], (0, 2, 1))]
    pallas_call x2, Pallas kernels: 1.6 us -> 66.1 us  [the longest x1 41.4 us: run_gather(): pl.pallas_call(gather_kernel, out_shape=(jax.ShapeDtypeStruct((PEERS, 6 *...]
    all_to_all x1 -> x0, blocking collectives: 22.7 us -> none  [exchanged(): lax.all_to_all(boxes, 'space', split_axis=0, concat_axis=0, tiled=True)]
    all_to_all x1 -> x0, starting transfers between devices: 13.2 us -> none  [exchanged(): lax.all_to_all(boxes, 'space', split_axis=0, concat_axis=0, tiled=True)]
    ppermute x4 -> x0, starting transfers between devices: 9.8 us -> none  [shifted(): return lax.ppermute(block, 'space', route)]
    ppermute x4 -> x0, waiting for transfers between devices: 5.77 us -> none  [shifted(): return lax.ppermute(block, 'space', route)]
    unnamed x13 -> x16, local copies, waits for them, and re-layouts: 4.66 us -> 9.71 us
  transfers between devices with their start and end apart: 6 -> 0, of which waited for: 3 -> 0; matrix products, arithmetic and copies ran while one was open for 0% -> 0% of each run, Pallas kernels for 1% -> 0%
where the time goes in v2:
time: 92.5 us; the launch traced here: 92.2 us
  Pallas kernels  81.1 us (88%)
  local copies, waits for them, and re-layouts  9.71 us (10%)
  between operations  1.32 us (1%)
    pallas_call x1, Pallas kernels, run_gather(): pl.pallas_call(gather_kernel, out_shape=(jax.ShapeDtypeStruct((PEERS, 6 *...  41.4 us
    pallas_call x1, Pallas kernels, run_spread(): pl.pallas_call(spread_kernel, out_shape=(halo, halo, halo, jax.ShapeDtype...  24.8 us
    pallas_call x1, Pallas kernels, run_blocks(): pl.pallas_call(block_kernel, out_shape=(jax.ShapeDtypeStruct((64, 8, L),...  15 us
    unnamed x16, local copies, waits for them, and re-layouts  9.71 us

profile of v2, /device:TPU:1, one launch (start us, length us, event | category | flops | bytes accessed | tf_op | source)
XLA Modules:
  0.0 92.2 jit_solution(9335990226364107207)
XLA Ops:
  1.3 0.0 copy-start.2
  1.3 0.9 copy-done.2
  2.2 0.0 copy-start.3
  2.2 0.9 copy-done.3
  3.1 0.0 copy-start.4
  3.1 0.7 copy-done.4
  3.8 24.8 %shard_map.102 = (bf16[2,512,128]{2,1,0:T(8,128)(2,1)S(1)}, bf16[2,512,128]{2,1,0:T(8,128)(2,1)S(1)}, bf16[2,512,128]{2,1,0:T(8,128)(2,1)S(1)}, f32[512,128]{1,0:T(8,128)S(1)}) custom-call(s32[1]{0:T(128)S(6)} %copy.15.live_ref, s32[2,16]{1,0:T(2,128)S(1)} %copy-done.4, bf16[2,96,512]{2,1,0:T(8,128)(2,1)S(1)} %copy-done.2, bf16[64,768]{1,0:T(8,128)(2,1)S(1)} %copy-done.3), custom_call_target="tpu_custom_call" | custom-call | tf_op jit(solution)/shard_map/pallas_call | solution.py:400
  28.5 0.0 copy-start
  28.6 1.1 %copy-done = bf16[27,96,96]{2,1,0:T(8,128)(2,1)S(1)} copy-done((bf16[27,96,96]{2,1,0:T(8,128)(2,1)S(1)}, bf16[27,96,96]{2,1,0:T(8,128)(2,1)}, u32[]{:S(2)}) %copy-start) | copy-done | bytes 497688
  29.6 0.0 copy-start.1
  29.6 0.9 %copy-done.1 = bf16[8,96,96]{2,1,0:T(8,128)(2,1)S(1)} copy-done((bf16[8,96,96]{2,1,0:T(8,128)(2,1)S(1)}, bf16[8,96,96]{2,1,0:T(8,128)(2,1)}, u32[]{:S(2)}) %copy-start.1) | copy-done | bytes 147480
  30.6 0.0 copy-start.5
  30.6 0.7 copy-done.5
  31.2 15.0 %shard_map.103 = (f32[64,8,128]{2,1,0:T(8,128)S(1)}, f32[2,512,128]{2,1,0:T(8,128)S(1)}, bf16[2,512,128]{2,1,0:T(8,128)(2,1)S(1)}, bf16[2,512,128]{2,1,0:T(8,128)(2,1)S(1)}, bf16[2592,128]{1,0:T(8,128)(2,1)S(1)}) custom-call(s32[2,27]{1,0:T(2,128)S(1)} %copy-done.5, s32[1]{0:T(128)S(6)} %copy.15.live_ref, bf16[2,512,128]{2,1,0:T(8,128)(2,1)S(1)} %get-tuple-element.13.lower, ...), custom_call_target="tpu_custom_call" | custom-call | tf_op jit(solution)/shard_map/pallas_call | solution.py:367
  46.3 41.4 %shard_map.104 = (bf16[64,768]{1,0:T(8,128)(2,1)S(1)}, bf16[2,96,512]{2,1,0:T(8,128)(2,1)S(1)}, f32[27,96,96]{2,1,0:T(8,128)}, f32[8,96,96]{2,1,0:T(8,128)S(1)}) custom-call(f32[512,128]{1,0:T(8,128)S(1)} %bitcast.2, f32[2,512,128]{2,1,0:T(8,128)S(1)} %get-tuple-element.18.part_own, bf16[2,512,128]{2,1,0:T(8,128)(2,1)S(1)} %get-tuple-element.19.part_lower, ...), custom_call_target="tpu_custom_call" | custom-call | tf_op jit(solution)/shard_map/pallas_call | solution.py:620
  87.6 0.6 copy.16
  88.3 0.7 copy.17
  89.0 2.5 %copy.18 = f32[27,96,96]{2,1,0:T(8,128)} copy(f32[27,96,96]{2,1,0:T(8,128)} %get-tuple-element.28) | data formatting | bytes 1990656
  91.4 0.7 copy.19
Async XLA Ops:
  1.3 0.9 %copy-start.2 = (bf16[2,96,512]{2,1,0:T(8,128)(2,1)S(1)}, bf16[2,96,512]{2,1,0:T(8,128)(2,1)}, u32[]{:S(2)}) copy-start(bf16[2,96,512]{2,1,0:T(8,128)(2,1)} %features_ref.1) | copy-start | bytes 589828
  2.2 0.9 copy-start.3
  3.1 0.7 copy-start.4
  28.5 1.1 %copy-start = (bf16[27,96,96]{2,1,0:T(8,128)(2,1)S(1)}, bf16[27,96,96]{2,1,0:T(8,128)(2,1)}, u32[]{:S(2)}) copy-start(bf16[27,96,96]{2,1,0:T(8,128)(2,1)} %w_subm.1) | copy-start | bytes 1492996
  29.6 0.9 %copy-start.1 = (bf16[8,96,96]{2,1,0:T(8,128)(2,1)S(1)}, bf16[8,96,96]{2,1,0:T(8,128)(2,1)}, u32[]{:S(2)}) copy-start(bf16[8,96,96]{2,1,0:T(8,128)(2,1)} %w_down.1) | copy-start | bytes 442372
  30.6 0.7 copy-start.5

commit v3 on v1

v3 whole, which is shorter than its diff:
```python
import functools

import jax
import jax.numpy as jnp
from jax import lax
from jax.experimental import pallas as pl
from jax.experimental.pallas import tpu as pltpu
from jax.sharding import PartitionSpec as P

C, L, V = 96, 128, 512
OFFSETS = [(a, b, c) for a in (-1, 0, 1) for b in (-1, 0, 1) for c in (-1, 0, 1)]
PEERS = 64
HALF, YPART, ZPART = 1344, 336, 48
VMEM_LIMIT = 50 * 2**20
F32, BF16 = jnp.float32, jnp.bfloat16
NT = (((1,), (1,)), ((), ()))


def segments(a, b, c):
    span = {-1: [(7, 0)], 0: [(i, i + 1) for i in range(8)], 1: [(0, 9)]}
    xs, ys, zs = span[a], span[b], span[c]
    if c == 0:
        return [(x * 64 + y * 8, 1, tx * 100 + ty * 10 + 1, 1, 8) for x, tx in xs for y, ty in ys]
    z, tz = zs[0]
    if b == 0:
        return [(x * 64 + z, 8, tx * 100 + 10 + tz, 10, 8) for x, tx in xs]
    y, ty = ys[0]
    if a == 0:
        return [(y * 8 + z, 64, 100 + ty * 10 + tz, 100, 8)]
    x, tx = xs[0]
    return [(x * 64 + y * 8 + z, 1, tx * 100 + ty * 10 + tz, 1, 1)]


def rows(start, count, stride):
    return pl.ds(start, count) if stride == 1 else pl.ds(start, count, stride=stride)


def mask_row(words, live, g):
    lane = lax.broadcasted_iota(jnp.int32, (1, V), 1)
    word = jnp.zeros((1, V), jnp.int32)
    for w in range(16):
        word = jnp.where(lane // 32 == w, words[g, w], word)
    bit = jnp.bitwise_and(jnp.right_shift(word, jnp.bitwise_and(lane, 31)), 1)
    return jnp.where(g < live, bit, 0)


def masked_rows(features, words, live, g):
    bit = mask_row(words, live, g)
    values = jnp.where(bit > 0, features[g].astype(F32), 0.0)
    marks = jnp.broadcast_to(bit.astype(F32), (L - C, V))
    return jnp.transpose(jnp.concatenate([values, marks], axis=0)).astype(BF16)


def remote(source, target, sent, arrived, peer):
    return pltpu.make_async_remote_copy(
        src_ref=source, dst_ref=target, send_sem=sent, recv_sem=arrived,
        device_id={"space": peer}, device_id_type=pl.DeviceIdType.MESH,
    )


def greet_all(me):
    barrier = pltpu.get_barrier_semaphore()

    def tell(i, carry):
        pl.semaphore_signal(
            barrier, inc=1, device_id={"space": lax.rem(me + i, PEERS)},
            device_id_type=pl.DeviceIdType.MESH,
        )
        return carry

    lax.fori_loop(1, PEERS, tell, 0)


def greeted():
    pl.semaphore_wait(pltpu.get_barrier_semaphore(), PEERS - 1)


def swap(me, outbox, inbox, sent, arrived):
    def box(i):
        peer = lax.rem(me + i, PEERS)
        return pl.ds(pl.multiple_of(peer * 8, 8), 8), peer

    def start(i, carry):
        at, peer = box(i)
        mine = pl.ds(pl.multiple_of(me * 8, 8), 8)
        remote(outbox.at[at], inbox.at[mine], sent.at[peer], arrived.at[me], peer).start()
        return carry

    def finish(i, carry):
        at, peer = box(i)
        remote(outbox.at[at], inbox.at[at], sent.at[peer], arrived.at[peer], peer).wait()
        return carry

    return (
        lambda: lax.fori_loop(1, PEERS, start, 0),
        lambda: lax.fori_loop(1, PEERS, finish, 0),
    )


def section_kernel(
    table, live_ref, occupancy_ref, features_hbm, cotangent_hbm, w_subm_hbm, w_down_hbm,
    coarse_in, grad_features, total,
    features, cotangent, w_subm, w_down,
    own, lower, upper, outbox, inbox, coarse_box,
    source, pad, cols, wf, wb, wd, perm, spread, pre, dpre3, u, gpad, gsource,
    sums32, sums16, pair_in, chip32, chip16, y_in, y32, y16, z_in,
    part_lower, part_upper, from_lower, from_upper,
    load_sem, box_sent, box_arrived, back_sent, back_arrived, halo_sent, halo_arrived,
    rim_sent, rim_arrived, pair_sent, pair_arrived, ysent, yarrived, zsent, zarrived,
    gzsent, gzarrived, gysent, gyarrived, copy_sent, copy_arrived,
):
    me = lax.axis_index("space")
    y, z, core = me // 16, lax.rem(me // 2, 8), lax.rem(me, 2)
    partner = me + 1 - 2 * core
    has_up, has_down = me < PEERS - 1, me > 0
    loads = [
        pltpu.make_async_copy(hbm, ref, load_sem.at[n])
        for n, (hbm, ref) in enumerate(
            ((features_hbm, features), (cotangent_hbm, cotangent), (w_subm_hbm, w_subm), (w_down_hbm, w_down))
        )
    ]
    for load in loads:
        load.start()
    greet_all(me)

    i = lax.broadcasted_iota(jnp.int32, (V, V), 0)
    v = lax.broadcasted_iota(jnp.int32, (V, V), 1)
    j, t = i // 64, i % 64
    vx, vy, vz = 2 * (t // 16) + j // 4, 2 * (t // 4 % 4) + j // 2 % 2, 2 * (t % 4) + j % 2
    perm[...] = jnp.where(vx * 64 + vy * 8 + vz == v, 1.0, 0.0).astype(BF16)
    spread[...] = jnp.where(
        lax.broadcasted_iota(jnp.int32, (L, 6 * L), 1) // 8
        == lax.broadcasted_iota(jnp.int32, (L, 6 * L), 0),
        1.0, 0.0,
    ).astype(BF16)
    wf[...] = jnp.zeros_like(wf)
    wb[...] = jnp.zeros_like(wb)
    wd[...] = jnp.zeros_like(wd)
    dpre3[...] = jnp.zeros_like(dpre3)
    coarse_box[...] = jnp.zeros_like(coarse_box)
    source[6 * V :, :] = jnp.zeros((V, L), F32)

    loads[0].wait()
    for g in range(2):
        own[g] = masked_rows(features, occupancy_ref, live_ref[0], g)
    loads[1].wait()
    for n in range(6):
        outbox[pl.ds(n, PEERS, stride=8), :] = cotangent[:, n * L : (n + 1) * L].astype(F32)
    counts = jnp.broadcast_to(live_ref[0].astype(F32), (PEERS, L))
    for n in (6, 7):
        outbox[pl.ds(n, PEERS, stride=8), :] = counts

    greeted()
    up = remote(own, lower, halo_sent.at[0], halo_arrived.at[0], lax.min(me + 1, PEERS - 1))
    down = remote(own, upper, halo_sent.at[1], halo_arrived.at[1], lax.max(me - 1, 0))

    @pl.when(has_up)
    def _():
        up.start()

    @pl.when(has_down)
    def _():
        down.start()

    box_start, box_finish = swap(me, outbox, inbox, box_sent, box_arrived)
    box_start()
    mine = pl.ds(pl.multiple_of(me * 8, 8), 8)
    inbox[mine, :] = outbox[mine, :]

    loads[2].wait()
    loads[3].wait()
    for k in range(27):
        a, bc = divmod(k, 9)
        w = w_subm[k]
        wf[k * L : k * L + C, :C] = w
        wb[bc * L : bc * L + C, a * L : a * L + C] = w
    for j in range(8):
        wd[j * L : j * L + C, :C] = w_down[j]

    for g in range(2):
        source[(2 + g) * V : (3 + g) * V, :] = own[g].astype(F32)

    @pl.when(has_down)
    def _():
        up.wait_recv()

    @pl.when(jnp.logical_not(has_down))
    def _():
        lower[...] = jnp.zeros_like(lower)

    @pl.when(has_up)
    def _():
        down.wait_recv()

    @pl.when(jnp.logical_not(has_up))
    def _():
        upper[...] = jnp.zeros_like(upper)

    for g in range(2):
        source[g * V : (g + 1) * V, :] = lower[g].astype(F32)
        source[(4 + g) * V : (5 + g) * V, :] = upper[g].astype(F32)

    for g in range(2):
        for k, offset in enumerate(OFFSETS):
            base = (2 + g) * V if k == 13 else table[g, k] * V
            for s0, ss, p0, ps, count in segments(*offset):
                pad[rows(g * 1000 + p0, count, ps), :] = source[rows(base + s0, count, ss), :]

    def columns(gx, carry):
        for b in range(3):
            for c in range(3):
                piece = jnp.concatenate(
                    [pad[pl.ds(gx * 100 + (yy + b) * 10 + c, 8), :] for yy in range(8)], axis=0
                )
                bc = 3 * b + c
                cols[pl.ds(pl.multiple_of(gx * 64, 64), 64), bc * L : (bc + 1) * L] = piece.astype(BF16)
        return carry

    lax.fori_loop(0, 20, columns, 0)

    for g in range(2):
        acc = jnp.zeros((V, L), F32)
        for a in range(3):
            acc += jnp.dot(
                cols[g * 640 + a * 64 : g * 640 + a * 64 + V, :],
                wf[a * 9 * L : (a + 1) * 9 * L, :],
                preferred_element_type=F32,
            )
        pre[g * V : (g + 1) * V, :] = acc

    box_finish()
    boxes = jnp.concatenate(
        [inbox[pl.ds(n, PEERS, stride=8), :] for n in range(6)], axis=1
    ).astype(BF16)
    below = jnp.where(
        lax.broadcasted_iota(jnp.int32, (PEERS, L), 0) < me, inbox[pl.ds(6, PEERS, stride=8), :], 0.0
    )
    first = jnp.sum(below, axis=0, keepdims=True).astype(jnp.int32)[:, :64]
    pick = (
        lax.broadcasted_iota(jnp.int32, (64, 6 * L), 1) % 8
        == lax.broadcasted_iota(jnp.int32, (64, 6 * L), 0) % 8
    )
    peer = lax.broadcasted_iota(jnp.int32, (64, 64), 1)
    piece = lax.broadcasted_iota(jnp.int32, (64, 64), 0) // 8
    live = live_ref[0]
    s, q = 0.7978845608028654, 0.044715
    down_sums = jnp.zeros((L, 8 * L), F32)
    dealt = jnp.zeros((PEERS, 6 * L), F32)
    for g in range(2):
        mask = jnp.broadcast_to(own[g, :, C : C + 1].astype(F32), (V, L))
        tt = pre[g * V : (g + 1) * V, :]
        th = jnp.tanh(s * (tt + q * tt * tt * tt))
        hidden = (0.5 * tt * (1.0 + th) * mask).astype(BF16)
        slope = (0.5 * (1.0 + th) + 0.5 * tt * (1.0 - th * th) * (s * (1.0 + 3.0 * q * tt * tt))) * mask
        both = jnp.dot(
            perm[...], jnp.concatenate([hidden, mask.astype(BF16)], axis=1),
            preferred_element_type=F32,
        )
        kids = both[:, :L].astype(BF16)
        cmask = both[:64, L:]
        coarse = jnp.dot(kids[:64], wd[:L, :], preferred_element_type=F32)
        for j in range(1, 8):
            cmask = jnp.maximum(cmask, both[j * 64 : (j + 1) * 64, L:])
            coarse += jnp.dot(
                kids[j * 64 : (j + 1) * 64], wd[j * L : (j + 1) * L, :], preferred_element_type=F32
            )
        coarse = (coarse * cmask).astype(BF16)
        holder = jnp.bitwise_and(jnp.broadcast_to(first, (64, 64)) + g, 7) * 8 + piece
        chosen = jnp.where((holder == peer) & (g < live), 1.0, 0.0).astype(BF16)
        flat = jnp.dot(coarse, spread[...], preferred_element_type=F32)
        flat = jnp.where(pick, flat, 0.0).astype(BF16)
        dealt += lax.dot_general(chosen, flat, (((0,), (0,)), ((), ())), preferred_element_type=F32)
        dz = jnp.dot(chosen, boxes, preferred_element_type=F32)
        dz = jnp.where(pick, dz, 0.0).astype(BF16)
        dz = lax.dot_general(dz, spread[...], NT, preferred_element_type=F32)
        dz = jnp.where(cmask > 0, dz, 0.0)
        dzt = jnp.transpose(dz).astype(BF16)
        dz = dz.astype(BF16)
        down_sums += jnp.dot(
            dzt, jnp.concatenate([kids[j * 64 : (j + 1) * 64] for j in range(8)], axis=1),
            preferred_element_type=F32,
        )
        dh = jnp.concatenate(
            [
                lax.dot_general(dz, wd[j * L : (j + 1) * L, :], NT, preferred_element_type=F32)
                for j in range(8)
            ],
            axis=0,
        )
        high = dh.astype(BF16)
        low = (dh - high.astype(F32)).astype(BF16)
        dh = lax.dot_general(
            perm[...], jnp.concatenate([high, low], axis=1), (((0,), (0,)), ((), ())),
            preferred_element_type=F32,
        )
        dpre = slope * (dh[:, :L] + dh[:, L:])
        dpre16 = dpre.astype(BF16)
        for a in range(3):
            dpre3[g * 640 + a * 64 : g * 640 + a * 64 + V, a * L : (a + 1) * L] = dpre16
        pre[g * V : (g + 1) * V, :] = dpre
    for n in range(6):
        coarse_box[pl.ds(n, PEERS, stride=8), :] = dealt[:, n * L : (n + 1) * L]

    lane = lax.broadcasted_iota(jnp.int32, (C, L), 1)
    held = {}

    def keep(k, product):
        held[k % 4] = jnp.transpose(product)[:C]
        if k % 4 == 3 or k == 34:
            last = held.get(3)
            for n in range(3):
                slab = held[n]
                if last is not None:
                    slab = jnp.where(lane < C, slab, pltpu.roll(last, C - 32 * n, 1))
                at = (3 * (k // 4) + n) * C
                sums32[at : at + C, :] = slab
                sums16[at : at + C, :] = slab.astype(BF16)
            held.clear()

    dt = jnp.transpose(pre[...]).astype(BF16)
    for a in range(3):
        for bc in range(0, 9, 2):
            lanes = slice(bc * L, min(bc + 2, 9) * L)
            value = jnp.dot(
                dt[:, :V], cols[a * 64 : a * 64 + V, lanes], preferred_element_type=F32
            ) + jnp.dot(
                dt[:, V:], cols[640 + a * 64 : 640 + a * 64 + V, lanes], preferred_element_type=F32
            )
            for n in range(min(2, 9 - bc)):
                keep(a * 9 + bc + n, value[:, n * L : (n + 1) * L])
    for j in range(8):
        keep(27 + j, down_sums[:, j * L : (j + 1) * L])
    sums32[27 * C :, :] = jnp.zeros((C, L), F32)
    sums16[27 * C :, :] = jnp.zeros((C, L), BF16)

    def span(at, count):
        return pl.ds(pl.multiple_of(at, 16), count)

    def device(yy, zz):
        return yy * 16 + zz * 2 + core

    pair = remote(sums16.at[span((1 - core) * HALF, HALF)], pair_in, pair_sent, pair_arrived, partner)
    pair.start()
    back_start, back_finish = swap(me, coarse_box, coarse_in, back_sent, back_arrived)
    back_start()
    coarse_in[mine, :] = coarse_box[mine, :]
    pair.wait_recv()
    value = sums32[span(core * HALF, HALF), :] + pair_in[...].astype(F32)
    chip32[...] = value
    chip16[...] = value.astype(BF16)
    ysteps = []
    for n in range(3):
        yy = jnp.bitwise_and(y + n + 1, 3)
        ysteps.append(
            remote(chip16.at[span(yy * YPART, YPART)], y_in.at[n], ysent.at[n], yarrived.at[n], device(yy, z))
        )
        ysteps[n].start()

    gpad[...] = jnp.zeros_like(gpad)
    for bc in range(0, 9, 2):
        width = min(2, 9 - bc)
        u[:, : width * L] = lax.dot_general(
            dpre3[...], wb[bc * L : (bc + width) * L, :], NT, preferred_element_type=F32
        )

        def add(gx, carry):
            for n in range(width):
                b, c = divmod(bc + n, 3)
                for yy in range(8):
                    at = pl.ds(gx * 100 + (yy + b) * 10 + c, 8)
                    gpad[at, :] += u[pl.ds(pl.multiple_of(gx * 64 + yy * 8, 8), 8), n * L : (n + 1) * L]
            return carry

        lax.fori_loop(0, 20, add, 0)

    value = chip32[span(y * YPART, YPART), :]
    for n in range(3):
        ysteps[n].wait_recv()
        value = value + y_in[n].astype(F32)
    y32[...] = value
    y16[...] = value.astype(BF16)

    def zstep(n):
        zz = jnp.bitwise_and(z + n + 1, 7)
        at = span(lax.min(zz, 6) * ZPART, ZPART)
        return zz < 7, remote(y16.at[at], z_in.at[n], zsent.at[n], zarrived.at[n], device(y, zz))

    for n in range(7):
        wanted, copy = zstep(n)

        @pl.when(wanted)
        def _():
            copy.start()

    gsource[...] = jnp.zeros_like(gsource)
    for g in range(2):
        for s0, ss, p0, ps, count in segments(0, 0, 0):
            gsource[rows((2 + g) * V + s0, count, ss), :] = gpad[rows(g * 1000 + p0, count, ps), :]

    def give(n, carry):
        for g in range(2):
            for k, offset in enumerate(OFFSETS):
                if k != 13:
                    here = jnp.where(table[g, k] == n, 1.0, 0.0)
                    for s0, ss, p0, ps, count in segments(*offset):
                        at = rows(n * V + s0, count, ss)
                        gsource[at, :] += gpad[rows(g * 1000 + p0, count, ps), :] * here
        return carry

    lax.fori_loop(0, 6, give, 0)
    for g in range(2):
        part_lower[g] = gsource[g * V : (g + 1) * V, :].astype(BF16)
        part_upper[g] = gsource[(4 + g) * V : (5 + g) * V, :].astype(BF16)
    rim_up = remote(part_upper, from_lower, rim_sent.at[0], rim_arrived.at[0], lax.min(me + 1, PEERS - 1))
    rim_down = remote(part_lower, from_upper, rim_sent.at[1], rim_arrived.at[1], lax.max(me - 1, 0))

    @pl.when(has_up)
    def _():
        rim_up.start()

    @pl.when(has_down)
    def _():
        rim_down.start()

    def gzstep(n, owner, to):
        at = span(core * HALF + y * YPART + owner * ZPART, ZPART)
        return remote(total.at[at], total.at[at], gzsent.at[n], gzarrived.at[n], device(y, to))

    @pl.when(z < 7)
    def _():
        value = y32[span(z * ZPART, ZPART), :]
        for n in range(7):
            zstep(n)[1].wait_recv()
            value = value + z_in[n].astype(F32)
        total[span(core * HALF + y * YPART + z * ZPART, ZPART), :] = value.astype(BF16)
        for n in range(7):
            gzstep(n, z, jnp.bitwise_and(z + n + 1, 7)).start()

    @pl.when(has_down)
    def _():
        rim_up.wait_recv()

    @pl.when(jnp.logical_not(has_down))
    def _():
        from_lower[...] = jnp.zeros_like(from_lower)

    @pl.when(has_up)
    def _():
        rim_down.wait_recv()

    @pl.when(jnp.logical_not(has_up))
    def _():
        from_upper[...] = jnp.zeros_like(from_upper)

    for g in range(2):
        value = gsource[(2 + g) * V : (3 + g) * V, :] + from_lower[g].astype(F32) + from_upper[g].astype(F32)
        value = value * jnp.broadcast_to(own[g, :, C : C + 1].astype(F32), (V, L))
        grad_features[g] = jnp.transpose(value)[:C, :].astype(BF16)

    for n in range(7):
        owner = jnp.bitwise_and(z + 7 - n, 7)

        @pl.when(owner < 7)
        def _():
            gzstep(n, lax.min(owner, 6), owner).wait_recv()

    def gystep(n, owner, to):
        at = span(core * HALF + owner * YPART, YPART)
        return remote(total.at[at], total.at[at], gysent.at[n], gyarrived.at[n], device(to, z))

    def across(n, which, owner):
        at = span(which * HALF + owner * YPART, YPART)
        return remote(total.at[at], total.at[at], copy_sent.at[n], copy_arrived.at[n], partner)

    owners = [jnp.bitwise_and(y + 4 - n, 3) for n in range(4)]
    for n in range(3):
        gystep(n, y, jnp.bitwise_and(y + n + 1, 3)).start()
    across(0, core, y).start()
    for n in range(3):
        gystep(n, owners[n + 1], owners[n + 1]).wait_recv()
        across(n + 1, core, owners[n + 1]).start()
    back_finish()
    for n in range(4):
        across(n, 1 - core, owners[n]).wait_recv()

    @pl.when(has_up)
    def _():
        up.wait_send()
        rim_up.wait_send()

    @pl.when(has_down)
    def _():
        down.wait_send()
        rim_down.wait_send()

    pair.wait_send()
    for n in range(3):
        ysteps[n].wait_send()
        gystep(n, y, jnp.bitwise_and(y + n + 1, 3)).wait_send()
    for n in range(7):
        wanted, copy = zstep(n)

        @pl.when(wanted)
        def _():
            copy.wait_send()

    @pl.when(z < 7)
    def _():
        for n in range(7):
            gzstep(n, z, jnp.bitwise_and(z + n + 1, 7)).wait_send()

    for n in range(4):
        across(n, core, owners[n]).wait_send()


def smem():
    return pl.BlockSpec(memory_space=pltpu.SMEM)


def vmem(n):
    return [pl.BlockSpec(memory_space=pltpu.VMEM)] * n


def hbm(n):
    return [pl.BlockSpec(memory_space=pl.ANY)] * n


def run_section(neighbours, live_count, occupancy, features, grad_coarse, w_subm, w_down):
    dma = pltpu.SemaphoreType.DMA
    block = pltpu.VMEM((2, V, L), BF16)
    boxes = pltpu.VMEM((8 * PEERS, L), F32)
    return pl.pallas_call(
        section_kernel,
        out_shape=(
            jax.ShapeDtypeStruct((8 * PEERS, L), F32),
            jax.ShapeDtypeStruct((2, C, V), BF16),
            jax.ShapeDtypeStruct((2 * HALF, L), BF16),
        ),
        in_specs=[smem(), smem(), smem()] + hbm(4),
        out_specs=tuple(vmem(3)),
        scratch_shapes=[
            pltpu.VMEM((2, C, V), BF16),
            pltpu.VMEM((PEERS, 6 * L), BF16),
            pltpu.VMEM((27, C, C), BF16),
            pltpu.VMEM((8, C, C), BF16),
            block, block, block, boxes, boxes, boxes,
            pltpu.VMEM((7 * V, L), F32),
            pltpu.VMEM((2000, L), F32),
            pltpu.VMEM((1280, 9 * L), BF16),
            pltpu.VMEM((27 * L, L), BF16),
            pltpu.VMEM((9 * L, 3 * L), BF16),
            pltpu.VMEM((8 * L, L), BF16),
            pltpu.VMEM((V, V), BF16),
            pltpu.VMEM((L, 6 * L), BF16),
            pltpu.VMEM((2 * V, L), F32),
            pltpu.VMEM((1280, 3 * L), BF16),
            pltpu.VMEM((1280, 2 * L), F32),
            pltpu.VMEM((2000, L), F32),
            pltpu.VMEM((6 * V, L), F32),
            pltpu.VMEM((2 * HALF, L), F32),
            pltpu.VMEM((2 * HALF, L), BF16),
            pltpu.VMEM((HALF, L), BF16),
            pltpu.VMEM((HALF, L), F32),
            pltpu.VMEM((HALF, L), BF16),
            pltpu.VMEM((3, YPART, L), BF16),
            pltpu.VMEM((YPART, L), F32),
            pltpu.VMEM((YPART, L), BF16),
            pltpu.VMEM((7, ZPART, L), BF16),
            block, block, block, block,
            dma((4,)), dma((PEERS,)), dma((PEERS,)), dma((PEERS,)), dma((PEERS,)),
            dma((2,)), dma((2,)), dma((2,)), dma((2,)), dma(()), dma(()),
            dma((3,)), dma((3,)), dma((7,)), dma((7,)), dma((7,)), dma((7,)),
            dma((3,)), dma((3,)), dma((4,)), dma((4,)),
        ],
        compiler_params=pltpu.CompilerParams(
            vmem_limit_bytes=VMEM_LIMIT, collective_id=0, has_side_effects=True
        ),
    )(neighbours, live_count, occupancy, features, grad_coarse, w_subm, w_down)


def final_kernel(
    coarse_in, features_in, total, coarse_out, grad_features, grad_subm, grad_down,
    coarse, subm, down, sem,
):
    copies = [pltpu.make_async_copy(features_in, grad_features, sem.at[0])]
    copies[0].start()
    for n in range(6):
        coarse[:, n * L : (n + 1) * L] = coarse_in[pl.ds(n, PEERS, stride=8), :].astype(BF16)
    copies.append(pltpu.make_async_copy(coarse, coarse_out, sem.at[1]))
    copies[1].start()
    lane = lax.broadcasted_iota(jnp.int32, (C, L), 1)
    for k in range(35):
        quad, n = divmod(k, 4)
        if n < 3:
            at = (3 * quad + n) * C
            value = total[at : at + C, :].astype(F32)[:, :C]
        else:
            value = jnp.zeros((C, L), F32)
            for m in range(3):
                at = (3 * quad + m) * C
                piece = pltpu.roll(total[at : at + C, :].astype(F32), 32 + 32 * m, 1)
                value = jnp.where(lane // 32 == m, piece, value)
            value = value[:, :C]
        if k < 27:
            subm[k] = value
        else:
            down[k - 27] = value
        if k in (8, 17, 26):
            part = pl.ds(k - 8, 9)
            copies.append(pltpu.make_async_copy(subm.at[part], grad_subm.at[part], sem.at[2 + k // 9]))
            copies[-1].start()
    copies.append(pltpu.make_async_copy(down, grad_down, sem.at[5]))
    copies[-1].start()
    for copy in copies:
        copy.wait()


def run_final(coarse_in, grad_features, total):
    return pl.pallas_call(
        final_kernel,
        out_shape=(
            jax.ShapeDtypeStruct((PEERS, 6 * L), BF16),
            jax.ShapeDtypeStruct((2, C, V), BF16),
            jax.ShapeDtypeStruct((27, C, C), F32),
            jax.ShapeDtypeStruct((8, C, C), F32),
        ),
        in_specs=vmem(3),
        out_specs=tuple(hbm(4)),
        scratch_shapes=[
            pltpu.VMEM((PEERS, 6 * L), BF16),
            pltpu.VMEM((27, C, C), F32),
            pltpu.VMEM((8, C, C), F32),
            pltpu.SemaphoreType.DMA((6,)),
        ],
        compiler_params=pltpu.CompilerParams(vmem_limit_bytes=VMEM_LIMIT),
    )(coarse_in, grad_features, total)


def per_device(features, occupancy, neighbours, live_count, w_subm, w_down, grad_coarse):
    return run_final(
        *run_section(neighbours, live_count, occupancy, features, grad_coarse, w_subm, w_down)
    )


def solution(mesh):
    blocks = P(("rep", "space"), None)
    return jax.shard_map(
        per_device,
        mesh=mesh,
        in_specs=(
            P(("rep", "space"), None, None), blocks, blocks, P(("rep", "space")), P(), P(), blocks,
        ),
        out_specs=(
            blocks, P(("rep", "space"), None, None), P("rep", None, None), P("rep", None, None),
        ),
        check_vma=False,
    )
```

time: 252 us -> 69.1 us (0.27)
  waiting for transfers between devices: 165 us -> 0 us
  Pallas kernels: 17.6 us -> 62.4 us
  starting transfers between devices: 23 us -> 0 us
  blocking collectives: 22.7 us -> 0 us
  between operations: 14.9 us -> 1.3 us
  local copies, waits for them, and re-layouts: 8.09 us -> 5.18 us
    psum x1 -> x0, waiting for transfers between devices: 159 us -> none  [per_device(): sums = jnp.transpose(lax.psum(sums, 'space')[:, :, :C], (0, 2, 1))]
    pallas_call x3 -> x2, Pallas kernels: 17.6 us -> 62.4 us  [the longest x1 61 us: run_section(): pl.pallas_call(section_kernel, out_shape=(jax.ShapeDtypeStruct((8 * PEERS...]
    all_to_all x1 -> x0, blocking collectives: 22.7 us -> none  [exchanged(): lax.all_to_all(boxes, 'space', split_axis=0, concat_axis=0, tiled=True)]
    all_to_all x1 -> x0, starting transfers between devices: 13.2 us -> none  [exchanged(): lax.all_to_all(boxes, 'space', split_axis=0, concat_axis=0, tiled=True)]
    ppermute x4 -> x0, starting transfers between devices: 9.8 us -> none  [shifted(): return lax.ppermute(block, 'space', route)]
    ppermute x4 -> x0, waiting for transfers between devices: 5.77 us -> none  [shifted(): return lax.ppermute(block, 'space', route)]
    unnamed x13 -> x12, local copies, waits for them, and re-layouts: 4.66 us -> 5.18 us
  transfers between devices with their start and end apart: 6 -> 0, of which waited for: 3 -> 0; matrix products, arithmetic and copies ran while one was open for 0% -> 0% of each run, Pallas kernels for 1% -> 0%
where the time goes in v3:
time: 69.1 us; the launch traced here: 68.9 us
  Pallas kernels  62.4 us (90%)
  local copies, waits for them, and re-layouts  5.18 us (7%)
  between operations  1.3 us (2%)
    pallas_call x1, Pallas kernels, run_section(): pl.pallas_call(section_kernel, out_shape=(jax.ShapeDtypeStruct((8 * PEERS...  61 us
    unnamed x12, local copies, waits for them, and re-layouts  5.18 us

profile of v3, /device:TPU:1, one launch (start us, length us, event | category | flops | bytes accessed | tf_op | source)
XLA Modules:
  0.0 68.9 jit_solution(8907568431573430653)
XLA Ops:
  1.3 0.0 copy-start
  1.3 1.1 %copy-done = bf16[27,96,96]{2,1,0:T(8,128)(2,1)S(1)} copy-done((bf16[27,96,96]{2,1,0:T(8,128)(2,1)S(1)}, bf16[27,96,96]{2,1,0:T(8,128)(2,1)}, u32[]{:S(2)}) %copy-start) | copy-done | bytes 497688
  2.4 0.0 copy-start.1
  2.4 0.9 %copy-done.1 = bf16[2,96,512]{2,1,0:T(8,128)(2,1)S(1)} copy-done((bf16[2,96,512]{2,1,0:T(8,128)(2,1)S(1)}, bf16[2,96,512]{2,1,0:T(8,128)(2,1)}, u32[]{:S(2)}) %copy-start.1) | copy-done | bytes 196632
  3.3 0.0 copy-start.2
  3.3 0.9 %copy-done.2 = bf16[8,96,96]{2,1,0:T(8,128)(2,1)S(1)} copy-done((bf16[8,96,96]{2,1,0:T(8,128)(2,1)S(1)}, bf16[8,96,96]{2,1,0:T(8,128)(2,1)}, u32[]{:S(2)}) %copy-start.2) | copy-done | bytes 147480
  4.2 0.0 copy-start.3
  4.2 0.9 %copy-done.3 = bf16[64,768]{1,0:T(8,128)(2,1)S(1)} copy-done((bf16[64,768]{1,0:T(8,128)(2,1)S(1)}, bf16[64,768]{1,0:T(8,128)(2,1)}, u32[]{:S(2)}) %copy-start.3) | copy-done | bytes 98328
  5.1 0.0 copy-start.4
  5.1 0.7 copy-done.4
  5.8 0.0 copy-start.5
  5.8 0.7 copy-done.5
  6.5 61.0 %shard_map.102 = (f32[512,128]{1,0:T(8,128)S(1)}, bf16[2,96,512]{2,1,0:T(8,128)(2,1)S(1)}, bf16[2688,128]{1,0:T(8,128)(2,1)S(1)}) custom-call(s32[2,27]{1,0:T(2,128)S(1)} %copy-done.4, s32[1]{0:T(128)S(6)} %copy.11.live_ref, s32[2,16]{1,0:T(2,128)S(1)} %copy-done.5, bf16[2,96,512]{2,1,0:T(8,128)(2,1)S(1)} %copy-done.1, bf16[64,768]{1,0:T(8,128)(2,1)S(1)} %copy-done.3, ...), custom_call_target="tpu_custom_call" | custom-call | tf_op jit(solution)/shard_map/pallas_call | solution.py:532
  67.5 1.4 %shard_map.103 = (bf16[64,768]{1,0:T(8,128)(2,1)}, bf16[2,96,512]{2,1,0:T(8,128)(2,1)}, f32[27,96,96]{2,1,0:T(8,128)}, f32[8,96,96]{2,1,0:T(8,128)}) custom-call(f32[512,128]{1,0:T(8,128)S(1)} %get-tuple-element.7.coarse_in, bf16[2,96,512]{2,1,0:T(8,128)(2,1)S(1)} %get-tuple-element.8.features_in, bf16[2688,128]{1,0:T(8,128)(2,1)S(1)} %get-tuple-element.9.total), custom_call_target="tpu_custom_call" | custom-call | tf_op jit(solution)/shard_map/pallas_call | solution.py:619
Async XLA Ops:
  1.3 1.1 %copy-start = (bf16[27,96,96]{2,1,0:T(8,128)(2,1)S(1)}, bf16[27,96,96]{2,1,0:T(8,128)(2,1)}, u32[]{:S(2)}) copy-start(bf16[27,96,96]{2,1,0:T(8,128)(2,1)} %w_subm_hbm.1) | copy-start | bytes 1492996
  2.4 0.9 %copy-start.1 = (bf16[2,96,512]{2,1,0:T(8,128)(2,1)S(1)}, bf16[2,96,512]{2,1,0:T(8,128)(2,1)}, u32[]{:S(2)}) copy-start(bf16[2,96,512]{2,1,0:T(8,128)(2,1)} %features_hbm.1) | copy-start | bytes 589828
  3.3 0.9 %copy-start.2 = (bf16[8,96,96]{2,1,0:T(8,128)(2,1)S(1)}, bf16[8,96,96]{2,1,0:T(8,128)(2,1)}, u32[]{:S(2)}) copy-start(bf16[8,96,96]{2,1,0:T(8,128)(2,1)} %w_down_hbm.1) | copy-start | bytes 442372
  4.2 0.9 %copy-start.3 = (bf16[64,768]{1,0:T(8,128)(2,1)S(1)}, bf16[64,768]{1,0:T(8,128)(2,1)}, u32[]{:S(2)}) copy-start(bf16[64,768]{1,0:T(8,128)(2,1)} %cotangent_hbm.1) | copy-start | bytes 294916
  5.1 0.7 copy-start.4
  5.8 0.7 copy-start.5

commit v4 on v3

--- a/solution.py
+++ b/solution.py
@@ -11,7 +11,7 @@
 OFFSETS = [(a, b, c) for a in (-1, 0, 1) for b in (-1, 0, 1) for c in (-1, 0, 1)]
 PEERS = 64
 HALF, YPART, ZPART = 1344, 336, 48
-VMEM_LIMIT = 50 * 2**20
+VMEM_LIMIT = 63 * 2**20 + 2**19
 F32, BF16 = jnp.float32, jnp.bfloat16
 NT = (((1,), (1,)), ((), ()))
 
@@ -228,14 +228,6 @@
             )
         pre[g * V : (g + 1) * V, :] = acc
 
-    box_finish()
-    boxes = jnp.concatenate(
-        [inbox[pl.ds(n, PEERS, stride=8), :] for n in range(6)], axis=1
-    ).astype(BF16)
-    below = jnp.where(
-        lax.broadcasted_iota(jnp.int32, (PEERS, L), 0) < me, inbox[pl.ds(6, PEERS, stride=8), :], 0.0
-    )
-    first = jnp.sum(below, axis=0, keepdims=True).astype(jnp.int32)[:, :64]
     pick = (
         lax.broadcasted_iota(jnp.int32, (64, 6 * L), 1) % 8
         == lax.broadcasted_iota(jnp.int32, (64, 6 * L), 0) % 8
@@ -246,6 +238,7 @@
     s, q = 0.7978845608028654, 0.044715
     down_sums = jnp.zeros((L, 8 * L), F32)
     dealt = jnp.zeros((PEERS, 6 * L), F32)
+    halves = []
     for g in range(2):
         mask = jnp.broadcast_to(own[g, :, C : C + 1].astype(F32), (V, L))
         tt = pre[g * V : (g + 1) * V, :]
@@ -265,10 +258,21 @@
                 kids[j * 64 : (j + 1) * 64], wd[j * L : (j + 1) * L, :], preferred_element_type=F32
             )
         coarse = (coarse * cmask).astype(BF16)
+        flat = jnp.dot(coarse, spread[...], preferred_element_type=F32)
+        halves.append((slope, kids, cmask, jnp.where(pick, flat, 0.0).astype(BF16)))
+
+    box_finish()
+    boxes = jnp.concatenate(
+        [inbox[pl.ds(n, PEERS, stride=8), :] for n in range(6)], axis=1
+    ).astype(BF16)
+    below = jnp.where(
+        lax.broadcasted_iota(jnp.int32, (PEERS, L), 0) < me, inbox[pl.ds(6, PEERS, stride=8), :], 0.0
+    )
+    first = jnp.sum(below, axis=0, keepdims=True).astype(jnp.int32)[:, :64]
+    for g in range(2):
+        slope, kids, cmask, flat = halves[g]
         holder = jnp.bitwise_and(jnp.broadcast_to(first, (64, 64)) + g, 7) * 8 + piece
         chosen = jnp.where((holder == peer) & (g < live), 1.0, 0.0).astype(BF16)
-        flat = jnp.dot(coarse, spread[...], preferred_element_type=F32)
-        flat = jnp.where(pick, flat, 0.0).astype(BF16)
         dealt += lax.dot_general(chosen, flat, (((0,), (0,)), ((), ())), preferred_element_type=F32)
         dz = jnp.dot(chosen, boxes, preferred_element_type=F32)
         dz = jnp.where(pick, dz, 0.0).astype(BF16)
@@ -341,9 +345,6 @@
 
     pair = remote(sums16.at[span((1 - core) * HALF, HALF)], pair_in, pair_sent, pair_arrived, partner)
     pair.start()
-    back_start, back_finish = swap(me, coarse_box, coarse_in, back_sent, back_arrived)
-    back_start()
-    coarse_in[mine, :] = coarse_box[mine, :]
     pair.wait_recv()
     value = sums32[span(core * HALF, HALF), :] + pair_in[...].astype(F32)
     chip32[...] = value
@@ -392,6 +393,10 @@
         def _():
             copy.start()
 
+    back_start, back_finish = swap(me, coarse_box, coarse_in, back_sent, back_arrived)
+    back_start()
+    coarse_in[mine, :] = coarse_box[mine, :]
+
     gsource[...] = jnp.zeros_like(gsource)
     for g in range(2):
         for s0, ss, p0, ps, count in segments(0, 0, 0):
@@ -436,27 +441,6 @@
         for n in range(7):
             gzstep(n, z, jnp.bitwise_and(z + n + 1, 7)).start()
 
-    @pl.when(has_down)
-    def _():
-        rim_up.wait_recv()
-
-    @pl.when(jnp.logical_not(has_down))
-    def _():
-        from_lower[...] = jnp.zeros_like(from_lower)
-
-    @pl.when(has_up)
-    def _():
-        rim_down.wait_recv()
-
-    @pl.when(jnp.logical_not(has_up))
-    def _():
-        from_upper[...] = jnp.zeros_like(from_upper)
-
-    for g in range(2):
-        value = gsource[(2 + g) * V : (3 + g) * V, :] + from_lower[g].astype(F32) + from_upper[g].astype(F32)
-        value = value * jnp.broadcast_to(own[g, :, C : C + 1].astype(F32), (V, L))
-        grad_features[g] = jnp.transpose(value)[:C, :].astype(BF16)
-
     for n in range(7):
         owner = jnp.bitwise_and(z + 7 - n, 7)
 
@@ -476,6 +460,28 @@
     for n in range(3):
         gystep(n, y, jnp.bitwise_and(y + n + 1, 3)).start()
     across(0, core, y).start()
+
+    @pl.when(has_down)
+    def _():
+        rim_up.wait_recv()
+
+    @pl.when(jnp.logical_not(has_down))
+    def _():
+        from_lower[...] = jnp.zeros_like(from_lower)
+
+    @pl.when(has_up)
+    def _():
+        rim_down.wait_recv()
+
+    @pl.when(jnp.logical_not(has_up))
+    def _():
+        from_upper[...] = jnp.zeros_like(from_upper)
+
+    for g in range(2):
+        value = gsource[(2 + g) * V : (3 + g) * V, :] + from_lower[g].astype(F32) + from_upper[g].astype(F32)
+        value = value * jnp.broadcast_to(own[g, :, C : C + 1].astype(F32), (V, L))
+        grad_features[g] = jnp.transpose(value)[:C, :].astype(BF16)
+
     for n in range(3):
         gystep(n, owners[n + 1], owners[n + 1]).wait_recv()
         across(n + 1, core, owners[n + 1]).start()
@@ -522,7 +528,7 @@
 
 
 def hbm(n):
-    return [pl.BlockSpec(memory_space=pl.ANY)] * n
+    return [pl.BlockSpec(memory_space=pltpu.HBM)] * n
 
 
 def run_section(neighbours, live_count, occupancy, features, grad_coarse, w_subm, w_down):

time: 69.1 us -> 65.7 us (0.951)
  local copies, waits for them, and re-layouts: 5.18 us -> 0 us
  Pallas kernels: 62.4 us -> 64.3 us
    unnamed x12 -> x0, local copies, waits for them, and re-layouts: 5.18 us -> none
    pallas_call x1, Pallas kernels: 1.37 us -> 2.65 us  [run_final(): pl.pallas_call(final_kernel, out_shape=(jax.ShapeDtypeStruct((PEERS, 6 *...]
where the time goes in v4:
time: 65.7 us; the launch traced here: 65.6 us
  Pallas kernels  64.3 us (98%)
  between operations  1.29 us (2%)
    pallas_call x1, Pallas kernels, run_section(): pl.pallas_call(section_kernel, out_shape=(jax.ShapeDtypeStruct((8 * PEERS...  61.7 us
    pallas_call x1, Pallas kernels, run_final(): pl.pallas_call(final_kernel, out_shape=(jax.ShapeDtypeStruct((PEERS, 6 *...  2.65 us

profile of v4, /device:TPU:1, one launch (start us, length us, event | category | flops | bytes accessed | tf_op | source)
XLA Modules:
  0.0 65.6 jit_solution(15642100943089438451)
XLA Ops:
  1.3 61.7 %shard_map.102 = (f32[512,128]{1,0:T(8,128)}, bf16[2,96,512]{2,1,0:T(8,128)(2,1)}, bf16[2688,128]{1,0:T(8,128)(2,1)}) custom-call(s32[2,27]{1,0:T(2,128)} %table.1, s32[1]{0:T(128)S(6)} %copy.11.live_ref, s32[2,16]{1,0:T(2,128)} %occupancy_ref.1, bf16[2,96,512]{2,1,0:T(8,128)(2,1)} %features_hbm.1, bf16[64,768]{1,0:T(8,128)(2,1)} %cotangent_hbm.1, ...), custom_call_target="tpu_custom_call" | custom-call | tf_op jit(solution)/shard_map/pallas_call | solution.py:538
  62.9 2.7 %shard_map.103 = (bf16[64,768]{1,0:T(8,128)(2,1)}, bf16[2,96,512]{2,1,0:T(8,128)(2,1)}, f32[27,96,96]{2,1,0:T(8,128)}, f32[8,96,96]{2,1,0:T(8,128)}) custom-call(f32[512,128]{1,0:T(8,128)} %get-tuple-element.7.coarse_in, bf16[2,96,512]{2,1,0:T(8,128)(2,1)} %get-tuple-element.8.features_in, bf16[2688,128]{1,0:T(8,128)(2,1)} %get-tuple-element.9.total), custom_call_target="tpu_custom_call" | custom-call | tf_op jit(solution)/shard_map/pallas_call | solution.py:625

commit v5 on v4

--- a/solution.py
+++ b/solution.py
@@ -9,7 +9,7 @@
 
 C, L, V = 96, 128, 512
 OFFSETS = [(a, b, c) for a in (-1, 0, 1) for b in (-1, 0, 1) for c in (-1, 0, 1)]
-PEERS = 64
+PEERS, CHIPS = 64, 32
 HALF, YPART, ZPART = 1344, 336, 48
 VMEM_LIMIT = 63 * 2**20 + 2**19
 F32, BF16 = jnp.float32, jnp.bfloat16
@@ -58,54 +58,78 @@
     )
 
 
-def greet_all(me):
+def greet(me):
     barrier = pltpu.get_barrier_semaphore()
-
-    def tell(i, carry):
+    here, core = me // 2, lax.rem(me, 2)
+
+    def tell(peer):
         pl.semaphore_signal(
-            barrier, inc=1, device_id={"space": lax.rem(me + i, PEERS)},
-            device_id_type=pl.DeviceIdType.MESH,
+            barrier, inc=1, device_id={"space": peer}, device_id_type=pl.DeviceIdType.MESH
         )
+
+    tell(lax.rem(me + 2 * core - 1 + PEERS, PEERS))
+    tell(me + 1 - 2 * core)
+
+    def tell_chip(i, carry):
+        tell(jnp.bitwise_and(here + i, CHIPS - 1) * 2 + core)
         return carry
 
-    lax.fori_loop(1, PEERS, tell, 0)
+    lax.fori_loop(1, CHIPS, tell_chip, 0)
 
 
 def greeted():
-    pl.semaphore_wait(pltpu.get_barrier_semaphore(), PEERS - 1)
-
-
-def swap(me, outbox, inbox, sent, arrived):
-    def box(i):
-        peer = lax.rem(me + i, PEERS)
-        return pl.ds(pl.multiple_of(peer * 8, 8), 8), peer
-
-    def start(i, carry):
-        at, peer = box(i)
-        mine = pl.ds(pl.multiple_of(me * 8, 8), 8)
-        remote(outbox.at[at], inbox.at[mine], sent.at[peer], arrived.at[me], peer).start()
-        return carry
-
-    def finish(i, carry):
-        at, peer = box(i)
-        remote(outbox.at[at], inbox.at[at], sent.at[peer], arrived.at[peer], peer).wait()
-        return carry
-
-    return (
-        lambda: lax.fori_loop(1, PEERS, start, 0),
-        lambda: lax.fori_loop(1, PEERS, finish, 0),
-    )
+    pl.semaphore_wait(pltpu.get_barrier_semaphore(), CHIPS + 1)
+
+
+class Deal:
+    def __init__(self, me, outbox, near, far, sent, arrived, far_sent, far_arrived):
+        self.here, self.core = me // 2, lax.rem(me, 2)
+        self.outbox, self.near = outbox, near
+        self.sems = sent, arrived
+        self.across = remote(near, far, far_sent, far_arrived, me + 1 - 2 * self.core)
+        every = pl.ds(0, 16 * (CHIPS - 1))
+        self.every = remote(outbox.at[every], near.at[every], sent, arrived, me + 1 - 2 * self.core)
+
+    def tile(self, chip):
+        return pl.ds(pl.multiple_of(chip * 16, 16), 16)
+
+    def start(self):
+        def send(i, carry):
+            there = jnp.bitwise_and(self.here + i, CHIPS - 1)
+            remote(
+                self.outbox.at[self.tile(there)], self.near.at[self.tile(self.here)],
+                *self.sems, there * 2 + self.core,
+            ).start()
+            return carry
+
+        lax.fori_loop(1, CHIPS, send, 0)
+        self.near[self.tile(self.here), :] = self.outbox[self.tile(self.here), :]
+
+    def forward(self):
+        self.every.wait_recv()
+        self.across.start()
+
+    def finish(self):
+        self.across.wait_recv()
+
+    def close(self):
+        self.every.wait_send()
+        self.across.wait_send()
+
+
+def box_rows(core, n):
+    return pl.ds(core * 8 + n, CHIPS, stride=16)
 
 
 def section_kernel(
     table, live_ref, occupancy_ref, features_hbm, cotangent_hbm, w_subm_hbm, w_down_hbm,
-    coarse_in, grad_features, total,
+    coarse_out, grad_features, total,
     features, cotangent, w_subm, w_down,
-    own, lower, upper, outbox, inbox, coarse_box,
-    source, pad, cols, wf, wb, wd, perm, spread, pre, dpre3, u, gpad, gsource,
+    own, lower, upper, box32, near32, far32, out32, outbox, near, far, back, back_near, back_far,
+    source, pad, cols, wf, wb, wd, perm, permt, spread, pre, dpre3, u, gpad, gsource,
     sums32, sums16, pair_in, chip32, chip16, y_in, y32, y16, z_in,
     part_lower, part_upper, from_lower, from_upper,
-    load_sem, box_sent, box_arrived, back_sent, back_arrived, halo_sent, halo_arrived,
+    load_sem, box_sem, back_sem, halo_sent, halo_arrived,
     rim_sent, rim_arrived, pair_sent, pair_arrived, ysent, yarrived, zsent, zarrived,
     gzsent, gzarrived, gysent, gyarrived, copy_sent, copy_arrived,
 ):
@@ -121,13 +145,18 @@
     ]
     for load in loads:
         load.start()
-    greet_all(me)
+    greet(me)
 
     i = lax.broadcasted_iota(jnp.int32, (V, V), 0)
     v = lax.broadcasted_iota(jnp.int32, (V, V), 1)
-    j, t = i // 64, i % 64
-    vx, vy, vz = 2 * (t // 16) + j // 4, 2 * (t // 4 % 4) + j // 2 % 2, 2 * (t % 4) + j % 2
-    perm[...] = jnp.where(vx * 64 + vy * 8 + vz == v, 1.0, 0.0).astype(BF16)
+
+    def placed(index, parts):
+        return sum(((index >> a) & b) << c for a, b, c in parts)
+
+    to_voxel = ((8, 1, 6), (7, 1, 3), (6, 1, 0), (4, 3, 7), (2, 3, 4), (0, 3, 1))
+    to_child = tuple((c, b, a) for a, b, c in to_voxel)
+    perm[...] = jnp.where(placed(i[:, :1], to_voxel) == v, 1.0, 0.0).astype(BF16)
+    permt[...] = jnp.where(placed(i[:, :1], to_child) == v, 1.0, 0.0).astype(BF16)
     spread[...] = jnp.where(
         lax.broadcasted_iota(jnp.int32, (L, 6 * L), 1) // 8
         == lax.broadcasted_iota(jnp.int32, (L, 6 * L), 0),
@@ -137,7 +166,6 @@
     wb[...] = jnp.zeros_like(wb)
     wd[...] = jnp.zeros_like(wd)
     dpre3[...] = jnp.zeros_like(dpre3)
-    coarse_box[...] = jnp.zeros_like(coarse_box)
     source[6 * V :, :] = jnp.zeros((V, L), F32)
 
     loads[0].wait()
@@ -145,10 +173,11 @@
         own[g] = masked_rows(features, occupancy_ref, live_ref[0], g)
     loads[1].wait()
     for n in range(6):
-        outbox[pl.ds(n, PEERS, stride=8), :] = cotangent[:, n * L : (n + 1) * L].astype(F32)
+        box32[pl.ds(n, PEERS, stride=8), :] = cotangent[:, n * L : (n + 1) * L].astype(F32)
     counts = jnp.broadcast_to(live_ref[0].astype(F32), (PEERS, L))
     for n in (6, 7):
-        outbox[pl.ds(n, PEERS, stride=8), :] = counts
+        box32[pl.ds(n, PEERS, stride=8), :] = counts
+    outbox[...] = box32[...].astype(BF16)
 
     greeted()
     up = remote(own, lower, halo_sent.at[0], halo_arrived.at[0], lax.min(me + 1, PEERS - 1))
@@ -162,10 +191,8 @@
     def _():
         down.start()
 
-    box_start, box_finish = swap(me, outbox, inbox, box_sent, box_arrived)
-    box_start()
-    mine = pl.ds(pl.multiple_of(me * 8, 8), 8)
-    inbox[mine, :] = outbox[mine, :]
+    deal = Deal(me, outbox, near, far, *(box_sem.at[n] for n in range(4)))
+    deal.start()
 
     loads[2].wait()
     loads[3].wait()
@@ -217,6 +244,7 @@
         return carry
 
     lax.fori_loop(0, 20, columns, 0)
+    deal.forward()
 
     for g in range(2):
         acc = jnp.zeros((V, L), F32)
@@ -232,7 +260,6 @@
         lax.broadcasted_iota(jnp.int32, (64, 6 * L), 1) % 8
         == lax.broadcasted_iota(jnp.int32, (64, 6 * L), 0) % 8
     )
-    peer = lax.broadcasted_iota(jnp.int32, (64, 64), 1)
     piece = lax.broadcasted_iota(jnp.int32, (64, 64), 0) // 8
     live = live_ref[0]
     s, q = 0.7978845608028654, 0.044715
@@ -261,18 +288,24 @@
         flat = jnp.dot(coarse, spread[...], preferred_element_type=F32)
         halves.append((slope, kids, cmask, jnp.where(pick, flat, 0.0).astype(BF16)))
 
-    box_finish()
-    boxes = jnp.concatenate(
-        [inbox[pl.ds(n, PEERS, stride=8), :] for n in range(6)], axis=1
-    ).astype(BF16)
-    below = jnp.where(
-        lax.broadcasted_iota(jnp.int32, (PEERS, L), 0) < me, inbox[pl.ds(6, PEERS, stride=8), :], 0.0
-    )
+    deal.finish()
+    near32[...] = near[...].astype(F32)
+    far32[...] = far[...].astype(F32)
+
+    def lines(n):
+        return jnp.concatenate([near32[box_rows(core, n), :], far32[box_rows(core, n), :]], axis=0)
+
+    def peers(dim, shape):
+        order = lax.broadcasted_iota(jnp.int32, shape, dim)
+        return jnp.where(order < CHIPS, 2 * order + core, 2 * (order - CHIPS) + 1 - core)
+
+    boxes = jnp.concatenate([lines(n) for n in range(6)], axis=1).astype(BF16)
+    below = jnp.where(peers(0, (PEERS, L)) < me, lines(6), 0.0)
     first = jnp.sum(below, axis=0, keepdims=True).astype(jnp.int32)[:, :64]
     for g in range(2):
         slope, kids, cmask, flat = halves[g]
         holder = jnp.bitwise_and(jnp.broadcast_to(first, (64, 64)) + g, 7) * 8 + piece
-        chosen = jnp.where((holder == peer) & (g < live), 1.0, 0.0).astype(BF16)
+        chosen = jnp.where((holder == peers(1, (64, 64))) & (g < live), 1.0, 0.0).astype(BF16)
         dealt += lax.dot_general(chosen, flat, (((0,), (0,)), ((), ())), preferred_element_type=F32)
         dz = jnp.dot(chosen, boxes, preferred_element_type=F32)
         dz = jnp.where(pick, dz, 0.0).astype(BF16)
@@ -294,7 +327,7 @@
         high = dh.astype(BF16)
         low = (dh - high.astype(F32)).astype(BF16)
         dh = lax.dot_general(
-            perm[...], jnp.concatenate([high, low], axis=1), (((0,), (0,)), ((), ())),
+            permt[...], jnp.concatenate([high, low], axis=1), (((1,), (0,)), ((), ())),
             preferred_element_type=F32,
         )
         dpre = slope * (dh[:, :L] + dh[:, L:])
@@ -303,7 +336,9 @@
             dpre3[g * 640 + a * 64 : g * 640 + a * 64 + V, a * L : (a + 1) * L] = dpre16
         pre[g * V : (g + 1) * V, :] = dpre
     for n in range(6):
-        coarse_box[pl.ds(n, PEERS, stride=8), :] = dealt[:, n * L : (n + 1) * L]
+        box32[box_rows(core, n), :] = dealt[:CHIPS, n * L : (n + 1) * L]
+        box32[box_rows(1 - core, n), :] = dealt[CHIPS:, n * L : (n + 1) * L]
+    back[...] = box32[...].astype(BF16)
 
     lane = lax.broadcasted_iota(jnp.int32, (C, L), 1)
     held = {}
@@ -393,9 +428,8 @@
         def _():
             copy.start()
 
-    back_start, back_finish = swap(me, coarse_box, coarse_in, back_sent, back_arrived)
-    back_start()
-    coarse_in[mine, :] = coarse_box[mine, :]
+    deal_back = Deal(me, back, back_near, back_far, *(back_sem.at[n] for n in range(4)))
+    deal_back.start()
 
     gsource[...] = jnp.zeros_like(gsource)
     for g in range(2):
@@ -441,6 +475,7 @@
         for n in range(7):
             gzstep(n, z, jnp.bitwise_and(z + n + 1, 7)).start()
 
+    deal_back.forward()
     for n in range(7):
         owner = jnp.bitwise_and(z + 7 - n, 7)
 
@@ -485,7 +520,14 @@
     for n in range(3):
         gystep(n, owners[n + 1], owners[n + 1]).wait_recv()
         across(n + 1, core, owners[n + 1]).start()
-    back_finish()
+    deal_back.finish()
+    near32[...] = back_near[...].astype(F32)
+    far32[...] = back_far[...].astype(F32)
+    for n in range(6):
+        out32[pl.ds(n * PEERS + core, CHIPS, stride=2), :] = near32[box_rows(core, n), :]
+        out32[pl.ds(n * PEERS + 1 - core, CHIPS, stride=2), :] = far32[box_rows(core, n), :]
+    for n in range(6):
+        coarse_out[:, n * L : (n + 1) * L] = out32[n * PEERS : (n + 1) * PEERS, :].astype(BF16)
     for n in range(4):
         across(n, 1 - core, owners[n]).wait_recv()
 
@@ -499,6 +541,8 @@
         down.wait_send()
         rim_down.wait_send()
 
+    deal.close()
+    deal_back.close()
     pair.wait_send()
     for n in range(3):
         ysteps[n].wait_send()
@@ -535,10 +579,11 @@
     dma = pltpu.SemaphoreType.DMA
     block = pltpu.VMEM((2, V, L), BF16)
     boxes = pltpu.VMEM((8 * PEERS, L), F32)
+    sent = pltpu.VMEM((8 * PEERS, L), BF16)
     return pl.pallas_call(
         section_kernel,
         out_shape=(
-            jax.ShapeDtypeStruct((8 * PEERS, L), F32),
+            jax.ShapeDtypeStruct((PEERS, 6 * L), BF16),
             jax.ShapeDtypeStruct((2, C, V), BF16),
             jax.ShapeDtypeStruct((2 * HALF, L), BF16),
         ),
@@ -549,13 +594,15 @@
             pltpu.VMEM((PEERS, 6 * L), BF16),
             pltpu.VMEM((27, C, C), BF16),
             pltpu.VMEM((8, C, C), BF16),
-            block, block, block, boxes, boxes, boxes,
+            block, block, block, boxes, boxes, boxes, pltpu.VMEM((6 * PEERS, L), F32),
+            sent, sent, sent, sent, sent, sent,
             pltpu.VMEM((7 * V, L), F32),
             pltpu.VMEM((2000, L), F32),
             pltpu.VMEM((1280, 9 * L), BF16),
             pltpu.VMEM((27 * L, L), BF16),
             pltpu.VMEM((9 * L, 3 * L), BF16),
             pltpu.VMEM((8 * L, L), BF16),
+            pltpu.VMEM((V, V), BF16),
             pltpu.VMEM((V, V), BF16),
             pltpu.VMEM((L, 6 * L), BF16),
             pltpu.VMEM((2 * V, L), F32),
@@ -573,7 +620,7 @@
             pltpu.VMEM((YPART, L), BF16),
             pltpu.VMEM((7, ZPART, L), BF16),
             block, block, block, block,
-            dma((4,)), dma((PEERS,)), dma((PEERS,)), dma((PEERS,)), dma((PEERS,)),
+            dma((4,)), dma((4,)), dma((4,)),
             dma((2,)), dma((2,)), dma((2,)), dma((2,)), dma(()), dma(()),
             dma((3,)), dma((3,)), dma((7,)), dma((7,)), dma((7,)), dma((7,)),
             dma((3,)), dma((3,)), dma((4,)), dma((4,)),
@@ -585,18 +632,28 @@
 
 
 def final_kernel(
-    coarse_in, features_in, total, coarse_out, grad_features, grad_subm, grad_down,
-    coarse, subm, down, sem,
+    coarse_in, features_in, total_in, coarse_out, grad_features, grad_subm, grad_down,
+    total, subm, down, load_sem, sem,
 ):
-    copies = [pltpu.make_async_copy(features_in, grad_features, sem.at[0])]
+    def chunk(n):
+        return pl.ds(9 * C * n, 9 * C)
+
+    loads = [
+        pltpu.make_async_copy(total_in.at[chunk(n)], total.at[chunk(n)], load_sem.at[n]) for n in range(3)
+    ]
+    for load in loads:
+        load.start()
+    copies = [
+        pltpu.make_async_copy(features_in, grad_features, sem.at[0]),
+        pltpu.make_async_copy(coarse_in, coarse_out, sem.at[1]),
+    ]
     copies[0].start()
-    for n in range(6):
-        coarse[:, n * L : (n + 1) * L] = coarse_in[pl.ds(n, PEERS, stride=8), :].astype(BF16)
-    copies.append(pltpu.make_async_copy(coarse, coarse_out, sem.at[1]))
     copies[1].start()
     lane = lax.broadcasted_iota(jnp.int32, (C, L), 1)
     for k in range(35):
         quad, n = divmod(k, 4)
+        if k % 12 == 0:
+            loads[k // 12].wait()
         if n < 3:
             at = (3 * quad + n) * C
             value = total[at : at + C, :].astype(F32)[:, :C]
@@ -611,9 +668,9 @@
             subm[k] = value
         else:
             down[k - 27] = value
-        if k in (8, 17, 26):
-            part = pl.ds(k - 8, 9)
-            copies.append(pltpu.make_async_copy(subm.at[part], grad_subm.at[part], sem.at[2 + k // 9]))
+        if k in (11, 23, 26):
+            part = pl.ds(k // 12 * 12, 12 if k < 26 else 3)
+            copies.append(pltpu.make_async_copy(subm.at[part], grad_subm.at[part], sem.at[2 + k // 12]))
             copies[-1].start()
     copies.append(pltpu.make_async_copy(down, grad_down, sem.at[5]))
     copies[-1].start()
@@ -630,12 +687,13 @@
             jax.ShapeDtypeStruct((27, C, C), F32),
             jax.ShapeDtypeStruct((8, C, C), F32),
         ),
-        in_specs=vmem(3),
+        in_specs=hbm(3),
         out_specs=tuple(hbm(4)),
         scratch_shapes=[
-            pltpu.VMEM((PEERS, 6 * L), BF16),
+            pltpu.VMEM((27 * C, L), BF16),
             pltpu.VMEM((27, C, C), F32),
             pltpu.VMEM((8, C, C), F32),
+            pltpu.SemaphoreType.DMA((3,)),
             pltpu.SemaphoreType.DMA((6,)),
         ],
         compiler_params=pltpu.CompilerParams(vmem_limit_bytes=VMEM_LIMIT),

time: 65.7 us -> 67.7 us (1.030)
  Pallas kernels: 64.3 us -> 66.3 us
    pallas_call x1, Pallas kernels: 2.65 us -> 10.1 us  [run_final(): pl.pallas_call(final_kernel, out_shape=(jax.ShapeDtypeStruct((PEERS, 6 *...]
    pallas_call x1, Pallas kernels: 61.7 us -> 56.1 us  [run_section(): pl.pallas_call(section_kernel, out_shape=(jax.ShapeDtypeStruct((PEERS, 6...]
where the time goes in v5:
time: 67.7 us; the launch traced here: 67.5 us
  Pallas kernels  66.3 us (98%)
  between operations  1.29 us (2%)
    pallas_call x1, Pallas kernels, run_section(): pl.pallas_call(section_kernel, out_shape=(jax.ShapeDtypeStruct((PEERS, 6...  56.1 us
    pallas_call x1, Pallas kernels, run_final(): pl.pallas_call(final_kernel, out_shape=(jax.ShapeDtypeStruct((PEERS, 6 *...  10.1 us

profile of v5, /device:TPU:1, one launch (start us, length us, event | category | flops | bytes accessed | tf_op | source)
XLA Modules:
  0.0 67.5 jit_solution(12116442989342722492)
XLA Ops:
  1.3 56.1 %shard_map.102 = (bf16[64,768]{1,0:T(8,128)(2,1)}, bf16[2,96,512]{2,1,0:T(8,128)(2,1)}, bf16[2688,128]{1,0:T(8,128)(2,1)}) custom-call(s32[2,27]{1,0:T(2,128)} %table.1, s32[1]{0:T(128)S(6)} %copy.11.live_ref, s32[2,16]{1,0:T(2,128)} %occupancy_ref.1, bf16[2,96,512]{2,1,0:T(8,128)(2,1)} %features_hbm.1, bf16[64,768]{1,0:T(8,128)(2,1)} %cotangent_hbm.1, ...), custom_call_target="tpu_custom_call" | custom-call | tf_op jit(solution)/shard_map/pallas_call | solution.py:583
  57.4 10.1 %shard_map.103 = (bf16[64,768]{1,0:T(8,128)(2,1)}, bf16[2,96,512]{2,1,0:T(8,128)(2,1)}, f32[27,96,96]{2,1,0:T(8,128)}, f32[8,96,96]{2,1,0:T(8,128)}) custom-call(bf16[64,768]{1,0:T(8,128)(2,1)} %get-tuple-element.7.coarse_in, bf16[2,96,512]{2,1,0:T(8,128)(2,1)} %get-tuple-element.8.features_in, bf16[2688,128]{1,0:T(8,128)(2,1)} %get-tuple-element.9.total_in), custom_call_target="tpu_custom_call" | custom-call | tf_op jit(solution)/shard_map/pallas_call | solution.py:682

commit v6 on v5

--- a/solution.py
+++ b/solution.py
@@ -256,37 +256,26 @@
             )
         pre[g * V : (g + 1) * V, :] = acc
 
-    pick = (
-        lax.broadcasted_iota(jnp.int32, (64, 6 * L), 1) % 8
-        == lax.broadcasted_iota(jnp.int32, (64, 6 * L), 0) % 8
-    )
-    piece = lax.broadcasted_iota(jnp.int32, (64, 64), 0) // 8
     live = live_ref[0]
     s, q = 0.7978845608028654, 0.044715
-    down_sums = jnp.zeros((L, 8 * L), F32)
-    dealt = jnp.zeros((PEERS, 6 * L), F32)
-    halves = []
+    slopes, hiddens = [], []
     for g in range(2):
         mask = jnp.broadcast_to(own[g, :, C : C + 1].astype(F32), (V, L))
         tt = pre[g * V : (g + 1) * V, :]
         th = jnp.tanh(s * (tt + q * tt * tt * tt))
-        hidden = (0.5 * tt * (1.0 + th) * mask).astype(BF16)
-        slope = (0.5 * (1.0 + th) + 0.5 * tt * (1.0 - th * th) * (s * (1.0 + 3.0 * q * tt * tt))) * mask
-        both = jnp.dot(
-            perm[...], jnp.concatenate([hidden, mask.astype(BF16)], axis=1),
-            preferred_element_type=F32,
-        )
-        kids = both[:, :L].astype(BF16)
-        cmask = both[:64, L:]
-        coarse = jnp.dot(kids[:64], wd[:L, :], preferred_element_type=F32)
-        for j in range(1, 8):
-            cmask = jnp.maximum(cmask, both[j * 64 : (j + 1) * 64, L:])
-            coarse += jnp.dot(
-                kids[j * 64 : (j + 1) * 64], wd[j * L : (j + 1) * L, :], preferred_element_type=F32
-            )
-        coarse = (coarse * cmask).astype(BF16)
-        flat = jnp.dot(coarse, spread[...], preferred_element_type=F32)
-        halves.append((slope, kids, cmask, jnp.where(pick, flat, 0.0).astype(BF16)))
+        hidden = 0.5 * tt * (1.0 + th) * mask
+        slopes.append((0.5 * (1.0 + th) + 0.5 * tt * (1.0 - th * th) * (s * (1.0 + 3.0 * q * tt * tt))) * mask)
+        hiddens.append(jnp.where(lax.broadcasted_iota(jnp.int32, (V, L), 1) < C, hidden, mask).astype(BF16))
+    both = jnp.dot(perm[...], jnp.concatenate(hiddens, axis=1), preferred_element_type=F32)
+    kids = []
+    cmask = jnp.zeros((2 * 64, L), F32)
+    coarse = jnp.zeros((2 * 64, L), F32)
+    for j in range(8):
+        kid = jnp.concatenate([both[j * 64 : (j + 1) * 64, :L], both[j * 64 : (j + 1) * 64, L:]], axis=0)
+        cmask = jnp.maximum(cmask, kid)
+        kids.append(kid.astype(BF16))
+        coarse += jnp.dot(kids[j], wd[j * L : (j + 1) * L, :], preferred_element_type=F32)
+    cmask = jnp.broadcast_to(cmask[:, C : C + 1], (2 * 64, L))
 
     deal.finish()
     near32[...] = near[...].astype(F32)
@@ -302,43 +291,36 @@
     boxes = jnp.concatenate([lines(n) for n in range(6)], axis=1).astype(BF16)
     below = jnp.where(peers(0, (PEERS, L)) < me, lines(6), 0.0)
     first = jnp.sum(below, axis=0, keepdims=True).astype(jnp.int32)[:, :64]
-    for g in range(2):
-        slope, kids, cmask, flat = halves[g]
-        holder = jnp.bitwise_and(jnp.broadcast_to(first, (64, 64)) + g, 7) * 8 + piece
-        chosen = jnp.where((holder == peers(1, (64, 64))) & (g < live), 1.0, 0.0).astype(BF16)
-        dealt += lax.dot_general(chosen, flat, (((0,), (0,)), ((), ())), preferred_element_type=F32)
-        dz = jnp.dot(chosen, boxes, preferred_element_type=F32)
-        dz = jnp.where(pick, dz, 0.0).astype(BF16)
-        dz = lax.dot_general(dz, spread[...], NT, preferred_element_type=F32)
-        dz = jnp.where(cmask > 0, dz, 0.0)
-        dzt = jnp.transpose(dz).astype(BF16)
-        dz = dz.astype(BF16)
-        down_sums += jnp.dot(
-            dzt, jnp.concatenate([kids[j * 64 : (j + 1) * 64] for j in range(8)], axis=1),
-            preferred_element_type=F32,
-        )
-        dh = jnp.concatenate(
-            [
-                lax.dot_general(dz, wd[j * L : (j + 1) * L, :], NT, preferred_element_type=F32)
-                for j in range(8)
-            ],
-            axis=0,
-        )
-        high = dh.astype(BF16)
-        low = (dh - high.astype(F32)).astype(BF16)
-        dh = lax.dot_general(
-            permt[...], jnp.concatenate([high, low], axis=1), (((1,), (0,)), ((), ())),
-            preferred_element_type=F32,
-        )
-        dpre = slope * (dh[:, :L] + dh[:, L:])
+    row = lax.broadcasted_iota(jnp.int32, (128, 64), 0)
+    block, piece = row >> 6, (row >> 3) & 7
+    holder = jnp.bitwise_and(jnp.broadcast_to(first, (128, 64)) + block, 7) * 8 + piece
+    chosen = jnp.where((holder == peers(1, (128, 64))) & (block < live), 1.0, 0.0).astype(BF16)
+    pick = (
+        lax.broadcasted_iota(jnp.int32, (128, 6 * L), 1) & 7
+        == lax.broadcasted_iota(jnp.int32, (128, 6 * L), 0) & 7
+    )
+    dz = jnp.dot(chosen, boxes, preferred_element_type=F32)
+    dz = jnp.where(pick, dz, 0.0).astype(BF16)
+    dz = lax.dot_general(dz, spread[...], NT, preferred_element_type=F32)
+    dz = jnp.where(cmask > 0, dz, 0.0)
+    dzt = jnp.transpose(dz).astype(BF16)
+    dz = dz.astype(BF16)
+    dh = [
+        lax.dot_general(dz, wd[j * L : (j + 1) * L, :], NT, preferred_element_type=F32) for j in range(8)
+    ]
+    parts = []
+    for g in range(2):
+        part = jnp.concatenate([piece[g * 64 : (g + 1) * 64] for piece in dh], axis=0)
+        high = part.astype(BF16)
+        parts += [high, (part - high.astype(F32)).astype(BF16)]
+    dh = jnp.dot(permt[...], jnp.concatenate(parts, axis=1), preferred_element_type=F32)
+    for g in range(2):
+        dpre = slopes[g] * (dh[:, 2 * g * L : (2 * g + 1) * L] + dh[:, (2 * g + 1) * L : (2 * g + 2) * L])
         dpre16 = dpre.astype(BF16)
         for a in range(3):
             dpre3[g * 640 + a * 64 : g * 640 + a * 64 + V, a * L : (a + 1) * L] = dpre16
         pre[g * V : (g + 1) * V, :] = dpre
-    for n in range(6):
-        box32[box_rows(core, n), :] = dealt[:CHIPS, n * L : (n + 1) * L]
-        box32[box_rows(1 - core, n), :] = dealt[CHIPS:, n * L : (n + 1) * L]
-    back[...] = box32[...].astype(BF16)
+    down_sums = jnp.dot(dzt, jnp.concatenate(kids, axis=1), preferred_element_type=F32)
 
     lane = lax.broadcasted_iota(jnp.int32, (C, L), 1)
     held = {}
@@ -392,6 +374,15 @@
         )
         ysteps[n].start()
 
+    deal_back = Deal(me, back, back_near, back_far, *(back_sem.at[n] for n in range(4)))
+    flat = jnp.dot((coarse * cmask).astype(BF16), spread[...], preferred_element_type=F32)
+    flat = jnp.where(pick, flat, 0.0).astype(BF16)
+    dealt = lax.dot_general(chosen, flat, (((0,), (0,)), ((), ())), preferred_element_type=F32)
+    for n in range(6):
+        box32[box_rows(core, n), :] = dealt[:CHIPS, n * L : (n + 1) * L]
+        box32[box_rows(1 - core, n), :] = dealt[CHIPS:, n * L : (n + 1) * L]
+    back[...] = box32[...].astype(BF16)
+
     gpad[...] = jnp.zeros_like(gpad)
     for bc in range(0, 9, 2):
         width = min(2, 9 - bc)
@@ -428,7 +419,6 @@
         def _():
             copy.start()
 
-    deal_back = Deal(me, back, back_near, back_far, *(back_sem.at[n] for n in range(4)))
     deal_back.start()
 
     gsource[...] = jnp.zeros_like(gsource)
@@ -633,7 +623,7 @@
 
 def final_kernel(
     coarse_in, features_in, total_in, coarse_out, grad_features, grad_subm, grad_down,
-    total, subm, down, load_sem, sem,
+    total, subm, down, coarse, features, load_sem, sem,
 ):
     def chunk(n):
         return pl.ds(9 * C * n, 9 * C)
@@ -641,14 +631,14 @@
     loads = [
         pltpu.make_async_copy(total_in.at[chunk(n)], total.at[chunk(n)], load_sem.at[n]) for n in range(3)
     ]
+    loads.append(pltpu.make_async_copy(features_in, features, load_sem.at[3]))
+    loads.append(pltpu.make_async_copy(coarse_in, coarse, load_sem.at[4]))
     for load in loads:
         load.start()
     copies = [
-        pltpu.make_async_copy(features_in, grad_features, sem.at[0]),
-        pltpu.make_async_copy(coarse_in, coarse_out, sem.at[1]),
+        pltpu.make_async_copy(features, grad_features, sem.at[0]),
+        pltpu.make_async_copy(coarse, coarse_out, sem.at[1]),
     ]
-    copies[0].start()
-    copies[1].start()
     lane = lax.broadcasted_iota(jnp.int32, (C, L), 1)
     for k in range(35):
         quad, n = divmod(k, 4)
@@ -672,6 +662,10 @@
             part = pl.ds(k // 12 * 12, 12 if k < 26 else 3)
             copies.append(pltpu.make_async_copy(subm.at[part], grad_subm.at[part], sem.at[2 + k // 12]))
             copies[-1].start()
+        if k == 11:
+            for n in range(2):
+                loads[3 + n].wait()
+                copies[n].start()
     copies.append(pltpu.make_async_copy(down, grad_down, sem.at[5]))
     copies[-1].start()
     for copy in copies:
@@ -693,7 +687,9 @@
             pltpu.VMEM((27 * C, L), BF16),
             pltpu.VMEM((27, C, C), F32),
             pltpu.VMEM((8, C, C), F32),
-            pltpu.SemaphoreType.DMA((3,)),
+            pltpu.VMEM((PEERS, 6 * L), BF16),
+            pltpu.VMEM((2, C, V), BF16),
+            pltpu.SemaphoreType.DMA((5,)),
             pltpu.SemaphoreType.DMA((6,)),
         ],
         compiler_params=pltpu.CompilerParams(vmem_limit_bytes=VMEM_LIMIT),

time: 67.7 us -> 59.2 us (0.87)
  Pallas kernels: 66.3 us -> 57.8 us
    pallas_call x1, Pallas kernels: 10.1 us -> 2.49 us  [run_final(): pl.pallas_call(final_kernel, out_shape=(jax.ShapeDtypeStruct((PEERS, 6 *...]
    pallas_call x1, Pallas kernels: 56.1 us -> 55.3 us  [run_section(): pl.pallas_call(section_kernel, out_shape=(jax.ShapeDtypeStruct((PEERS, 6...]
where the time goes in v6:
time: 59.2 us; the launch traced here: 59.1 us
  Pallas kernels  57.8 us (98%)
  between operations  1.29 us (2%)
    pallas_call x1, Pallas kernels, run_section(): pl.pallas_call(section_kernel, out_shape=(jax.ShapeDtypeStruct((PEERS, 6...  55.3 us
    pallas_call x1, Pallas kernels, run_final(): pl.pallas_call(final_kernel, out_shape=(jax.ShapeDtypeStruct((PEERS, 6 *...  2.49 us

profile of v6, /device:TPU:1, one launch (start us, length us, event | category | flops | bytes accessed | tf_op | source)
XLA Modules:
  0.0 59.1 jit_solution(8765389570342365685)
XLA Ops:
  1.3 55.3 %shard_map.102 = (bf16[64,768]{1,0:T(8,128)(2,1)}, bf16[2,96,512]{2,1,0:T(8,128)(2,1)}, bf16[2688,128]{1,0:T(8,128)(2,1)}) custom-call(s32[2,27]{1,0:T(2,128)} %table.1, s32[1]{0:T(128)S(6)} %copy.11.live_ref, s32[2,16]{1,0:T(2,128)} %occupancy_ref.1, bf16[2,96,512]{2,1,0:T(8,128)(2,1)} %features_hbm.1, bf16[64,768]{1,0:T(8,128)(2,1)} %cotangent_hbm.1, ...), custom_call_target="tpu_custom_call" | custom-call | tf_op jit(solution)/shard_map/pallas_call | solution.py:573
  56.6 2.5 %shard_map.103 = (bf16[64,768]{1,0:T(8,128)(2,1)}, bf16[2,96,512]{2,1,0:T(8,128)(2,1)}, f32[27,96,96]{2,1,0:T(8,128)}, f32[8,96,96]{2,1,0:T(8,128)}) custom-call(bf16[64,768]{1,0:T(8,128)(2,1)} %get-tuple-element.7.coarse_in, bf16[2,96,512]{2,1,0:T(8,128)(2,1)} %get-tuple-element.8.features_in, bf16[2688,128]{1,0:T(8,128)(2,1)} %get-tuple-element.9.total_in), custom_call_target="tpu_custom_call" | custom-call | tf_op jit(solution)/shard_map/pallas_call | solution.py:676

commit v7 on v6

--- a/solution.py
+++ b/solution.py
@@ -244,7 +244,6 @@
         return carry
 
     lax.fori_loop(0, 20, columns, 0)
-    deal.forward()
 
     for g in range(2):
         acc = jnp.zeros((V, L), F32)
@@ -256,6 +255,7 @@
             )
         pre[g * V : (g + 1) * V, :] = acc
 
+    deal.forward()
     live = live_ref[0]
     s, q = 0.7978845608028654, 0.044715
     slopes, hiddens = [], []
@@ -362,6 +362,15 @@
 
     pair = remote(sums16.at[span((1 - core) * HALF, HALF)], pair_in, pair_sent, pair_arrived, partner)
     pair.start()
+    deal_back = Deal(me, back, back_near, back_far, *(back_sem.at[n] for n in range(4)))
+    flat = jnp.dot((coarse * cmask).astype(BF16), spread[...], preferred_element_type=F32)
+    flat = jnp.where(pick, flat, 0.0).astype(BF16)
+    dealt = lax.dot_general(chosen, flat, (((0,), (0,)), ((), ())), preferred_element_type=F32)
+    for n in range(6):
+        box32[box_rows(core, n), :] = dealt[:CHIPS, n * L : (n + 1) * L]
+        box32[box_rows(1 - core, n), :] = dealt[CHIPS:, n * L : (n + 1) * L]
+    back[...] = box32[...].astype(BF16)
+    deal_back.start()
     pair.wait_recv()
     value = sums32[span(core * HALF, HALF), :] + pair_in[...].astype(F32)
     chip32[...] = value
@@ -374,15 +383,6 @@
         )
         ysteps[n].start()
 
-    deal_back = Deal(me, back, back_near, back_far, *(back_sem.at[n] for n in range(4)))
-    flat = jnp.dot((coarse * cmask).astype(BF16), spread[...], preferred_element_type=F32)
-    flat = jnp.where(pick, flat, 0.0).astype(BF16)
-    dealt = lax.dot_general(chosen, flat, (((0,), (0,)), ((), ())), preferred_element_type=F32)
-    for n in range(6):
-        box32[box_rows(core, n), :] = dealt[:CHIPS, n * L : (n + 1) * L]
-        box32[box_rows(1 - core, n), :] = dealt[CHIPS:, n * L : (n + 1) * L]
-    back[...] = box32[...].astype(BF16)
-
     gpad[...] = jnp.zeros_like(gpad)
     for bc in range(0, 9, 2):
         width = min(2, 9 - bc)
@@ -418,8 +418,6 @@
         @pl.when(wanted)
         def _():
             copy.start()
-
-    deal_back.start()
 
     gsource[...] = jnp.zeros_like(gsource)
     for g in range(2):
@@ -440,17 +438,6 @@
     for g in range(2):
         part_lower[g] = gsource[g * V : (g + 1) * V, :].astype(BF16)
         part_upper[g] = gsource[(4 + g) * V : (5 + g) * V, :].astype(BF16)
-    rim_up = remote(part_upper, from_lower, rim_sent.at[0], rim_arrived.at[0], lax.min(me + 1, PEERS - 1))
-    rim_down = remote(part_lower, from_upper, rim_sent.at[1], rim_arrived.at[1], lax.max(me - 1, 0))
-
-    @pl.when(has_up)
-    def _():
-        rim_up.start()
-
-    @pl.when(has_down)
-    def _():
-        rim_down.start()
-
     def gzstep(n, owner, to):
         at = span(core * HALF + y * YPART + owner * ZPART, ZPART)
         return remote(total.at[at], total.at[at], gzsent.at[n], gzarrived.at[n], device(y, to))
@@ -485,31 +472,17 @@
     for n in range(3):
         gystep(n, y, jnp.bitwise_and(y + n + 1, 3)).start()
     across(0, core, y).start()
+    rim_up = remote(part_upper, from_lower, rim_sent.at[0], rim_arrived.at[0], lax.min(me + 1, PEERS - 1))
+    rim_down = remote(part_lower, from_upper, rim_sent.at[1], rim_arrived.at[1], lax.max(me - 1, 0))
+
+    @pl.when(has_up)
+    def _():
+        rim_up.start()
 
     @pl.when(has_down)
     def _():
-        rim_up.wait_recv()
-
-    @pl.when(jnp.logical_not(has_down))
-    def _():
-        from_lower[...] = jnp.zeros_like(from_lower)
-
-    @pl.when(has_up)
-    def _():
-        rim_down.wait_recv()
-
-    @pl.when(jnp.logical_not(has_up))
-    def _():
-        from_upper[...] = jnp.zeros_like(from_upper)
-
-    for g in range(2):
-        value = gsource[(2 + g) * V : (3 + g) * V, :] + from_lower[g].astype(F32) + from_upper[g].astype(F32)
-        value = value * jnp.broadcast_to(own[g, :, C : C + 1].astype(F32), (V, L))
-        grad_features[g] = jnp.transpose(value)[:C, :].astype(BF16)
-
-    for n in range(3):
-        gystep(n, owners[n + 1], owners[n + 1]).wait_recv()
-        across(n + 1, core, owners[n + 1]).start()
+        rim_down.start()
+
     deal_back.finish()
     near32[...] = back_near[...].astype(F32)
     far32[...] = back_far[...].astype(F32)
@@ -518,6 +491,36 @@
         out32[pl.ds(n * PEERS + 1 - core, CHIPS, stride=2), :] = far32[box_rows(core, n), :]
     for n in range(6):
         coarse_out[:, n * L : (n + 1) * L] = out32[n * PEERS : (n + 1) * PEERS, :].astype(BF16)
+
+    def pass_on(n):
+        gystep(n, owners[n + 1], owners[n + 1]).wait_recv()
+        across(n + 1, core, owners[n + 1]).start()
+
+    pass_on(0)
+    pass_on(2)
+
+    @pl.when(has_down)
+    def _():
+        rim_up.wait_recv()
+
+    @pl.when(jnp.logical_not(has_down))
+    def _():
+        from_lower[...] = jnp.zeros_like(from_lower)
+
+    @pl.when(has_up)
+    def _():
+        rim_down.wait_recv()
+
+    @pl.when(jnp.logical_not(has_up))
+    def _():
+        from_upper[...] = jnp.zeros_like(from_upper)
+
+    for g in range(2):
+        value = gsource[(2 + g) * V : (3 + g) * V, :] + from_lower[g].astype(F32) + from_upper[g].astype(F32)
+        value = value * jnp.broadcast_to(own[g, :, C : C + 1].astype(F32), (V, L))
+        grad_features[g] = jnp.transpose(value)[:C, :].astype(BF16)
+
+    pass_on(1)
     for n in range(4):
         across(n, 1 - core, owners[n]).wait_recv()
 

time: 59.2 us -> 57 us (0.963)
  Pallas kernels: 57.8 us -> 55.6 us
    pallas_call x1, Pallas kernels: 55.3 us -> 53.1 us  [run_section(): pl.pallas_call(section_kernel, out_shape=(jax.ShapeDtypeStruct((PEERS, 6...]
where the time goes in v7:
time: 57 us; the launch traced here: 56.9 us
  Pallas kernels  55.6 us (98%)
  between operations  1.29 us (2%)
    pallas_call x1, Pallas kernels, run_section(): pl.pallas_call(section_kernel, out_shape=(jax.ShapeDtypeStruct((PEERS, 6...  53.1 us
    pallas_call x1, Pallas kernels, run_final(): pl.pallas_call(final_kernel, out_shape=(jax.ShapeDtypeStruct((PEERS, 6 *...  2.49 us

profile of v7, /device:TPU:1, one launch (start us, length us, event | category | flops | bytes accessed | tf_op | source)
XLA Modules:
  0.0 56.9 jit_solution(10104295615269532498)
XLA Ops:
  1.3 53.1 %shard_map.102 = (bf16[64,768]{1,0:T(8,128)(2,1)}, bf16[2,96,512]{2,1,0:T(8,128)(2,1)}, bf16[2688,128]{1,0:T(8,128)(2,1)}) custom-call(s32[2,27]{1,0:T(2,128)} %table.1, s32[1]{0:T(128)S(6)} %copy.11.live_ref, s32[2,16]{1,0:T(2,128)} %occupancy_ref.1, bf16[2,96,512]{2,1,0:T(8,128)(2,1)} %features_hbm.1, bf16[64,768]{1,0:T(8,128)(2,1)} %cotangent_hbm.1, ...), custom_call_target="tpu_custom_call" | custom-call | tf_op jit(solution)/shard_map/pallas_call | solution.py:576
  54.4 2.5 %shard_map.103 = (bf16[64,768]{1,0:T(8,128)(2,1)}, bf16[2,96,512]{2,1,0:T(8,128)(2,1)}, f32[27,96,96]{2,1,0:T(8,128)}, f32[8,96,96]{2,1,0:T(8,128)}) custom-call(bf16[64,768]{1,0:T(8,128)(2,1)} %get-tuple-element.7.coarse_in, bf16[2,96,512]{2,1,0:T(8,128)(2,1)} %get-tuple-element.8.features_in, bf16[2688,128]{1,0:T(8,128)(2,1)} %get-tuple-element.9.total_in), custom_call_target="tpu_custom_call" | custom-call | tf_op jit(solution)/shard_map/pallas_call | solution.py:679

commit v8 on v7

--- a/solution.py
+++ b/solution.py
@@ -9,7 +9,7 @@
 
 C, L, V = 96, 128, 512
 OFFSETS = [(a, b, c) for a in (-1, 0, 1) for b in (-1, 0, 1) for c in (-1, 0, 1)]
-PEERS, CHIPS = 64, 32
+PEERS, CHIPS, SHELL = 64, 32, 320
 HALF, YPART, ZPART = 1344, 336, 48
 VMEM_LIMIT = 63 * 2**20 + 2**19
 F32, BF16 = jnp.float32, jnp.bfloat16
@@ -19,16 +19,39 @@
 def segments(a, b, c):
     span = {-1: [(7, 0)], 0: [(i, i + 1) for i in range(8)], 1: [(0, 9)]}
     xs, ys, zs = span[a], span[b], span[c]
+    face = {0: 0, 7: 64}
     if c == 0:
-        return [(x * 64 + y * 8, 1, tx * 100 + ty * 10 + 1, 1, 8) for x, tx in xs for y, ty in ys]
+        return [
+            (face[x] + y * 8 if x in face else 112 + x * 16 + y // 7 * 8, 1, tx * 100 + ty * 10 + 1, 1, 8)
+            for x, tx in xs
+            for y, ty in ys
+        ]
     z, tz = zs[0]
     if b == 0:
-        return [(x * 64 + z, 8, tx * 100 + 10 + tz, 10, 8) for x, tx in xs]
+        return [
+            (face[x] + z, 8, tx * 100 + 10 + tz, 10, 8)
+            if x in face
+            else (208 + x * 16 + z // 7 * 8, 1, tx * 100 + 10 + tz, 10, 8)
+            for x, tx in xs
+        ]
     y, ty = ys[0]
     if a == 0:
-        return [(y * 8 + z, 64, 100 + ty * 10 + tz, 100, 8)]
+        at = ty * 10 + tz
+        return [
+            (y * 8 + z, 1, 100 + at, 1, 1),
+            (128 + y // 7 * 8 + z, 16, 200 + at, 100, 6),
+            (64 + y * 8 + z, 1, 800 + at, 1, 1),
+        ]
     x, tx = xs[0]
-    return [(x * 64 + y * 8 + z, 1, tx * 100 + ty * 10 + tz, 1, 1)]
+    return [(face[x] + y * 8 + z, 1, tx * 100 + ty * 10 + tz, 1, 1)]
+
+
+def shell_pieces():
+    pieces = [(0, 0, 1, 64), (64, 448, 1, 64)]
+    for x in range(1, 7):
+        pieces += [(112 + x * 16, x * 64, 1, 8), (120 + x * 16, x * 64 + 56, 1, 8)]
+        pieces += [(208 + x * 16, x * 64, 8, 8), (216 + x * 16, x * 64 + 7, 8, 8)]
+    return pieces
 
 
 def rows(start, count, stride):
@@ -48,7 +71,7 @@
     bit = mask_row(words, live, g)
     values = jnp.where(bit > 0, features[g].astype(F32), 0.0)
     marks = jnp.broadcast_to(bit.astype(F32), (L - C, V))
-    return jnp.transpose(jnp.concatenate([values, marks], axis=0)).astype(BF16)
+    return jnp.transpose(jnp.concatenate([values, marks], axis=0))
 
 
 def remote(source, target, sent, arrived, peer):
@@ -122,10 +145,10 @@
 
 
 def section_kernel(
-    table, live_ref, occupancy_ref, features_hbm, cotangent_hbm, w_subm_hbm, w_down_hbm,
+    table_hbm, live_hbm, occupancy_hbm, features_hbm, cotangent_hbm, w_subm_hbm, w_down_hbm,
     coarse_out, grad_features, total,
-    features, cotangent, w_subm, w_down,
-    own, lower, upper, box32, near32, far32, out32, outbox, near, far, back, back_near, back_far,
+    table, live_ref, occupancy_ref, features, cotangent, w_subm, w_down,
+    own32, own, lower, upper, box32, near32, far32, out32, outbox, near, far, back, back_near, back_far,
     source, pad, cols, wf, wb, wd, perm, permt, spread, pre, dpre3, u, gpad, gsource,
     sums32, sums16, pair_in, chip32, chip16, y_in, y32, y16, z_in,
     part_lower, part_upper, from_lower, from_upper,
@@ -140,7 +163,10 @@
     loads = [
         pltpu.make_async_copy(hbm, ref, load_sem.at[n])
         for n, (hbm, ref) in enumerate(
-            ((features_hbm, features), (cotangent_hbm, cotangent), (w_subm_hbm, w_subm), (w_down_hbm, w_down))
+            (
+                (features_hbm, features), (cotangent_hbm, cotangent), (w_subm_hbm, w_subm), (w_down_hbm, w_down),
+                (table_hbm, table), (live_hbm, live_ref), (occupancy_hbm, occupancy_ref),
+            )
         )
     ]
     for load in loads:
@@ -166,11 +192,15 @@
     wb[...] = jnp.zeros_like(wb)
     wd[...] = jnp.zeros_like(wd)
     dpre3[...] = jnp.zeros_like(dpre3)
-    source[6 * V :, :] = jnp.zeros((V, L), F32)
-
-    loads[0].wait()
-    for g in range(2):
-        own[g] = masked_rows(features, occupancy_ref, live_ref[0], g)
+    source[6 * SHELL :, :] = jnp.zeros((SHELL, L), F32)
+
+    for n in (0, 4, 5, 6):
+        loads[n].wait()
+    for g in range(2):
+        own32[g * V : (g + 1) * V, :] = masked_rows(features, occupancy_ref, live_ref[0], g)
+        for s0, v0, vs, count in shell_pieces():
+            source[(2 + g) * SHELL + s0 : (2 + g) * SHELL + s0 + count, :] = own32[rows(g * V + v0, count, vs), :]
+        own[g] = source[(2 + g) * SHELL : (3 + g) * SHELL, :].astype(BF16)
     loads[1].wait()
     for n in range(6):
         box32[pl.ds(n, PEERS, stride=8), :] = cotangent[:, n * L : (n + 1) * L].astype(F32)
@@ -204,8 +234,6 @@
     for j in range(8):
         wd[j * L : j * L + C, :C] = w_down[j]
 
-    for g in range(2):
-        source[(2 + g) * V : (3 + g) * V, :] = own[g].astype(F32)
 
     @pl.when(has_down)
     def _():
@@ -224,14 +252,20 @@
         upper[...] = jnp.zeros_like(upper)
 
     for g in range(2):
-        source[g * V : (g + 1) * V, :] = lower[g].astype(F32)
-        source[(4 + g) * V : (5 + g) * V, :] = upper[g].astype(F32)
+        source[g * SHELL : (g + 1) * SHELL, :] = lower[g].astype(F32)
+        source[(4 + g) * SHELL : (5 + g) * SHELL, :] = upper[g].astype(F32)
 
     for g in range(2):
         for k, offset in enumerate(OFFSETS):
-            base = (2 + g) * V if k == 13 else table[g, k] * V
+            if k == 13:
+                continue
+            base = table[g, k] * SHELL
             for s0, ss, p0, ps, count in segments(*offset):
                 pad[rows(g * 1000 + p0, count, ps), :] = source[rows(base + s0, count, ss), :]
+
+        for x in range(8):
+            for yy in range(8):
+                pad[pl.ds(g * 1000 + x * 100 + yy * 10 + 111, 8), :] = own32[pl.ds(g * V + x * 64 + yy * 8, 8), :]
 
     def columns(gx, carry):
         for b in range(3):
@@ -260,7 +294,7 @@
     s, q = 0.7978845608028654, 0.044715
     slopes, hiddens = [], []
     for g in range(2):
-        mask = jnp.broadcast_to(own[g, :, C : C + 1].astype(F32), (V, L))
+        mask = jnp.broadcast_to(own32[g * V : (g + 1) * V, C : C + 1], (V, L))
         tt = pre[g * V : (g + 1) * V, :]
         th = jnp.tanh(s * (tt + q * tt * tt * tt))
         hidden = 0.5 * tt * (1.0 + th) * mask
@@ -384,7 +418,7 @@
         ysteps[n].start()
 
     gpad[...] = jnp.zeros_like(gpad)
-    for bc in range(0, 9, 2):
+    def pad_gradient(bc):
         width = min(2, 9 - bc)
         u[:, : width * L] = lax.dot_general(
             dpre3[...], wb[bc * L : (bc + width) * L, :], NT, preferred_element_type=F32
@@ -400,6 +434,9 @@
 
         lax.fori_loop(0, 20, add, 0)
 
+    for bc in (0, 2, 4):
+        pad_gradient(bc)
+
     value = chip32[span(y * YPART, YPART), :]
     for n in range(3):
         ysteps[n].wait_recv()
@@ -419,10 +456,10 @@
         def _():
             copy.start()
 
+    for bc in (6, 8):
+        pad_gradient(bc)
+
     gsource[...] = jnp.zeros_like(gsource)
-    for g in range(2):
-        for s0, ss, p0, ps, count in segments(0, 0, 0):
-            gsource[rows((2 + g) * V + s0, count, ss), :] = gpad[rows(g * 1000 + p0, count, ps), :]
 
     def give(n, carry):
         for g in range(2):
@@ -430,14 +467,14 @@
                 if k != 13:
                     here = jnp.where(table[g, k] == n, 1.0, 0.0)
                     for s0, ss, p0, ps, count in segments(*offset):
-                        at = rows(n * V + s0, count, ss)
+                        at = rows(n * SHELL + s0, count, ss)
                         gsource[at, :] += gpad[rows(g * 1000 + p0, count, ps), :] * here
         return carry
 
     lax.fori_loop(0, 6, give, 0)
     for g in range(2):
-        part_lower[g] = gsource[g * V : (g + 1) * V, :].astype(BF16)
-        part_upper[g] = gsource[(4 + g) * V : (5 + g) * V, :].astype(BF16)
+        part_lower[g] = gsource[g * SHELL : (g + 1) * SHELL, :].astype(BF16)
+        part_upper[g] = gsource[(4 + g) * SHELL : (5 + g) * SHELL, :].astype(BF16)
     def gzstep(n, owner, to):
         at = span(core * HALF + y * YPART + owner * ZPART, ZPART)
         return remote(total.at[at], total.at[at], gzsent.at[n], gzarrived.at[n], device(y, to))
@@ -516,8 +553,15 @@
         from_upper[...] = jnp.zeros_like(from_upper)
 
     for g in range(2):
-        value = gsource[(2 + g) * V : (3 + g) * V, :] + from_lower[g].astype(F32) + from_upper[g].astype(F32)
-        value = value * jnp.broadcast_to(own[g, :, C : C + 1].astype(F32), (V, L))
+        shell = gsource[(2 + g) * SHELL : (3 + g) * SHELL, :]
+        shell = shell + from_lower[g].astype(F32) + from_upper[g].astype(F32)
+        for x in range(8):
+            for yy in range(8):
+                pre[pl.ds(g * V + x * 64 + yy * 8, 8), :] = gpad[pl.ds(g * 1000 + x * 100 + yy * 10 + 111, 8), :]
+        for s0, v0, vs, count in shell_pieces():
+            pre[rows(g * V + v0, count, vs), :] += shell[s0 : s0 + count]
+        value = pre[g * V : (g + 1) * V, :]
+        value = value * jnp.broadcast_to(own32[g * V : (g + 1) * V, C : C + 1], (V, L))
         grad_features[g] = jnp.transpose(value)[:C, :].astype(BF16)
 
     pass_on(1)
@@ -556,10 +600,6 @@
         across(n, core, owners[n]).wait_send()
 
 
-def smem():
-    return pl.BlockSpec(memory_space=pltpu.SMEM)
-
-
 def vmem(n):
     return [pl.BlockSpec(memory_space=pltpu.VMEM)] * n
 
@@ -570,7 +610,7 @@
 
 def run_section(neighbours, live_count, occupancy, features, grad_coarse, w_subm, w_down):
     dma = pltpu.SemaphoreType.DMA
-    block = pltpu.VMEM((2, V, L), BF16)
+    block = pltpu.VMEM((2, SHELL, L), BF16)
     boxes = pltpu.VMEM((8 * PEERS, L), F32)
     sent = pltpu.VMEM((8 * PEERS, L), BF16)
     return pl.pallas_call(
@@ -580,16 +620,20 @@
             jax.ShapeDtypeStruct((2, C, V), BF16),
             jax.ShapeDtypeStruct((2 * HALF, L), BF16),
         ),
-        in_specs=[smem(), smem(), smem()] + hbm(4),
+        in_specs=hbm(7),
         out_specs=tuple(vmem(3)),
         scratch_shapes=[
+            pltpu.SMEM((2, 27), jnp.int32),
+            pltpu.SMEM((1,), jnp.int32),
+            pltpu.SMEM((2, 16), jnp.int32),
             pltpu.VMEM((2, C, V), BF16),
             pltpu.VMEM((PEERS, 6 * L), BF16),
             pltpu.VMEM((27, C, C), BF16),
             pltpu.VMEM((8, C, C), BF16),
+            pltpu.VMEM((2 * V, L), F32),
             block, block, block, boxes, boxes, boxes, pltpu.VMEM((6 * PEERS, L), F32),
             sent, sent, sent, sent, sent, sent,
-            pltpu.VMEM((7 * V, L), F32),
+            pltpu.VMEM((7 * SHELL, L), F32),
             pltpu.VMEM((2000, L), F32),
             pltpu.VMEM((1280, 9 * L), BF16),
             pltpu.VMEM((27 * L, L), BF16),
@@ -602,7 +646,7 @@
             pltpu.VMEM((1280, 3 * L), BF16),
             pltpu.VMEM((1280, 2 * L), F32),
             pltpu.VMEM((2000, L), F32),
-            pltpu.VMEM((6 * V, L), F32),
+            pltpu.VMEM((6 * SHELL, L), F32),
             pltpu.VMEM((2 * HALF, L), F32),
             pltpu.VMEM((2 * HALF, L), BF16),
             pltpu.VMEM((HALF, L), BF16),
@@ -613,7 +657,7 @@
             pltpu.VMEM((YPART, L), BF16),
             pltpu.VMEM((7, ZPART, L), BF16),
             block, block, block, block,
-            dma((4,)), dma((4,)), dma((4,)),
+            dma((7,)), dma((4,)), dma((4,)),
             dma((2,)), dma((2,)), dma((2,)), dma((2,)), dma(()), dma(()),
             dma((3,)), dma((3,)), dma((7,)), dma((7,)), dma((7,)), dma((7,)),
             dma((3,)), dma((3,)), dma((4,)), dma((4,)),

time: 57 us -> 54 us (0.947)
  Pallas kernels: 55.6 us -> 52.6 us
    pallas_call x1, Pallas kernels: 53.1 us -> 50.2 us  [run_section(): pl.pallas_call(section_kernel, out_shape=(jax.ShapeDtypeStruct((PEERS, 6...]
where the time goes in v8:
time: 54 us; the launch traced here: 53.9 us
  Pallas kernels  52.6 us (97%)
  between operations  1.29 us (2%)
    pallas_call x1, Pallas kernels, run_section(): pl.pallas_call(section_kernel, out_shape=(jax.ShapeDtypeStruct((PEERS, 6...  50.2 us
    pallas_call x1, Pallas kernels, run_final(): pl.pallas_call(final_kernel, out_shape=(jax.ShapeDtypeStruct((PEERS, 6 *...  2.49 us

profile of v8, /device:TPU:1, one launch (start us, length us, event | category | flops | bytes accessed | tf_op | source)
XLA Modules:
  0.0 53.9 jit_solution(16983920355761750015)
XLA Ops:
  1.3 50.2 %shard_map.102 = (bf16[64,768]{1,0:T(8,128)(2,1)}, bf16[2,96,512]{2,1,0:T(8,128)(2,1)}, bf16[2688,128]{1,0:T(8,128)(2,1)}) custom-call(s32[2,27]{1,0:T(2,128)} %table_hbm.1, s32[1]{0:T(128)S(6)} %copy.11.live_hbm, s32[2,16]{1,0:T(2,128)} %occupancy_hbm.1, bf16[2,96,512]{2,1,0:T(8,128)(2,1)} %features_hbm.1, bf16[64,768]{1,0:T(8,128)(2,1)} %cotangent_hbm.1, ...), custom_call_target="tpu_custom_call" | custom-call | tf_op jit(solution)/shard_map/pallas_call | solution.py:616
  51.4 2.5 %shard_map.103 = (bf16[64,768]{1,0:T(8,128)(2,1)}, bf16[2,96,512]{2,1,0:T(8,128)(2,1)}, f32[27,96,96]{2,1,0:T(8,128)}, f32[8,96,96]{2,1,0:T(8,128)}) custom-call(bf16[64,768]{1,0:T(8,128)(2,1)} %get-tuple-element.7.coarse_in, bf16[2,96,512]{2,1,0:T(8,128)(2,1)} %get-tuple-element.8.features_in, bf16[2688,128]{1,0:T(8,128)(2,1)} %get-tuple-element.9.total_in), custom_call_target="tpu_custom_call" | custom-call | tf_op jit(solution)/shard_map/pallas_call | solution.py:723

commit v9 on v8

--- a/solution.py
+++ b/solution.py
@@ -10,6 +10,7 @@
 C, L, V = 96, 128, 512
 OFFSETS = [(a, b, c) for a in (-1, 0, 1) for b in (-1, 0, 1) for c in (-1, 0, 1)]
 PEERS, CHIPS, SHELL = 64, 32, 320
+YORDER, ZORDER = (1, 0, 2), (3, 2, 4, 1, 5, 0, 6)
 HALF, YPART, ZPART = 1344, 336, 48
 VMEM_LIMIT = 63 * 2**20 + 2**19
 F32, BF16 = jnp.float32, jnp.bfloat16
@@ -81,6 +82,16 @@
     )
 
 
+def far_first():
+    offsets = [(dy, dz) for dy in range(4) for dz in range(8) if dy or dz]
+    return sorted(offsets, key=lambda at: -min(at[0], 4 - at[0]) - min(at[1], 8 - at[1]))
+
+
+def chip_at(here, offset):
+    dy, dz = offset
+    return jnp.bitwise_and(here + 8 * dy, CHIPS - 8) + jnp.bitwise_and(here + dz, 7)
+
+
 def greet(me):
     barrier = pltpu.get_barrier_semaphore()
     here, core = me // 2, lax.rem(me, 2)
@@ -90,14 +101,10 @@
             barrier, inc=1, device_id={"space": peer}, device_id_type=pl.DeviceIdType.MESH
         )
 
+    for offset in far_first():
+        tell(chip_at(here, offset) * 2 + core)
     tell(lax.rem(me + 2 * core - 1 + PEERS, PEERS))
     tell(me + 1 - 2 * core)
-
-    def tell_chip(i, carry):
-        tell(jnp.bitwise_and(here + i, CHIPS - 1) * 2 + core)
-        return carry
-
-    lax.fori_loop(1, CHIPS, tell_chip, 0)
 
 
 def greeted():
@@ -117,15 +124,12 @@
         return pl.ds(pl.multiple_of(chip * 16, 16), 16)
 
     def start(self):
-        def send(i, carry):
-            there = jnp.bitwise_and(self.here + i, CHIPS - 1)
+        for offset in far_first():
+            there = chip_at(self.here, offset)
             remote(
                 self.outbox.at[self.tile(there)], self.near.at[self.tile(self.here)],
                 *self.sems, there * 2 + self.core,
             ).start()
-            return carry
-
-        lax.fori_loop(1, CHIPS, send, 0)
         self.near[self.tile(self.here), :] = self.outbox[self.tile(self.here), :]
 
     def forward(self):
@@ -415,6 +419,8 @@
         ysteps.append(
             remote(chip16.at[span(yy * YPART, YPART)], y_in.at[n], ysent.at[n], yarrived.at[n], device(yy, z))
         )
+
+    for n in YORDER:
         ysteps[n].start()
 
     gpad[...] = jnp.zeros_like(gpad)
@@ -449,7 +455,7 @@
         at = span(lax.min(zz, 6) * ZPART, ZPART)
         return zz < 7, remote(y16.at[at], z_in.at[n], zsent.at[n], zarrived.at[n], device(y, zz))
 
-    for n in range(7):
+    for n in ZORDER:
         wanted, copy = zstep(n)
 
         @pl.when(wanted)
@@ -486,7 +492,7 @@
             zstep(n)[1].wait_recv()
             value = value + z_in[n].astype(F32)
         total[span(core * HALF + y * YPART + z * ZPART, ZPART), :] = value.astype(BF16)
-        for n in range(7):
+        for n in ZORDER:
             gzstep(n, z, jnp.bitwise_and(z + n + 1, 7)).start()
 
     deal_back.forward()
@@ -506,7 +512,7 @@
         return remote(total.at[at], total.at[at], copy_sent.at[n], copy_arrived.at[n], partner)
 
     owners = [jnp.bitwise_and(y + 4 - n, 3) for n in range(4)]
-    for n in range(3):
+    for n in YORDER:
         gystep(n, y, jnp.bitwise_and(y + n + 1, 3)).start()
     across(0, core, y).start()
     rim_up = remote(part_upper, from_lower, rim_sent.at[0], rim_arrived.at[0], lax.min(me + 1, PEERS - 1))

time: 54 us -> 52.8 us (0.978)
  Pallas kernels: 52.6 us -> 51.4 us
    pallas_call x1, Pallas kernels: 50.2 us -> 48.9 us  [run_section(): pl.pallas_call(section_kernel, out_shape=(jax.ShapeDtypeStruct((PEERS, 6...]
where the time goes in v9:
time: 52.8 us; the launch traced here: 52.7 us
  Pallas kernels  51.4 us (97%)
  between operations  1.29 us (2%)
    pallas_call x1, Pallas kernels, run_section(): pl.pallas_call(section_kernel, out_shape=(jax.ShapeDtypeStruct((PEERS, 6...  48.9 us
    pallas_call x1, Pallas kernels, run_final(): pl.pallas_call(final_kernel, out_shape=(jax.ShapeDtypeStruct((PEERS, 6 *...  2.49 us

profile of v9, /device:TPU:1, one launch (start us, length us, event | category | flops | bytes accessed | tf_op | source)
XLA Modules:
  0.0 52.7 jit_solution(17990309571946619914)
XLA Ops:
  1.3 48.9 %shard_map.102 = (bf16[64,768]{1,0:T(8,128)(2,1)}, bf16[2,96,512]{2,1,0:T(8,128)(2,1)}, bf16[2688,128]{1,0:T(8,128)(2,1)}) custom-call(s32[2,27]{1,0:T(2,128)} %table_hbm.1, s32[1]{0:T(128)S(6)} %copy.11.live_hbm, s32[2,16]{1,0:T(2,128)} %occupancy_hbm.1, bf16[2,96,512]{2,1,0:T(8,128)(2,1)} %features_hbm.1, bf16[64,768]{1,0:T(8,128)(2,1)} %cotangent_hbm.1, ...), custom_call_target="tpu_custom_call" | custom-call | tf_op jit(solution)/shard_map/pallas_call | solution.py:622
  50.2 2.5 %shard_map.103 = (bf16[64,768]{1,0:T(8,128)(2,1)}, bf16[2,96,512]{2,1,0:T(8,128)(2,1)}, f32[27,96,96]{2,1,0:T(8,128)}, f32[8,96,96]{2,1,0:T(8,128)}) custom-call(bf16[64,768]{1,0:T(8,128)(2,1)} %get-tuple-element.7.coarse_in, bf16[2,96,512]{2,1,0:T(8,128)(2,1)} %get-tuple-element.8.features_in, bf16[2688,128]{1,0:T(8,128)(2,1)} %get-tuple-element.9.total_in), custom_call_target="tpu_custom_call" | custom-call | tf_op jit(solution)/shard_map/pallas_call | solution.py:729

commit v10 on v9

--- a/solution.py
+++ b/solution.py
@@ -11,7 +11,7 @@
 OFFSETS = [(a, b, c) for a in (-1, 0, 1) for b in (-1, 0, 1) for c in (-1, 0, 1)]
 PEERS, CHIPS, SHELL = 64, 32, 320
 YORDER, ZORDER = (1, 0, 2), (3, 2, 4, 1, 5, 0, 6)
-HALF, YPART, ZPART = 1344, 336, 48
+HALF, YPART, ZPART, OWNED = 1344, 336, 192, 48
 VMEM_LIMIT = 63 * 2**20 + 2**19
 F32, BF16 = jnp.float32, jnp.bfloat16
 NT = (((1,), (1,)), ((), ()))
@@ -154,7 +154,7 @@
     table, live_ref, occupancy_ref, features, cotangent, w_subm, w_down,
     own32, own, lower, upper, box32, near32, far32, out32, outbox, near, far, back, back_near, back_far,
     source, pad, cols, wf, wb, wd, perm, permt, spread, pre, dpre3, u, gpad, gsource,
-    sums32, sums16, pair_in, chip32, chip16, y_in, y32, y16, z_in,
+    sums32, sums16, pair_in, chip32, chip16, y_in, y32, y16, z_own, z_in, z32, z16, y_own,
     part_lower, part_upper, from_lower, from_upper,
     load_sem, box_sem, back_sem, halo_sent, halo_arrived,
     rim_sent, rim_arrived, pair_sent, pair_arrived, ysent, yarrived, zsent, zarrived,
@@ -395,9 +395,6 @@
     def span(at, count):
         return pl.ds(pl.multiple_of(at, 16), count)
 
-    def device(yy, zz):
-        return yy * 16 + zz * 2 + core
-
     pair = remote(sums16.at[span((1 - core) * HALF, HALF)], pair_in, pair_sent, pair_arrived, partner)
     pair.start()
     deal_back = Deal(me, back, back_near, back_far, *(back_sem.at[n] for n in range(4)))
@@ -413,15 +410,92 @@
     value = sums32[span(core * HALF, HALF), :] + pair_in[...].astype(F32)
     chip32[...] = value
     chip16[...] = value.astype(BF16)
-    ysteps = []
-    for n in range(3):
-        yy = jnp.bitwise_and(y + n + 1, 3)
-        ysteps.append(
-            remote(chip16.at[span(yy * YPART, YPART)], y_in.at[n], ysent.at[n], yarrived.at[n], device(yy, z))
-        )
-
-    for n in YORDER:
-        ysteps[n].start()
+
+    on_y, on_z, owner = core == 0, core == 1, z < 7
+
+    def copies(order, place, size, step, wanted=None):
+        def act(what, back=False):
+            for n in order:
+                to = jnp.bitwise_and(place + (size - n - 1 if back else n + 1), size - 1)
+                copy = step(n, to)
+                if wanted is None:
+                    what(copy)
+                else:
+                    pl.when(wanted(to))(functools.partial(what, copy))
+
+        return act
+
+    def start(copy):
+        copy.start()
+
+    def wait_recv(copy):
+        copy.wait_recv()
+
+    def wait_send(copy):
+        copy.wait_send()
+
+    def owns(zz):
+        return zz < 7
+
+    def low(zz):
+        return lax.min(zz, 6)
+
+    def y_first(n, yy):
+        return remote(
+            chip16.at[span(yy * YPART, YPART)], y_in.at[n], ysent.at[n], yarrived.at[n], yy * 16 + z * 2
+        )
+
+    def z_second(n, zz):
+        return remote(
+            y16.at[span(low(zz) * OWNED, OWNED)], z_own.at[n], zsent.at[n], zarrived.at[n], y * 16 + zz * 2
+        )
+
+    def z_first(n, zz):
+        return remote(
+            chip16.at[span(low(zz) * ZPART, ZPART)], z_in.at[n], zsent.at[n], zarrived.at[n],
+            y * 16 + zz * 2 + 1,
+        )
+
+    def y_second(n, yy):
+        return remote(
+            z16.at[span(yy * OWNED, OWNED)], y_own.at[n], ysent.at[n], yarrived.at[n], yy * 16 + z * 2 + 1
+        )
+
+    def on_total(at, count, sent, arrived, peer):
+        at = span(at, count)
+        return remote(total.at[at], total.at[at], sent, arrived, peer)
+
+    def back_z_first(n, to, source):
+        return on_total(
+            y * YPART + low(source) * OWNED, OWNED, gzsent.at[n], gzarrived.at[n], y * 16 + to * 2
+        )
+
+    def back_y_second(n, to, source):
+        return on_total(source * YPART, YPART, gysent.at[n], gyarrived.at[n], to * 16 + z * 2)
+
+    def back_y_first(n, to, source):
+        return on_total(
+            HALF + low(z) * ZPART + source * OWNED, OWNED, gysent.at[n], gyarrived.at[n], to * 16 + z * 2 + 1
+        )
+
+    def back_z_second(n, to, source):
+        return on_total(
+            HALF + low(source) * ZPART, ZPART, gzsent.at[n], gzarrived.at[n], y * 16 + to * 2 + 1
+        )
+
+    def sends(step, mine):
+        return lambda n, to: step(n, to, mine)
+
+    def comes(step):
+        return lambda n, source: step(n, source, source)
+
+    @pl.when(on_y)
+    def _():
+        copies(YORDER, y, 4, y_first)(start)
+
+    @pl.when(on_z)
+    def _():
+        copies(ZORDER, z, 8, z_first, owns)(start)
 
     gpad[...] = jnp.zeros_like(gpad)
     def pad_gradient(bc):
@@ -440,30 +514,30 @@
 
         lax.fori_loop(0, 20, add, 0)
 
-    for bc in (0, 2, 4):
+    for bc in (0, 2, 4, 6):
         pad_gradient(bc)
 
-    value = chip32[span(y * YPART, YPART), :]
-    for n in range(3):
-        ysteps[n].wait_recv()
-        value = value + y_in[n].astype(F32)
-    y32[...] = value
-    y16[...] = value.astype(BF16)
-
-    def zstep(n):
-        zz = jnp.bitwise_and(z + n + 1, 7)
-        at = span(lax.min(zz, 6) * ZPART, ZPART)
-        return zz < 7, remote(y16.at[at], z_in.at[n], zsent.at[n], zarrived.at[n], device(y, zz))
-
-    for n in ZORDER:
-        wanted, copy = zstep(n)
-
-        @pl.when(wanted)
-        def _():
-            copy.start()
-
-    for bc in (6, 8):
-        pad_gradient(bc)
+    @pl.when(on_y)
+    def _():
+        copies(range(3), y, 4, y_first)(wait_recv)
+        value = chip32[span(y * YPART, YPART), :]
+        for n in range(3):
+            value = value + y_in[n].astype(F32)
+        y32[...] = value
+        y16[...] = value.astype(BF16)
+        copies(ZORDER, z, 8, z_second, owns)(start)
+
+    @pl.when(on_z & owner)
+    def _():
+        copies(range(7), z, 8, z_first)(wait_recv)
+        value = chip32[span(z * ZPART, ZPART), :]
+        for n in range(7):
+            value = value + z_in[n].astype(F32)
+        z32[...] = value
+        z16[...] = value.astype(BF16)
+        copies(YORDER, y, 4, y_second)(start)
+
+    pad_gradient(8)
 
     gsource[...] = jnp.zeros_like(gsource)
 
@@ -481,40 +555,24 @@
     for g in range(2):
         part_lower[g] = gsource[g * SHELL : (g + 1) * SHELL, :].astype(BF16)
         part_upper[g] = gsource[(4 + g) * SHELL : (5 + g) * SHELL, :].astype(BF16)
-    def gzstep(n, owner, to):
-        at = span(core * HALF + y * YPART + owner * ZPART, ZPART)
-        return remote(total.at[at], total.at[at], gzsent.at[n], gzarrived.at[n], device(y, to))
-
-    @pl.when(z < 7)
-    def _():
-        value = y32[span(z * ZPART, ZPART), :]
+    @pl.when(on_y & owner)
+    def _():
+        copies(range(7), z, 8, z_second)(wait_recv)
+        value = y32[span(z * OWNED, OWNED), :]
         for n in range(7):
-            zstep(n)[1].wait_recv()
-            value = value + z_in[n].astype(F32)
-        total[span(core * HALF + y * YPART + z * ZPART, ZPART), :] = value.astype(BF16)
-        for n in ZORDER:
-            gzstep(n, z, jnp.bitwise_and(z + n + 1, 7)).start()
-
-    deal_back.forward()
-    for n in range(7):
-        owner = jnp.bitwise_and(z + 7 - n, 7)
-
-        @pl.when(owner < 7)
-        def _():
-            gzstep(n, lax.min(owner, 6), owner).wait_recv()
-
-    def gystep(n, owner, to):
-        at = span(core * HALF + owner * YPART, YPART)
-        return remote(total.at[at], total.at[at], gysent.at[n], gyarrived.at[n], device(to, z))
-
-    def across(n, which, owner):
-        at = span(which * HALF + owner * YPART, YPART)
-        return remote(total.at[at], total.at[at], copy_sent.at[n], copy_arrived.at[n], partner)
-
-    owners = [jnp.bitwise_and(y + 4 - n, 3) for n in range(4)]
-    for n in YORDER:
-        gystep(n, y, jnp.bitwise_and(y + n + 1, 3)).start()
-    across(0, core, y).start()
+            value = value + z_own[n].astype(F32)
+        total[span(y * YPART + z * OWNED, OWNED), :] = value.astype(BF16)
+        copies(ZORDER, z, 8, sends(back_z_first, z))(start)
+
+    @pl.when(on_z & owner)
+    def _():
+        copies(range(3), y, 4, y_second)(wait_recv)
+        value = z32[span(y * OWNED, OWNED), :]
+        for n in range(3):
+            value = value + y_own[n].astype(F32)
+        total[span(HALF + z * ZPART + y * OWNED, OWNED), :] = value.astype(BF16)
+        copies(YORDER, y, 4, sends(back_y_first, y))(start)
+
     rim_up = remote(part_upper, from_lower, rim_sent.at[0], rim_arrived.at[0], lax.min(me + 1, PEERS - 1))
     rim_down = remote(part_lower, from_upper, rim_sent.at[1], rim_arrived.at[1], lax.max(me - 1, 0))
 
@@ -525,6 +583,24 @@
     @pl.when(has_down)
     def _():
         rim_down.start()
+
+    deal_back.forward()
+
+    def across(which, part):
+        rows_at, count = (part * YPART, YPART) if which == 0 else (HALF + part * ZPART, ZPART)
+        return on_total(rows_at, count, copy_sent.at[part], copy_arrived.at[part], partner)
+
+    @pl.when(on_y)
+    def _():
+        copies(range(7), z, 8, comes(back_z_first), owns)(wait_recv, back=True)
+        copies(YORDER, y, 4, sends(back_y_second, y))(start)
+        across(0, y).start()
+
+    @pl.when(on_z & owner)
+    def _():
+        copies(range(3), y, 4, comes(back_y_first))(wait_recv, back=True)
+        copies(ZORDER, z, 8, sends(back_z_second, z))(start)
+        across(1, z).start()
 
     deal_back.finish()
     near32[...] = back_near[...].astype(F32)
@@ -535,12 +611,28 @@
     for n in range(6):
         coarse_out[:, n * L : (n + 1) * L] = out32[n * PEERS : (n + 1) * PEERS, :].astype(BF16)
 
-    def pass_on(n):
-        gystep(n, owners[n + 1], owners[n + 1]).wait_recv()
-        across(n + 1, core, owners[n + 1]).start()
-
-    pass_on(0)
-    pass_on(2)
+    def pass_on_y(n):
+        source = jnp.bitwise_and(y + 3 - n, 3)
+        back_y_second(n, source, source).wait_recv()
+        across(0, source).start()
+
+    def pass_on_z(n):
+        source = jnp.bitwise_and(z + 7 - n, 7)
+
+        @pl.when(owns(source))
+        def _():
+            back_z_second(n, source, source).wait_recv()
+            across(1, low(source)).start()
+
+    @pl.when(on_y)
+    def _():
+        pass_on_y(0)
+        pass_on_y(2)
+
+    @pl.when(on_z)
+    def _():
+        for n in (0, 6, 1, 5):
+            pass_on_z(n)
 
     @pl.when(has_down)
     def _():
@@ -570,9 +662,18 @@
         value = value * jnp.broadcast_to(own32[g * V : (g + 1) * V, C : C + 1], (V, L))
         grad_features[g] = jnp.transpose(value)[:C, :].astype(BF16)
 
-    pass_on(1)
-    for n in range(4):
-        across(n, 1 - core, owners[n]).wait_recv()
+    @pl.when(on_y)
+    def _():
+        pass_on_y(1)
+        for part in range(7):
+            across(1, part).wait_recv()
+
+    @pl.when(on_z)
+    def _():
+        for n in (2, 4, 3):
+            pass_on_z(n)
+        for part in range(4):
+            across(0, part).wait_recv()
 
     @pl.when(has_up)
     def _():
@@ -587,23 +688,30 @@
     deal.close()
     deal_back.close()
     pair.wait_send()
-    for n in range(3):
-        ysteps[n].wait_send()
-        gystep(n, y, jnp.bitwise_and(y + n + 1, 3)).wait_send()
-    for n in range(7):
-        wanted, copy = zstep(n)
-
-        @pl.when(wanted)
-        def _():
-            copy.wait_send()
-
-    @pl.when(z < 7)
-    def _():
-        for n in range(7):
-            gzstep(n, z, jnp.bitwise_and(z + n + 1, 7)).wait_send()
-
-    for n in range(4):
-        across(n, core, owners[n]).wait_send()
+
+    @pl.when(on_y)
+    def _():
+        copies(range(3), y, 4, y_first)(wait_send)
+        copies(range(7), z, 8, z_second, owns)(wait_send)
+        copies(range(3), y, 4, sends(back_y_second, y))(wait_send)
+        for part in range(4):
+            across(0, part).wait_send()
+
+    @pl.when(on_z)
+    def _():
+        copies(range(7), z, 8, z_first, owns)(wait_send)
+        for part in range(7):
+            across(1, part).wait_send()
+
+    @pl.when(on_y & owner)
+    def _():
+        copies(range(7), z, 8, sends(back_z_first, z))(wait_send)
+
+    @pl.when(on_z & owner)
+    def _():
+        copies(range(3), y, 4, y_second)(wait_send)
+        copies(range(3), y, 4, sends(back_y_first, y))(wait_send)
+        copies(range(7), z, 8, sends(back_z_second, z))(wait_send)
 
 
 def vmem(n):
@@ -661,12 +769,16 @@
             pltpu.VMEM((3, YPART, L), BF16),
             pltpu.VMEM((YPART, L), F32),
             pltpu.VMEM((YPART, L), BF16),
+            pltpu.VMEM((7, OWNED, L), BF16),
             pltpu.VMEM((7, ZPART, L), BF16),
+            pltpu.VMEM((ZPART, L), F32),
+            pltpu.VMEM((ZPART, L), BF16),
+            pltpu.VMEM((3, OWNED, L), BF16),
             block, block, block, block,
             dma((7,)), dma((4,)), dma((4,)),
             dma((2,)), dma((2,)), dma((2,)), dma((2,)), dma(()), dma(()),
             dma((3,)), dma((3,)), dma((7,)), dma((7,)), dma((7,)), dma((7,)),
-            dma((3,)), dma((3,)), dma((4,)), dma((4,)),
+            dma((3,)), dma((3,)), dma((7,)), dma((7,)),
         ],
         compiler_params=pltpu.CompilerParams(
             vmem_limit_bytes=VMEM_LIMIT, collective_id=0, has_side_effects=True

time: 52.8 us -> 51.1 us (0.968)
  Pallas kernels: 51.4 us -> 49.7 us
    pallas_call x1, Pallas kernels: 48.9 us -> 47.2 us  [run_section(): pl.pallas_call(section_kernel, out_shape=(jax.ShapeDtypeStruct((PEERS, 6...]
where the time goes in v10:
time: 51.1 us; the launch traced here: 51 us
  Pallas kernels  49.7 us (97%)
  between operations  1.29 us (3%)
    pallas_call x1, Pallas kernels, run_section(): pl.pallas_call(section_kernel, out_shape=(jax.ShapeDtypeStruct((PEERS, 6...  47.2 us
    pallas_call x1, Pallas kernels, run_final(): pl.pallas_call(final_kernel, out_shape=(jax.ShapeDtypeStruct((PEERS, 6 *...  2.49 us

profile of v10, /device:TPU:1, one launch (start us, length us, event | category | flops | bytes accessed | tf_op | source)
XLA Modules:
  0.0 51.0 jit_solution(9429132350345696364)
XLA Ops:
  1.3 47.2 %shard_map.102 = (bf16[64,768]{1,0:T(8,128)(2,1)}, bf16[2,96,512]{2,1,0:T(8,128)(2,1)}, bf16[2688,128]{1,0:T(8,128)(2,1)}) custom-call(s32[2,27]{1,0:T(2,128)} %table_hbm.1, s32[1]{0:T(128)S(6)} %copy.11.live_hbm, s32[2,16]{1,0:T(2,128)} %occupancy_hbm.1, bf16[2,96,512]{2,1,0:T(8,128)(2,1)} %features_hbm.1, bf16[64,768]{1,0:T(8,128)(2,1)} %cotangent_hbm.1, ...), custom_call_target="tpu_custom_call" | custom-call | tf_op jit(solution)/shard_map/pallas_call | solution.py:730
  48.5 2.5 %shard_map.103 = (bf16[64,768]{1,0:T(8,128)(2,1)}, bf16[2,96,512]{2,1,0:T(8,128)(2,1)}, f32[27,96,96]{2,1,0:T(8,128)}, f32[8,96,96]{2,1,0:T(8,128)}) custom-call(bf16[64,768]{1,0:T(8,128)(2,1)} %get-tuple-element.7.coarse_in, bf16[2,96,512]{2,1,0:T(8,128)(2,1)} %get-tuple-element.8.features_in, bf16[2688,128]{1,0:T(8,128)(2,1)} %get-tuple-element.9.total_in), custom_call_target="tpu_custom_call" | custom-call | tf_op jit(solution)/shard_map/pallas_call | solution.py:841

commit v11 on v10

--- a/solution.py
+++ b/solution.py
@@ -11,7 +11,7 @@
 OFFSETS = [(a, b, c) for a in (-1, 0, 1) for b in (-1, 0, 1) for c in (-1, 0, 1)]
 PEERS, CHIPS, SHELL = 64, 32, 320
 YORDER, ZORDER = (1, 0, 2), (3, 2, 4, 1, 5, 0, 6)
-HALF, YPART, ZPART, OWNED = 1344, 336, 192, 48
+SUMS, SPLIT, YPART, ZPART, YOWNED, ZOWNED = 2688, 1792, 448, 128, 64, 32
 VMEM_LIMIT = 63 * 2**20 + 2**19
 F32, BF16 = jnp.float32, jnp.bfloat16
 NT = (((1,), (1,)), ((), ()))
@@ -395,8 +395,23 @@
     def span(at, count):
         return pl.ds(pl.multiple_of(at, 16), count)
 
-    pair = remote(sums16.at[span((1 - core) * HALF, HALF)], pair_in, pair_sent, pair_arrived, partner)
-    pair.start()
+    on_y, on_z, owner = core == 0, core == 1, z < 7
+    pair_y = remote(
+        sums16.at[pl.ds(0, SPLIT)], pair_in, pair_sent, pair_arrived, partner
+    )
+    pair_z = remote(
+        sums16.at[pl.ds(SPLIT, SUMS - SPLIT)], pair_in.at[pl.ds(0, SUMS - SPLIT)], pair_sent, pair_arrived,
+        partner,
+    )
+
+    @pl.when(on_y)
+    def _():
+        pair_z.start()
+
+    @pl.when(on_z)
+    def _():
+        pair_y.start()
+
     deal_back = Deal(me, back, back_near, back_far, *(back_sem.at[n] for n in range(4)))
     flat = jnp.dot((coarse * cmask).astype(BF16), spread[...], preferred_element_type=F32)
     flat = jnp.where(pick, flat, 0.0).astype(BF16)
@@ -406,12 +421,20 @@
         box32[box_rows(1 - core, n), :] = dealt[CHIPS:, n * L : (n + 1) * L]
     back[...] = box32[...].astype(BF16)
     deal_back.start()
-    pair.wait_recv()
-    value = sums32[span(core * HALF, HALF), :] + pair_in[...].astype(F32)
-    chip32[...] = value
-    chip16[...] = value.astype(BF16)
-
-    on_y, on_z, owner = core == 0, core == 1, z < 7
+    def add_pair(copy, at, count):
+        copy.wait_recv()
+        value = sums32[at : at + count, :] + pair_in[:count].astype(F32)
+        chip32[:count] = value
+        chip16[:count] = value.astype(BF16)
+
+    @pl.when(on_y)
+    def _():
+        add_pair(pair_y, 0, SPLIT)
+
+    @pl.when(on_z)
+    def _():
+        add_pair(pair_z, SPLIT, SUMS - SPLIT)
+
 
     def copies(order, place, size, step, wanted=None):
         def act(what, back=False):
@@ -447,7 +470,7 @@
 
     def z_second(n, zz):
         return remote(
-            y16.at[span(low(zz) * OWNED, OWNED)], z_own.at[n], zsent.at[n], zarrived.at[n], y * 16 + zz * 2
+            y16.at[span(low(zz) * YOWNED, YOWNED)], z_own.at[n], zsent.at[n], zarrived.at[n], y * 16 + zz * 2
         )
 
     def z_first(n, zz):
@@ -458,7 +481,7 @@
 
     def y_second(n, yy):
         return remote(
-            z16.at[span(yy * OWNED, OWNED)], y_own.at[n], ysent.at[n], yarrived.at[n], yy * 16 + z * 2 + 1
+            z16.at[span(yy * ZOWNED, ZOWNED)], y_own.at[n], ysent.at[n], yarrived.at[n], yy * 16 + z * 2 + 1
         )
 
     def on_total(at, count, sent, arrived, peer):
@@ -467,7 +490,7 @@
 
     def back_z_first(n, to, source):
         return on_total(
-            y * YPART + low(source) * OWNED, OWNED, gzsent.at[n], gzarrived.at[n], y * 16 + to * 2
+            y * YPART + low(source) * YOWNED, YOWNED, gzsent.at[n], gzarrived.at[n], y * 16 + to * 2
         )
 
     def back_y_second(n, to, source):
@@ -475,12 +498,12 @@
 
     def back_y_first(n, to, source):
         return on_total(
-            HALF + low(z) * ZPART + source * OWNED, OWNED, gysent.at[n], gyarrived.at[n], to * 16 + z * 2 + 1
+            SPLIT + low(z) * ZPART + source * ZOWNED, ZOWNED, gysent.at[n], gyarrived.at[n], to * 16 + z * 2 + 1
         )
 
     def back_z_second(n, to, source):
         return on_total(
-            HALF + low(source) * ZPART, ZPART, gzsent.at[n], gzarrived.at[n], y * 16 + to * 2 + 1
+            SPLIT + low(source) * ZPART, ZPART, gzsent.at[n], gzarrived.at[n], y * 16 + to * 2 + 1
         )
 
     def sends(step, mine):
@@ -558,19 +581,19 @@
     @pl.when(on_y & owner)
     def _():
         copies(range(7), z, 8, z_second)(wait_recv)
-        value = y32[span(z * OWNED, OWNED), :]
+        value = y32[span(z * YOWNED, YOWNED), :]
         for n in range(7):
             value = value + z_own[n].astype(F32)
-        total[span(y * YPART + z * OWNED, OWNED), :] = value.astype(BF16)
+        total[span(y * YPART + z * YOWNED, YOWNED), :] = value.astype(BF16)
         copies(ZORDER, z, 8, sends(back_z_first, z))(start)
 
     @pl.when(on_z & owner)
     def _():
         copies(range(3), y, 4, y_second)(wait_recv)
-        value = z32[span(y * OWNED, OWNED), :]
+        value = z32[span(y * ZOWNED, ZOWNED), :]
         for n in range(3):
             value = value + y_own[n].astype(F32)
-        total[span(HALF + z * ZPART + y * OWNED, OWNED), :] = value.astype(BF16)
+        total[span(SPLIT + z * ZPART + y * ZOWNED, ZOWNED), :] = value.astype(BF16)
         copies(YORDER, y, 4, sends(back_y_first, y))(start)
 
     rim_up = remote(part_upper, from_lower, rim_sent.at[0], rim_arrived.at[0], lax.min(me + 1, PEERS - 1))
@@ -587,7 +610,7 @@
     deal_back.forward()
 
     def across(which, part):
-        rows_at, count = (part * YPART, YPART) if which == 0 else (HALF + part * ZPART, ZPART)
+        rows_at, count = (part * YPART, YPART) if which == 0 else (SPLIT + part * ZPART, ZPART)
         return on_total(rows_at, count, copy_sent.at[part], copy_arrived.at[part], partner)
 
     @pl.when(on_y)
@@ -687,10 +710,9 @@
 
     deal.close()
     deal_back.close()
-    pair.wait_send()
-
     @pl.when(on_y)
     def _():
+        pair_z.wait_send()
         copies(range(3), y, 4, y_first)(wait_send)
         copies(range(7), z, 8, z_second, owns)(wait_send)
         copies(range(3), y, 4, sends(back_y_second, y))(wait_send)
@@ -699,6 +721,7 @@
 
     @pl.when(on_z)
     def _():
+        pair_y.wait_send()
         copies(range(7), z, 8, z_first, owns)(wait_send)
         for part in range(7):
             across(1, part).wait_send()
@@ -732,7 +755,7 @@
         out_shape=(
             jax.ShapeDtypeStruct((PEERS, 6 * L), BF16),
             jax.ShapeDtypeStruct((2, C, V), BF16),
-            jax.ShapeDtypeStruct((2 * HALF, L), BF16),
+            jax.ShapeDtypeStruct((SUMS, L), BF16),
         ),
         in_specs=hbm(7),
         out_specs=tuple(vmem(3)),
@@ -761,19 +784,19 @@
             pltpu.VMEM((1280, 2 * L), F32),
             pltpu.VMEM((2000, L), F32),
             pltpu.VMEM((6 * SHELL, L), F32),
-            pltpu.VMEM((2 * HALF, L), F32),
-            pltpu.VMEM((2 * HALF, L), BF16),
-            pltpu.VMEM((HALF, L), BF16),
-            pltpu.VMEM((HALF, L), F32),
-            pltpu.VMEM((HALF, L), BF16),
+            pltpu.VMEM((SUMS, L), F32),
+            pltpu.VMEM((SUMS, L), BF16),
+            pltpu.VMEM((SPLIT, L), BF16),
+            pltpu.VMEM((SPLIT, L), F32),
+            pltpu.VMEM((SPLIT, L), BF16),
             pltpu.VMEM((3, YPART, L), BF16),
             pltpu.VMEM((YPART, L), F32),
             pltpu.VMEM((YPART, L), BF16),
-            pltpu.VMEM((7, OWNED, L), BF16),
+            pltpu.VMEM((7, YOWNED, L), BF16),
             pltpu.VMEM((7, ZPART, L), BF16),
             pltpu.VMEM((ZPART, L), F32),
             pltpu.VMEM((ZPART, L), BF16),
-            pltpu.VMEM((3, OWNED, L), BF16),
+            pltpu.VMEM((3, ZOWNED, L), BF16),
             block, block, block, block,
             dma((7,)), dma((4,)), dma((4,)),
             dma((2,)), dma((2,)), dma((2,)), dma((2,)), dma(()), dma(()),

time: 51.1 us -> 52.8 us (1.033)
  Pallas kernels: 49.7 us -> 51.3 us
    pallas_call x1, Pallas kernels: 47.2 us -> 48.8 us  [run_section(): pl.pallas_call(section_kernel, out_shape=(jax.ShapeDtypeStruct((PEERS, 6...]
where the time goes in v11:
time: 52.8 us; the launch traced here: 52.6 us
  Pallas kernels  51.3 us (97%)
  between operations  1.29 us (2%)
    pallas_call x1, Pallas kernels, run_section(): pl.pallas_call(section_kernel, out_shape=(jax.ShapeDtypeStruct((PEERS, 6...  48.8 us
    pallas_call x1, Pallas kernels, run_final(): pl.pallas_call(final_kernel, out_shape=(jax.ShapeDtypeStruct((PEERS, 6 *...  2.49 us

profile of v11, /device:TPU:1, one launch (start us, length us, event | category | flops | bytes accessed | tf_op | source)
XLA Modules:
  0.0 52.6 jit_solution(6696846681017616207)
XLA Ops:
  1.3 48.8 %shard_map.102 = (bf16[64,768]{1,0:T(8,128)(2,1)}, bf16[2,96,512]{2,1,0:T(8,128)(2,1)}, bf16[2688,128]{1,0:T(8,128)(2,1)}) custom-call(s32[2,27]{1,0:T(2,128)} %table_hbm.1, s32[1]{0:T(128)S(6)} %copy.11.live_hbm, s32[2,16]{1,0:T(2,128)} %occupancy_hbm.1, bf16[2,96,512]{2,1,0:T(8,128)(2,1)} %features_hbm.1, bf16[64,768]{1,0:T(8,128)(2,1)} %cotangent_hbm.1, ...), custom_call_target="tpu_custom_call" | custom-call | tf_op jit(solution)/shard_map/pallas_call | solution.py:753
  50.1 2.5 %shard_map.103 = (bf16[64,768]{1,0:T(8,128)(2,1)}, bf16[2,96,512]{2,1,0:T(8,128)(2,1)}, f32[27,96,96]{2,1,0:T(8,128)}, f32[8,96,96]{2,1,0:T(8,128)}) custom-call(bf16[64,768]{1,0:T(8,128)(2,1)} %get-tuple-element.7.coarse_in, bf16[2,96,512]{2,1,0:T(8,128)(2,1)} %get-tuple-element.8.features_in, bf16[2688,128]{1,0:T(8,128)(2,1)} %get-tuple-element.9.total_in), custom_call_target="tpu_custom_call" | custom-call | tf_op jit(solution)/shard_map/pallas_call | solution.py:864

commit v12 on v10

--- a/solution.py
+++ b/solution.py
@@ -397,6 +397,137 @@
 
     pair = remote(sums16.at[span((1 - core) * HALF, HALF)], pair_in, pair_sent, pair_arrived, partner)
     pair.start()
+    pair.wait_recv()
+    value = sums32[span(core * HALF, HALF), :] + pair_in[...].astype(F32)
+    chip32[...] = value
+    chip16[...] = value.astype(BF16)
+
+    on_y, on_z, owner = core == 0, core == 1, z < 7
+
+    def copies(order, place, size, step, wanted=None):
+        def act(what, back=False):
+            for n in order:
+                to = jnp.bitwise_and(place + (size - n - 1 if back else n + 1), size - 1)
+                copy = step(n, to)
+                if wanted is None:
+                    what(copy)
+                else:
+                    pl.when(wanted(to))(functools.partial(what, copy))
+
+        return act
+
+    def start(copy):
+        copy.start()
+
+    def wait_recv(copy):
+        copy.wait_recv()
+
+    def wait_send(copy):
+        copy.wait_send()
+
+    def owns(zz):
+        return zz < 7
+
+    def low(zz):
+        return lax.min(zz, 6)
+
+    def y_first(n, yy):
+        return remote(
+            chip16.at[span(yy * YPART, YPART)], y_in.at[n], ysent.at[n], yarrived.at[n], yy * 16 + z * 2
+        )
+
+    def z_second(n, zz):
+        return remote(
+            y16.at[span(low(zz) * OWNED, OWNED)], z_own.at[n], zsent.at[n], zarrived.at[n], y * 16 + zz * 2
+        )
+
+    def z_first(n, zz):
+        return remote(
+            chip16.at[span(low(zz) * ZPART, ZPART)], z_in.at[n], zsent.at[n], zarrived.at[n],
+            y * 16 + zz * 2 + 1,
+        )
+
+    def y_second(n, yy):
+        return remote(
+            z16.at[span(yy * OWNED, OWNED)], y_own.at[n], ysent.at[n], yarrived.at[n], yy * 16 + z * 2 + 1
+        )
+
+    def on_total(at, count, sent, arrived, peer):
+        at = span(at, count)
+        return remote(total.at[at], total.at[at], sent, arrived, peer)
+
+    def back_z_first(n, to, source):
+        return on_total(
+            y * YPART + low(source) * OWNED, OWNED, gzsent.at[n], gzarrived.at[n], y * 16 + to * 2
+        )
+
+    def back_y_second(n, to, source):
+        return on_total(source * YPART, YPART, gysent.at[n], gyarrived.at[n], to * 16 + z * 2)
+
+    def back_y_first(n, to, source):
+        return on_total(
+            HALF + low(z) * ZPART + source * OWNED, OWNED, gysent.at[n], gyarrived.at[n], to * 16 + z * 2 + 1
+        )
+
+    def back_z_second(n, to, source):
+        return on_total(
+            HALF + low(source) * ZPART, ZPART, gzsent.at[n], gzarrived.at[n], y * 16 + to * 2 + 1
+        )
+
+    def sends(step, mine):
+        return lambda n, to: step(n, to, mine)
+
+    def comes(step):
+        return lambda n, source: step(n, source, source)
+
+    @pl.when(on_y)
+    def _():
+        copies(YORDER, y, 4, y_first)(start)
+
+    @pl.when(on_z)
+    def _():
+        copies(ZORDER, z, 8, z_first, owns)(start)
+
+    gpad[...] = jnp.zeros_like(gpad)
+    def pad_gradient(bc):
+        width = min(2, 9 - bc)
+        u[:, : width * L] = lax.dot_general(
+            dpre3[...], wb[bc * L : (bc + width) * L, :], NT, preferred_element_type=F32
+        )
+
+        def add(gx, carry):
+            for n in range(width):
+                b, c = divmod(bc + n, 3)
+                for yy in range(8):
+                    at = pl.ds(gx * 100 + (yy + b) * 10 + c, 8)
+                    gpad[at, :] += u[pl.ds(pl.multiple_of(gx * 64 + yy * 8, 8), 8), n * L : (n + 1) * L]
+            return carry
+
+        lax.fori_loop(0, 20, add, 0)
+
+    for bc in (0, 2, 4, 6):
+        pad_gradient(bc)
+
+    @pl.when(on_y)
+    def _():
+        copies(range(3), y, 4, y_first)(wait_recv)
+        value = chip32[span(y * YPART, YPART), :]
+        for n in range(3):
+            value = value + y_in[n].astype(F32)
+        y32[...] = value
+        y16[...] = value.astype(BF16)
+        copies(ZORDER, z, 8, z_second, owns)(start)
+
+    @pl.when(on_z & owner)
+    def _():
+        copies(range(7), z, 8, z_first)(wait_recv)
+        value = chip32[span(z * ZPART, ZPART), :]
+        for n in range(7):
+            value = value + z_in[n].astype(F32)
+        z32[...] = value
+        z16[...] = value.astype(BF16)
+        copies(YORDER, y, 4, y_second)(start)
+
     deal_back = Deal(me, back, back_near, back_far, *(back_sem.at[n] for n in range(4)))
     flat = jnp.dot((coarse * cmask).astype(BF16), spread[...], preferred_element_type=F32)
     flat = jnp.where(pick, flat, 0.0).astype(BF16)
@@ -406,136 +537,24 @@
         box32[box_rows(1 - core, n), :] = dealt[CHIPS:, n * L : (n + 1) * L]
     back[...] = box32[...].astype(BF16)
     deal_back.start()
-    pair.wait_recv()
-    value = sums32[span(core * HALF, HALF), :] + pair_in[...].astype(F32)
-    chip32[...] = value
-    chip16[...] = value.astype(BF16)
-
-    on_y, on_z, owner = core == 0, core == 1, z < 7
-
-    def copies(order, place, size, step, wanted=None):
-        def act(what, back=False):
-            for n in order:
-                to = jnp.bitwise_and(place + (size - n - 1 if back else n + 1), size - 1)
-                copy = step(n, to)
-                if wanted is None:
-                    what(copy)
-                else:
-                    pl.when(wanted(to))(functools.partial(what, copy))
-
-        return act
-
-    def start(copy):
-        copy.start()
-
-    def wait_recv(copy):
-        copy.wait_recv()
-
-    def wait_send(copy):
-        copy.wait_send()
-
-    def owns(zz):
-        return zz < 7
-
-    def low(zz):
-        return lax.min(zz, 6)
-
-    def y_first(n, yy):
-        return remote(
-            chip16.at[span(yy * YPART, YPART)], y_in.at[n], ysent.at[n], yarrived.at[n], yy * 16 + z * 2
-        )
-
-    def z_second(n, zz):
-        return remote(
-            y16.at[span(low(zz) * OWNED, OWNED)], z_own.at[n], zsent.at[n], zarrived.at[n], y * 16 + zz * 2
-        )
-
-    def z_first(n, zz):
-        return remote(
-            chip16.at[span(low(zz) * ZPART, ZPART)], z_in.at[n], zsent.at[n], zarrived.at[n],
-            y * 16 + zz * 2 + 1,
-        )
-
-    def y_second(n, yy):
-        return remote(
-            z16.at[span(yy * OWNED, OWNED)], y_own.at[n], ysent.at[n], yarrived.at[n], yy * 16 + z * 2 + 1
-        )
-
-    def on_total(at, count, sent, arrived, peer):
-        at = span(at, count)
-        return remote(total.at[at], total.at[at], sent, arrived, peer)
-
-    def back_z_first(n, to, source):
-        return on_total(
-            y * YPART + low(source) * OWNED, OWNED, gzsent.at[n], gzarrived.at[n], y * 16 + to * 2
-        )
-
-    def back_y_second(n, to, source):
-        return on_total(source * YPART, YPART, gysent.at[n], gyarrived.at[n], to * 16 + z * 2)
-
-    def back_y_first(n, to, source):
-        return on_total(
-            HALF + low(z) * ZPART + source * OWNED, OWNED, gysent.at[n], gyarrived.at[n], to * 16 + z * 2 + 1
-        )
-
-    def back_z_second(n, to, source):
-        return on_total(
-            HALF + low(source) * ZPART, ZPART, gzsent.at[n], gzarrived.at[n], y * 16 + to * 2 + 1
-        )
-
-    def sends(step, mine):
-        return lambda n, to: step(n, to, mine)
-
-    def comes(step):
-        return lambda n, source: step(n, source, source)
-
-    @pl.when(on_y)
-    def _():
-        copies(YORDER, y, 4, y_first)(start)
-
-    @pl.when(on_z)
-    def _():
-        copies(ZORDER, z, 8, z_first, owns)(start)
-
-    gpad[...] = jnp.zeros_like(gpad)
-    def pad_gradient(bc):
-        width = min(2, 9 - bc)
-        u[:, : width * L] = lax.dot_general(
-            dpre3[...], wb[bc * L : (bc + width) * L, :], NT, preferred_element_type=F32
-        )
-
-        def add(gx, carry):
-            for n in range(width):
-                b, c = divmod(bc + n, 3)
-                for yy in range(8):
-                    at = pl.ds(gx * 100 + (yy + b) * 10 + c, 8)
-                    gpad[at, :] += u[pl.ds(pl.multiple_of(gx * 64 + yy * 8, 8), 8), n * L : (n + 1) * L]
-            return carry
-
-        lax.fori_loop(0, 20, add, 0)
-
-    for bc in (0, 2, 4, 6):
-        pad_gradient(bc)
-
-    @pl.when(on_y)
-    def _():
-        copies(range(3), y, 4, y_first)(wait_recv)
-        value = chip32[span(y * YPART, YPART), :]
+
+    @pl.when(on_y & owner)
+    def _():
+        copies(range(7), z, 8, z_second)(wait_recv)
+        value = y32[span(z * OWNED, OWNED), :]
+        for n in range(7):
+            value = value + z_own[n].astype(F32)
+        total[span(y * YPART + z * OWNED, OWNED), :] = value.astype(BF16)
+        copies(ZORDER, z, 8, sends(back_z_first, z))(start)
+
+    @pl.when(on_z & owner)
+    def _():
+        copies(range(3), y, 4, y_second)(wait_recv)
+        value = z32[span(y * OWNED, OWNED), :]
         for n in range(3):
-            value = value + y_in[n].astype(F32)
-        y32[...] = value
-        y16[...] = value.astype(BF16)
-        copies(ZORDER, z, 8, z_second, owns)(start)
-
-    @pl.when(on_z & owner)
-    def _():
-        copies(range(7), z, 8, z_first)(wait_recv)
-        value = chip32[span(z * ZPART, ZPART), :]
-        for n in range(7):
-            value = value + z_in[n].astype(F32)
-        z32[...] = value
-        z16[...] = value.astype(BF16)
-        copies(YORDER, y, 4, y_second)(start)
+            value = value + y_own[n].astype(F32)
+        total[span(HALF + z * ZPART + y * OWNED, OWNED), :] = value.astype(BF16)
+        copies(YORDER, y, 4, sends(back_y_first, y))(start)
 
     pad_gradient(8)
 
@@ -555,23 +574,6 @@
     for g in range(2):
         part_lower[g] = gsource[g * SHELL : (g + 1) * SHELL, :].astype(BF16)
         part_upper[g] = gsource[(4 + g) * SHELL : (5 + g) * SHELL, :].astype(BF16)
-    @pl.when(on_y & owner)
-    def _():
-        copies(range(7), z, 8, z_second)(wait_recv)
-        value = y32[span(z * OWNED, OWNED), :]
-        for n in range(7):
-            value = value + z_own[n].astype(F32)
-        total[span(y * YPART + z * OWNED, OWNED), :] = value.astype(BF16)
-        copies(ZORDER, z, 8, sends(back_z_first, z))(start)
-
-    @pl.when(on_z & owner)
-    def _():
-        copies(range(3), y, 4, y_second)(wait_recv)
-        value = z32[span(y * OWNED, OWNED), :]
-        for n in range(3):
-            value = value + y_own[n].astype(F32)
-        total[span(HALF + z * ZPART + y * OWNED, OWNED), :] = value.astype(BF16)
-        copies(YORDER, y, 4, sends(back_y_first, y))(start)
 
     rim_up = remote(part_upper, from_lower, rim_sent.at[0], rim_arrived.at[0], lax.min(me + 1, PEERS - 1))
     rim_down = remote(part_lower, from_upper, rim_sent.at[1], rim_arrived.at[1], lax.max(me - 1, 0))
@@ -583,8 +585,6 @@
     @pl.when(has_down)
     def _():
         rim_down.start()
-
-    deal_back.forward()
 
     def across(which, part):
         rows_at, count = (part * YPART, YPART) if which == 0 else (HALF + part * ZPART, ZPART)
@@ -602,14 +602,7 @@
         copies(ZORDER, z, 8, sends(back_z_second, z))(start)
         across(1, z).start()
 
-    deal_back.finish()
-    near32[...] = back_near[...].astype(F32)
-    far32[...] = back_far[...].astype(F32)
-    for n in range(6):
-        out32[pl.ds(n * PEERS + core, CHIPS, stride=2), :] = near32[box_rows(core, n), :]
-        out32[pl.ds(n * PEERS + 1 - core, CHIPS, stride=2), :] = far32[box_rows(core, n), :]
-    for n in range(6):
-        coarse_out[:, n * L : (n + 1) * L] = out32[n * PEERS : (n + 1) * PEERS, :].astype(BF16)
+    deal_back.forward()
 
     def pass_on_y(n):
         source = jnp.bitwise_and(y + 3 - n, 3)
@@ -661,6 +654,15 @@
         value = pre[g * V : (g + 1) * V, :]
         value = value * jnp.broadcast_to(own32[g * V : (g + 1) * V, C : C + 1], (V, L))
         grad_features[g] = jnp.transpose(value)[:C, :].astype(BF16)
+
+    deal_back.finish()
+    near32[...] = back_near[...].astype(F32)
+    far32[...] = back_far[...].astype(F32)
+    for n in range(6):
+        out32[pl.ds(n * PEERS + core, CHIPS, stride=2), :] = near32[box_rows(core, n), :]
+        out32[pl.ds(n * PEERS + 1 - core, CHIPS, stride=2), :] = far32[box_rows(core, n), :]
+    for n in range(6):
+        coarse_out[:, n * L : (n + 1) * L] = out32[n * PEERS : (n + 1) * PEERS, :].astype(BF16)
 
     @pl.when(on_y)
     def _():

time: 51.1 us -> 52.3 us (1.023)
  Pallas kernels: 49.7 us -> 50.9 us
    pallas_call x1, Pallas kernels: 47.2 us -> 48.4 us  [run_section(): pl.pallas_call(section_kernel, out_shape=(jax.ShapeDtypeStruct((PEERS, 6...]
where the time goes in v12:
time: 52.3 us; the launch traced here: 52.1 us
  Pallas kernels  50.9 us (97%)
  between operations  1.29 us (2%)
    pallas_call x1, Pallas kernels, run_section(): pl.pallas_call(section_kernel, out_shape=(jax.ShapeDtypeStruct((PEERS, 6...  48.4 us
    pallas_call x1, Pallas kernels, run_final(): pl.pallas_call(final_kernel, out_shape=(jax.ShapeDtypeStruct((PEERS, 6 *...  2.49 us

profile of v12, /device:TPU:1, one launch (start us, length us, event | category | flops | bytes accessed | tf_op | source)
XLA Modules:
  0.0 52.1 jit_solution(1612153094380388917)
XLA Ops:
  1.3 48.4 %shard_map.102 = (bf16[64,768]{1,0:T(8,128)(2,1)}, bf16[2,96,512]{2,1,0:T(8,128)(2,1)}, bf16[2688,128]{1,0:T(8,128)(2,1)}) custom-call(s32[2,27]{1,0:T(2,128)} %table_hbm.1, s32[1]{0:T(128)S(6)} %copy.11.live_hbm, s32[2,16]{1,0:T(2,128)} %occupancy_hbm.1, bf16[2,96,512]{2,1,0:T(8,128)(2,1)} %features_hbm.1, bf16[64,768]{1,0:T(8,128)(2,1)} %cotangent_hbm.1, ...), custom_call_target="tpu_custom_call" | custom-call | tf_op jit(solution)/shard_map/pallas_call | solution.py:732
  49.7 2.5 %shard_map.103 = (bf16[64,768]{1,0:T(8,128)(2,1)}, bf16[2,96,512]{2,1,0:T(8,128)(2,1)}, f32[27,96,96]{2,1,0:T(8,128)}, f32[8,96,96]{2,1,0:T(8,128)}) custom-call(bf16[64,768]{1,0:T(8,128)(2,1)} %get-tuple-element.7.coarse_in, bf16[2,96,512]{2,1,0:T(8,128)(2,1)} %get-tuple-element.8.features_in, bf16[2688,128]{1,0:T(8,128)(2,1)} %get-tuple-element.9.total_in), custom_call_target="tpu_custom_call" | custom-call | tf_op jit(solution)/shard_map/pallas_call | solution.py:843

commit v13 on v12

--- a/solution.py
+++ b/solution.py
@@ -343,9 +343,8 @@
     dz = jnp.where(cmask > 0, dz, 0.0)
     dzt = jnp.transpose(dz).astype(BF16)
     dz = dz.astype(BF16)
-    dh = [
-        lax.dot_general(dz, wd[j * L : (j + 1) * L, :], NT, preferred_element_type=F32) for j in range(8)
-    ]
+    dh = lax.dot_general(dz, wd[...], NT, preferred_element_type=F32)
+    dh = [dh[:, j * L : (j + 1) * L] for j in range(8)]
     parts = []
     for g in range(2):
         part = jnp.concatenate([piece[g * 64 : (g + 1) * 64] for piece in dh], axis=0)
@@ -488,46 +487,6 @@
     def _():
         copies(ZORDER, z, 8, z_first, owns)(start)
 
-    gpad[...] = jnp.zeros_like(gpad)
-    def pad_gradient(bc):
-        width = min(2, 9 - bc)
-        u[:, : width * L] = lax.dot_general(
-            dpre3[...], wb[bc * L : (bc + width) * L, :], NT, preferred_element_type=F32
-        )
-
-        def add(gx, carry):
-            for n in range(width):
-                b, c = divmod(bc + n, 3)
-                for yy in range(8):
-                    at = pl.ds(gx * 100 + (yy + b) * 10 + c, 8)
-                    gpad[at, :] += u[pl.ds(pl.multiple_of(gx * 64 + yy * 8, 8), 8), n * L : (n + 1) * L]
-            return carry
-
-        lax.fori_loop(0, 20, add, 0)
-
-    for bc in (0, 2, 4, 6):
-        pad_gradient(bc)
-
-    @pl.when(on_y)
-    def _():
-        copies(range(3), y, 4, y_first)(wait_recv)
-        value = chip32[span(y * YPART, YPART), :]
-        for n in range(3):
-            value = value + y_in[n].astype(F32)
-        y32[...] = value
-        y16[...] = value.astype(BF16)
-        copies(ZORDER, z, 8, z_second, owns)(start)
-
-    @pl.when(on_z & owner)
-    def _():
-        copies(range(7), z, 8, z_first)(wait_recv)
-        value = chip32[span(z * ZPART, ZPART), :]
-        for n in range(7):
-            value = value + z_in[n].astype(F32)
-        z32[...] = value
-        z16[...] = value.astype(BF16)
-        copies(YORDER, y, 4, y_second)(start)
-
     deal_back = Deal(me, back, back_near, back_far, *(back_sem.at[n] for n in range(4)))
     flat = jnp.dot((coarse * cmask).astype(BF16), spread[...], preferred_element_type=F32)
     flat = jnp.where(pick, flat, 0.0).astype(BF16)
@@ -538,6 +497,49 @@
     back[...] = box32[...].astype(BF16)
     deal_back.start()
 
+    gpad[...] = jnp.zeros_like(gpad)
+    def pad_gradient(bc):
+        width = min(2, 9 - bc)
+        u[:, : width * L] = lax.dot_general(
+            dpre3[...], wb[bc * L : (bc + width) * L, :], NT, preferred_element_type=F32
+        )
+
+        def add(gx, carry):
+            for n in range(width):
+                b, c = divmod(bc + n, 3)
+                for yy in range(8):
+                    at = pl.ds(gx * 100 + (yy + b) * 10 + c, 8)
+                    gpad[at, :] += u[pl.ds(pl.multiple_of(gx * 64 + yy * 8, 8), 8), n * L : (n + 1) * L]
+            return carry
+
+        lax.fori_loop(0, 20, add, 0)
+
+    for bc in (0, 2):
+        pad_gradient(bc)
+
+    @pl.when(on_y)
+    def _():
+        copies(range(3), y, 4, y_first)(wait_recv)
+        value = chip32[span(y * YPART, YPART), :]
+        for n in range(3):
+            value = value + y_in[n].astype(F32)
+        y32[...] = value
+        y16[...] = value.astype(BF16)
+        copies(ZORDER, z, 8, z_second, owns)(start)
+
+    @pl.when(on_z & owner)
+    def _():
+        copies(range(7), z, 8, z_first)(wait_recv)
+        value = chip32[span(z * ZPART, ZPART), :]
+        for n in range(7):
+            value = value + z_in[n].astype(F32)
+        z32[...] = value
+        z16[...] = value.astype(BF16)
+        copies(YORDER, y, 4, y_second)(start)
+
+    for bc in (4, 6):
+        pad_gradient(bc)
+
     @pl.when(on_y & owner)
     def _():
         copies(range(7), z, 8, z_second)(wait_recv)
@@ -556,6 +558,7 @@
         total[span(HALF + z * ZPART + y * OWNED, OWNED), :] = value.astype(BF16)
         copies(YORDER, y, 4, sends(back_y_first, y))(start)
 
+    deal_back.forward()
     pad_gradient(8)
 
     gsource[...] = jnp.zeros_like(gsource)
@@ -574,7 +577,6 @@
     for g in range(2):
         part_lower[g] = gsource[g * SHELL : (g + 1) * SHELL, :].astype(BF16)
         part_upper[g] = gsource[(4 + g) * SHELL : (5 + g) * SHELL, :].astype(BF16)
-
     rim_up = remote(part_upper, from_lower, rim_sent.at[0], rim_arrived.at[0], lax.min(me + 1, PEERS - 1))
     rim_down = remote(part_lower, from_upper, rim_sent.at[1], rim_arrived.at[1], lax.max(me - 1, 0))
 
@@ -602,7 +604,14 @@
         copies(ZORDER, z, 8, sends(back_z_second, z))(start)
         across(1, z).start()
 
-    deal_back.forward()
+    deal_back.finish()
+    near32[...] = back_near[...].astype(F32)
+    far32[...] = back_far[...].astype(F32)
+    for n in range(6):
+        out32[pl.ds(n * PEERS + core, CHIPS, stride=2), :] = near32[box_rows(core, n), :]
+        out32[pl.ds(n * PEERS + 1 - core, CHIPS, stride=2), :] = far32[box_rows(core, n), :]
+    for n in range(6):
+        coarse_out[:, n * L : (n + 1) * L] = out32[n * PEERS : (n + 1) * PEERS, :].astype(BF16)
 
     def pass_on_y(n):
         source = jnp.bitwise_and(y + 3 - n, 3)
@@ -654,15 +663,6 @@
         value = pre[g * V : (g + 1) * V, :]
         value = value * jnp.broadcast_to(own32[g * V : (g + 1) * V, C : C + 1], (V, L))
         grad_features[g] = jnp.transpose(value)[:C, :].astype(BF16)
-
-    deal_back.finish()
-    near32[...] = back_near[...].astype(F32)
-    far32[...] = back_far[...].astype(F32)
-    for n in range(6):
-        out32[pl.ds(n * PEERS + core, CHIPS, stride=2), :] = near32[box_rows(core, n), :]
-        out32[pl.ds(n * PEERS + 1 - core, CHIPS, stride=2), :] = far32[box_rows(core, n), :]
-    for n in range(6):
-        coarse_out[:, n * L : (n + 1) * L] = out32[n * PEERS : (n + 1) * PEERS, :].astype(BF16)
 
     @pl.when(on_y)
     def _():

time: 52.3 us -> 53.3 us (1.019)
  Pallas kernels: 50.9 us -> 51.9 us
    pallas_call x1, Pallas kernels: 48.4 us -> 49.4 us  [run_section(): pl.pallas_call(section_kernel, out_shape=(jax.ShapeDtypeStruct((PEERS, 6...]
where the time goes in v13:
time: 53.3 us; the launch traced here: 53.2 us
  Pallas kernels  51.9 us (97%)
  between operations  1.29 us (2%)
    pallas_call x1, Pallas kernels, run_section(): pl.pallas_call(section_kernel, out_shape=(jax.ShapeDtypeStruct((PEERS, 6...  49.4 us
    pallas_call x1, Pallas kernels, run_final(): pl.pallas_call(final_kernel, out_shape=(jax.ShapeDtypeStruct((PEERS, 6 *...  2.49 us

profile of v13, /device:TPU:1, one launch (start us, length us, event | category | flops | bytes accessed | tf_op | source)
XLA Modules:
  0.0 53.2 jit_solution(6352879299149436901)
XLA Ops:
  1.3 49.4 %shard_map.102 = (bf16[64,768]{1,0:T(8,128)(2,1)}, bf16[2,96,512]{2,1,0:T(8,128)(2,1)}, bf16[2688,128]{1,0:T(8,128)(2,1)}) custom-call(s32[2,27]{1,0:T(2,128)} %table_hbm.1, s32[1]{0:T(128)S(6)} %copy.11.live_hbm, s32[2,16]{1,0:T(2,128)} %occupancy_hbm.1, bf16[2,96,512]{2,1,0:T(8,128)(2,1)} %features_hbm.1, bf16[64,768]{1,0:T(8,128)(2,1)} %cotangent_hbm.1, ...), custom_call_target="tpu_custom_call" | custom-call | tf_op jit(solution)/shard_map/pallas_call | solution.py:732
  50.7 2.5 %shard_map.103 = (bf16[64,768]{1,0:T(8,128)(2,1)}, bf16[2,96,512]{2,1,0:T(8,128)(2,1)}, f32[27,96,96]{2,1,0:T(8,128)}, f32[8,96,96]{2,1,0:T(8,128)}) custom-call(bf16[64,768]{1,0:T(8,128)(2,1)} %get-tuple-element.7.coarse_in, bf16[2,96,512]{2,1,0:T(8,128)(2,1)} %get-tuple-element.8.features_in, bf16[2688,128]{1,0:T(8,128)(2,1)} %get-tuple-element.9.total_in), custom_call_target="tpu_custom_call" | custom-call | tf_op jit(solution)/shard_map/pallas_call | solution.py:843

commit v14 on v10

--- a/solution.py
+++ b/solution.py
@@ -123,14 +123,15 @@
     def tile(self, chip):
         return pl.ds(pl.multiple_of(chip * 16, 16), 16)
 
-    def start(self):
-        for offset in far_first():
+    def start(self, first=0, last=CHIPS - 1):
+        for offset in far_first()[first:last]:
             there = chip_at(self.here, offset)
             remote(
                 self.outbox.at[self.tile(there)], self.near.at[self.tile(self.here)],
                 *self.sems, there * 2 + self.core,
             ).start()
-        self.near[self.tile(self.here), :] = self.outbox[self.tile(self.here), :]
+        if last == CHIPS - 1:
+            self.near[self.tile(self.here), :] = self.outbox[self.tile(self.here), :]
 
     def forward(self):
         self.every.wait_recv()
@@ -405,7 +406,7 @@
         box32[box_rows(core, n), :] = dealt[:CHIPS, n * L : (n + 1) * L]
         box32[box_rows(1 - core, n), :] = dealt[CHIPS:, n * L : (n + 1) * L]
     back[...] = box32[...].astype(BF16)
-    deal_back.start()
+    deal_back.start(0, 12)
     pair.wait_recv()
     value = sums32[span(core * HALF, HALF), :] + pair_in[...].astype(F32)
     chip32[...] = value
@@ -496,6 +497,8 @@
     @pl.when(on_z)
     def _():
         copies(ZORDER, z, 8, z_first, owns)(start)
+
+    deal_back.start(12)
 
     gpad[...] = jnp.zeros_like(gpad)
     def pad_gradient(bc):

time: 51.1 us -> 50.9 us (level)
  no operation moved by 1% of the time
where the time goes in v14:
time: 50.9 us; the launch traced here: 50.8 us
  Pallas kernels  49.5 us (97%)
  between operations  1.29 us (3%)
    pallas_call x1, Pallas kernels, run_section(): pl.pallas_call(section_kernel, out_shape=(jax.ShapeDtypeStruct((PEERS, 6...  47 us
    pallas_call x1, Pallas kernels, run_final(): pl.pallas_call(final_kernel, out_shape=(jax.ShapeDtypeStruct((PEERS, 6 *...  2.49 us

profile of v14, /device:TPU:1, one launch (start us, length us, event | category | flops | bytes accessed | tf_op | source)
XLA Modules:
  0.0 50.8 jit_solution(11710366379264522668)
XLA Ops:
  1.3 47.0 %shard_map.102 = (bf16[64,768]{1,0:T(8,128)(2,1)}, bf16[2,96,512]{2,1,0:T(8,128)(2,1)}, bf16[2688,128]{1,0:T(8,128)(2,1)}) custom-call(s32[2,27]{1,0:T(2,128)} %table_hbm.1, s32[1]{0:T(128)S(6)} %copy.11.live_hbm, s32[2,16]{1,0:T(2,128)} %occupancy_hbm.1, bf16[2,96,512]{2,1,0:T(8,128)(2,1)} %features_hbm.1, bf16[64,768]{1,0:T(8,128)(2,1)} %cotangent_hbm.1, ...), custom_call_target="tpu_custom_call" | custom-call | tf_op jit(solution)/shard_map/pallas_call | solution.py:733
  48.3 2.5 %shard_map.103 = (bf16[64,768]{1,0:T(8,128)(2,1)}, bf16[2,96,512]{2,1,0:T(8,128)(2,1)}, f32[27,96,96]{2,1,0:T(8,128)}, f32[8,96,96]{2,1,0:T(8,128)}) custom-call(bf16[64,768]{1,0:T(8,128)(2,1)} %get-tuple-element.7.coarse_in, bf16[2,96,512]{2,1,0:T(8,128)(2,1)} %get-tuple-element.8.features_in, bf16[2688,128]{1,0:T(8,128)(2,1)} %get-tuple-element.9.total_in), custom_call_target="tpu_custom_call" | custom-call | tf_op jit(solution)/shard_map/pallas_call | solution.py:844

commit v15 on v13

--- a/solution.py
+++ b/solution.py
@@ -123,14 +123,15 @@
     def tile(self, chip):
         return pl.ds(pl.multiple_of(chip * 16, 16), 16)
 
-    def start(self):
-        for offset in far_first():
+    def start(self, first=0, last=CHIPS - 1):
+        for offset in far_first()[first:last]:
             there = chip_at(self.here, offset)
             remote(
                 self.outbox.at[self.tile(there)], self.near.at[self.tile(self.here)],
                 *self.sems, there * 2 + self.core,
             ).start()
-        self.near[self.tile(self.here), :] = self.outbox[self.tile(self.here), :]
+        if last == CHIPS - 1:
+            self.near[self.tile(self.here), :] = self.outbox[self.tile(self.here), :]
 
     def forward(self):
         self.every.wait_recv()
@@ -396,6 +397,15 @@
 
     pair = remote(sums16.at[span((1 - core) * HALF, HALF)], pair_in, pair_sent, pair_arrived, partner)
     pair.start()
+    deal_back = Deal(me, back, back_near, back_far, *(back_sem.at[n] for n in range(4)))
+    flat = jnp.dot((coarse * cmask).astype(BF16), spread[...], preferred_element_type=F32)
+    flat = jnp.where(pick, flat, 0.0).astype(BF16)
+    dealt = lax.dot_general(chosen, flat, (((0,), (0,)), ((), ())), preferred_element_type=F32)
+    for n in range(6):
+        box32[box_rows(core, n), :] = dealt[:CHIPS, n * L : (n + 1) * L]
+        box32[box_rows(1 - core, n), :] = dealt[CHIPS:, n * L : (n + 1) * L]
+    back[...] = box32[...].astype(BF16)
+    deal_back.start(0, 12)
     pair.wait_recv()
     value = sums32[span(core * HALF, HALF), :] + pair_in[...].astype(F32)
     chip32[...] = value
@@ -487,15 +497,7 @@
     def _():
         copies(ZORDER, z, 8, z_first, owns)(start)
 
-    deal_back = Deal(me, back, back_near, back_far, *(back_sem.at[n] for n in range(4)))
-    flat = jnp.dot((coarse * cmask).astype(BF16), spread[...], preferred_element_type=F32)
-    flat = jnp.where(pick, flat, 0.0).astype(BF16)
-    dealt = lax.dot_general(chosen, flat, (((0,), (0,)), ((), ())), preferred_element_type=F32)
-    for n in range(6):
-        box32[box_rows(core, n), :] = dealt[:CHIPS, n * L : (n + 1) * L]
-        box32[box_rows(1 - core, n), :] = dealt[CHIPS:, n * L : (n + 1) * L]
-    back[...] = box32[...].astype(BF16)
-    deal_back.start()
+    deal_back.start(12)
 
     gpad[...] = jnp.zeros_like(gpad)
     def pad_gradient(bc):
@@ -558,7 +560,6 @@
         total[span(HALF + z * ZPART + y * OWNED, OWNED), :] = value.astype(BF16)
         copies(YORDER, y, 4, sends(back_y_first, y))(start)
 
-    deal_back.forward()
     pad_gradient(8)
 
     gsource[...] = jnp.zeros_like(gsource)
@@ -587,6 +588,8 @@
     @pl.when(has_down)
     def _():
         rim_down.start()
+
+    deal_back.forward()
 
     def across(which, part):
         rows_at, count = (part * YPART, YPART) if which == 0 else (HALF + part * ZPART, ZPART)

time: 53.3 us -> 51.6 us (0.968)
  Pallas kernels: 51.9 us -> 50.2 us
    pallas_call x1, Pallas kernels: 49.4 us -> 47.7 us  [run_section(): pl.pallas_call(section_kernel, out_shape=(jax.ShapeDtypeStruct((PEERS, 6...]
where the time goes in v15:
time: 51.6 us; the launch traced here: 51.5 us
  Pallas kernels  50.2 us (97%)
  between operations  1.29 us (2%)
    pallas_call x1, Pallas kernels, run_section(): pl.pallas_call(section_kernel, out_shape=(jax.ShapeDtypeStruct((PEERS, 6...  47.7 us
    pallas_call x1, Pallas kernels, run_final(): pl.pallas_call(final_kernel, out_shape=(jax.ShapeDtypeStruct((PEERS, 6 *...  2.49 us

profile of v15, /device:TPU:1, one launch (start us, length us, event | category | flops | bytes accessed | tf_op | source)
XLA Modules:
  0.0 51.5 jit_solution(6171396061474115284)
XLA Ops:
  1.3 47.7 %shard_map.102 = (bf16[64,768]{1,0:T(8,128)(2,1)}, bf16[2,96,512]{2,1,0:T(8,128)(2,1)}, bf16[2688,128]{1,0:T(8,128)(2,1)}) custom-call(s32[2,27]{1,0:T(2,128)} %table_hbm.1, s32[1]{0:T(128)S(6)} %copy.11.live_hbm, s32[2,16]{1,0:T(2,128)} %occupancy_hbm.1, bf16[2,96,512]{2,1,0:T(8,128)(2,1)} %features_hbm.1, bf16[64,768]{1,0:T(8,128)(2,1)} %cotangent_hbm.1, ...), custom_call_target="tpu_custom_call" | custom-call | tf_op jit(solution)/shard_map/pallas_call | solution.py:735
  49.0 2.5 %shard_map.103 = (bf16[64,768]{1,0:T(8,128)(2,1)}, bf16[2,96,512]{2,1,0:T(8,128)(2,1)}, f32[27,96,96]{2,1,0:T(8,128)}, f32[8,96,96]{2,1,0:T(8,128)}) custom-call(bf16[64,768]{1,0:T(8,128)(2,1)} %get-tuple-element.7.coarse_in, bf16[2,96,512]{2,1,0:T(8,128)(2,1)} %get-tuple-element.8.features_in, bf16[2688,128]{1,0:T(8,128)(2,1)} %get-tuple-element.9.total_in), custom_call_target="tpu_custom_call" | custom-call | tf_op jit(solution)/shard_map/pallas_call | solution.py:846
